TPU v7x, 32 devices: a whole 2x2x4 slice. The times are simulated.
32 devices in a mesh: lat: 8 (over y, x, core), dep: 4 (over z).
Axes of the slice: x: 2, y: 2, z: 4, core: 2. Of those that a mesh axis runs over, the one named last changes fastest.
Arguments:
- estimate: float32 [16, 256, 1024], P(None, 'dep', 'lat'), may hold values from -6 to 6
- previous: float32 [16, 256, 1024], P(None, 'dep', 'lat'), may hold values from -6 to 6
- measured: float32 [16, 12, 1024], P('dep', None, 'lat'), may hold values from -21 to 21
- foot_table: bfloat16 [64, 128, 128], replicated, may hold values from -0.01953125 to 0.01953125
- foot_id: int32 [8, 12, 256, 3], P('lat', None, 'dep'), may hold values from 0 to 63
- foot_lo: int32 [8, 12, 256], P('lat', None, 'dep'), may hold values from -1 to 0, as said below
- foot_count: int32 [8, 12, 256], P('lat', None, 'dep'), may hold values from 1 to 3, as said below
- mask_table: float32 [16, 128], replicated, may hold values from 0.2 to 1
- mask_id: int32 [12, 8], P(None, 'lat'), may hold values from 0 to 15
- thresholds: float32 [256], replicated, may hold values from 0.02 to 0.5
Outputs:
- refined: float32 [16, 256, 1024], P(None, 'dep', 'lat')
- extrapolated: float32 [16, 256, 1024], P(None, 'dep', 'lat')
Inputs may be any that keep to these rules, and one draw needn't show every extreme that they name: The live offsets foot_lo .. foot_lo + foot_count - 1 of every detector tile, frame and plane lie within -1 .. 1; some entries have foot_lo = -1. `foot_count`: some entries have all three offsets live.
All inputs are finite; a program needn't handle non-finite values.
Results may differ from a plain program's by a relative error of at most 0.00099.
Values may be sent and summed in bfloat16 or wider, within the bound.
No kernel may reach another device: no remote copies, remote signals or barrier semaphores. Data moves between devices by JAX's collectives and lax.ppermute only.
A program may use at most 128 MiB of HBM per device.

v0:
```python
import math

import jax
import jax.numpy as jnp
from jax import lax
from jax.sharding import PartitionSpec as P

ITERS = 2
KSTART = 8


root_half = 0.7071067811865476
tiny_eps = 1e-06


def extended(cells, sides, width):
    for axis, dim in sides:
        count = lax.axis_size(axis)
        ends = count - 1
        head = lax.slice_in_dim(cells, 0, width, axis=dim)
        tail = lax.slice_in_dim(cells, cells.shape[dim] - width, cells.shape[dim], axis=dim)
        cells = jnp.concatenate(
            [
                lax.ppermute(tail, axis, [(i, (i + 1) % count) for i in range(ends)]),
                cells,
                lax.ppermute(head, axis, [((i + 1) % count, i) for i in range(ends)]),
            ],
            axis=dim,
        )
    return cells


def from_behind(shard, axis, by):
    count = lax.axis_size(axis)
    pairs = [(i, i + by) for i in range(count) if 0 <= i + by < count]
    return lax.ppermute(shard, axis, pairs)


def momentum_list():
    ratio_now = 1.0
    ratios = [ratio_now]
    for iteration in range(KSTART + ITERS + 3):
        ratio_now = (1.0 + math.sqrt(1.0 + 4.0 * ratio_now * ratio_now)) / 2.0
        ratios.append(ratio_now)
    return [
        (ratios[KSTART - 1 + iteration] - 1.0) / ratios[KSTART + iteration]
        for iteration in range(ITERS + 1)
    ]


def walsh(volume, bit_count):
    row_total, length, tail_size = volume.shape
    for section_bit in range(bit_count):
        stride = 2**section_bit
        shaped = volume.reshape(row_total, length // (2 * stride), 2, stride, tail_size)
        lower_half = shaped[:, :, 0]
        higher = shaped[:, :, 1]
        volume = jnp.stack(
            [(lower_half + higher) * root_half, (lower_half - higher) * root_half], axis=2
        ).reshape(row_total, length, tail_size)
    return volume


def local(
    estimate,
    previous,
    measured,
    foot_table,
    foot_id,
    foot_lo,
    foot_count,
    mask_table,
    mask_id,
    thresholds,
):
    row_total, depth_local, tile_width = estimate.shape
    depth_devices = lax.axis_size("dep")
    local_bits = depth_local.bit_length() - 1
    device_bits = depth_devices.bit_length() - 1
    momenta = momentum_list()
    offsets = jnp.arange(3, dtype=jnp.int32) - 1
    first_offset = foot_lo[0][..., None]
    active = (offsets >= first_offset) & (offsets < first_offset + foot_count[0][..., None])
    chosen = jnp.where(active[..., None, None], foot_table[foot_id[0]], jnp.zeros((), jnp.bfloat16))
    chooser = (
        mask_id[:, 0][:, None] == jnp.arange(mask_table.shape[0], dtype=jnp.int32)[None]
    ).astype(jnp.float32)
    mask_rows = jnp.dot(chooser, mask_table, precision=lax.Precision.HIGHEST)
    state = estimate
    current = estimate + momenta[0] * (estimate - previous)
    for iteration in range(ITERS):
        lifted = current.astype(jnp.bfloat16)
        widened = extended(lifted, (("lat", 2),), tile_width)
        widened = widened.reshape(row_total, depth_local, 3, tile_width)
        projected = lax.psum_scatter(
            jnp.einsum("rzoc,fzocd->rfd", widened, chosen, preferred_element_type=jnp.float32),
            "dep",
            scatter_dimension=0,
            tiled=True,
        )
        residual = mask_rows[None] * projected - measured
        misfit_local = jnp.sum(residual * residual)
        weighted = (mask_rows[None] * residual).astype(jnp.bfloat16)
        misfit = lax.psum(misfit_local, ("lat", "dep"))
        collected = jnp.einsum(
            "rfd,fzocd->rzoc",
            lax.all_gather(weighted, "dep", axis=0, tiled=True),
            chosen,
            preferred_element_type=jnp.float32,
        )
        gradient = collected[:, :, 1] + from_behind(collected[:, :, 2], "lat", 1)
        gradient = gradient + from_behind(collected[:, :, 0], "lat", -1)
        grad_local = jnp.sum(gradient * gradient)
        grad_sq = lax.psum(grad_local, ("lat", "dep"))
        step_size = 0.5 * misfit / (grad_sq + tiny_eps)
        moved = current - step_size * gradient
        coefficients = walsh(
            lax.all_to_all(moved, "dep", split_axis=0, concat_axis=1, tiled=True),
            local_bits + device_bits,
        )
        limit = step_size * thresholds[None, :, None]
        shrunk = coefficients - jnp.clip(coefficients, -limit, limit)
        fresh = lax.all_to_all(
            walsh(shrunk, local_bits + device_bits), "dep", split_axis=1, concat_axis=0, tiled=True
        )
        current = fresh + momenta[iteration + 1] * (fresh - state)
        state = fresh
    return (state, current)


def solution(mesh):
    in_specs = (
        P(None, "dep", "lat"),
        P(None, "dep", "lat"),
        P("dep", None, "lat"),
        P(),
        P("lat", None, "dep", None),
        P("lat", None, "dep"),
        P("lat", None, "dep"),
        P(),
        P(None, "lat"),
        P(),
    )
    out_specs = (P(None, "dep", "lat"), P(None, "dep", "lat"))
    return jax.shard_map(local, mesh=mesh, in_specs=in_specs, out_specs=out_specs, check_vma=False)
```

profile of v0, /device:TPU:0, one launch (start us, length us, event | category | flops | bytes accessed | tf_op | source)
XLA Modules:
  0.0 486.1 jit_solution(15713106999689812745)
XLA Ops:
  7.2 2.0 fusion.19
  9.2 1.3 collective-permute-start.1
  10.5 3.0 collective-permute-start
  13.5 0.7 compare_select_fusion
  14.7 0.7 bitcast_add_fusion
  15.5 0.8 copy.209
  16.3 51.0 %gather_fusion = bf16[2304,128,128]{2,1,0:T(8,128)(2,1)} fusion(bf16[64,128,128]{2,1,0:T(8,128)(2,1)S(1)} %copy-done, s32[3072]{0:T(1024)S(1)} %pad_clamp_fusion), kind=kCustom, calls=%fused_computation | custom fusion | bytes 151004160 | tf_op jit(solution)/shard_map/gather | solution.py:84
  67.5 0.7 copy-done.11
  68.2 24.4 %fusion.4 = f32[16,12,128]{2,0,1:T(8,128)} fusion(bf16[16,64,128]{2,0,1:T(8,128)(2,1)S(1)} %collective-permute-done.1, bf16[16,64,128]{2,0,1:T(8,128)(2,1)S(1)} %fusion.19, bf16[16,64,128]{2,0,1:T(8,128)(2,1)} %copy-done.11, bf16[12,64,3,128,128]{4,3,2,1,0:T(8,128)(2,1)} %bitcast.3, pred[12,64,3]{0,2,1:T(4,128)(4,1)S(1)} %compare_and_fusion), kind=kOutput, calls=%fused_computation.8 | convolution fusion | flops 1248067584 | bytes 76384512 | tf_op jit(solution)/shard_map/rzoc,fzocd->rfd/dot_general | solution.py:96
  92.8 0.6 dynamic-slice
  94.0 36.4 %all-reduce.7.cloned.1.call-done = f32[16,12,128]{2,0,1:T(8,128)} async-done(((f32[16,12,128]{2,0,1:T(8,128)}), f32[16,12,128]{2,0,1:T(8,128)}) %all-reduce.7.cloned.1.call-update) | async-done | bytes 98320
  130.4 1.4 multiply_convert_fusion.1
  131.8 13.3 %all_gather.6 = bf16[16,12,128]{2,1,0:T(8,128)(2,1)S(1)} all-gather(bf16[4,12,128]{2,1,0:T(8,128)(2,1)S(1)} %copy.149), channel_id=1, replica_groups=mesh['lat'=8,'dep'=4] {'dep'}, dimensions={0}, use_global_device_ids=true | all-gather | bytes 61440 | tf_op jit(solution)/shard_map/all_gather | solution.py:107
  145.1 24.9 %convolution_bitcast_fusion.1 = f32[16,64,3,128]{3,0,2,1:T(8,128)S(1)} fusion(bf16[16,12,128,1,1]{2,1,0,4,3:T(8,128)(2,1)S(1)} %bitcast.197, bf16[12,64,3,128,128]{4,3,2,1,0:T(8,128)(2,1)} %bitcast.3, pred[12,64,3]{0,2,1:T(4,128)(4,1)S(1)} %compare_and_fusion), kind=kOutput, calls=%fused_computation.7 | convolution fusion | flops 1245708288 | bytes 77121792 | tf_op jit(solution)/shard_map/rfd,fzocd->rzoc/dot_general | solution.py:105
  170.1 1.3 collective-permute-start.2
  171.4 1.3 collective-permute-start.3
  172.9 4.0 collective-permute-done.3
  176.9 0.8 multiply_reduce_fusion.1
  177.8 47.7 %all-reduce.3 = (f32[]{:T(128)}, f32[]{:T(128)}) all-reduce(f32[]{:T(128)} %get-tuple-element.91, f32[]{:T(128)} %multiply_reduce_fusion.1), channel_id=1, replica_groups=mesh['lat'=8,'dep'=4] {'lat','dep'}, use_global_device_ids=true, to_apply=%region_2.3 | all-reduce | flops 2 | bytes 16 | tf_op jit(solution)/shard_map/psum | solution.py:104
  226.7 2.0 multiply_subtract_fusion.1
  228.7 1.0 copy.153
  229.7 3.7 all-to-all-start
  233.7 13.6 %all-to-all-done = f32[16,64,128]{2,1,0:T(8,128)S(1)} async-done(((f32[16,64,128]{2,1,0:T(8,128)}), f32[16,64,128]{2,1,0:T(8,128)S(1)}, u32[]{:S(2)}, u32[]{:S(2)}) %all-to-all-start) | async-done | bytes 524320 | tf_op jit(solution)/shard_map/all_to_all | solution.py:118
  247.4 0.5 subtract_multiply_fusion.31
  248.1 0.6 add_multiply_fusion.29
  248.7 0.5 pad_maximum_fusion.1
  249.2 0.3 copy.157
  250.1 0.3 minimum_subtract_fusion.1
  250.4 0.5 subtract_multiply_fusion.23
  251.1 0.6 add_multiply_fusion.21
  251.8 0.5 pad_maximum_fusion.8
  252.2 0.3 copy.160
  253.1 0.3 copy.161
  253.5 16.4 %all_to_all.66 = f32[4,256,128]{2,0,1:T(4,128)S(1)} all-to-all(f32[4,256,128]{2,0,1:T(4,128)S(1)} %bitcast.183), channel_id=1, replica_groups=mesh['lat'=8,'dep'=4] {'dep'}, dimensions={1} | all-to-all | bytes 1048576 | tf_op jit(solution)/shard_map/all_to_all | solution.py:123
  270.2 0.4 fusion.18
  270.6 1.3 collective-permute-start.5
  271.9 3.0 collective-permute-start.4
  275.0 1.1 collective-permute-done.4
  276.1 24.2 %fusion.7 = f32[16,12,128]{2,0,1:T(8,128)} fusion(bf16[16,64,128]{2,0,1:T(8,128)(2,1)S(1)} %collective-permute-done.5, bf16[16,64,128]{2,0,1:T(8,128)(2,1)S(1)} %fusion.18, bf16[16,64,128]{2,0,1:T(8,128)(2,1)S(1)} %collective-permute-done.4, bf16[12,64,3,128,128]{4,3,2,1,0:T(8,128)(2,1)} %bitcast.3, pred[12,64,3]{0,2,1:T(4,128)(4,1)S(1)} %compare_and_fusion), kind=kOutput, calls=%fused_computation.9 | convolution fusion | flops 1248067584 | bytes 76384512 | tf_op jit(solution)/shard_map/rzoc,fzocd->rfd/dot_general | solution.py:96
  300.3 37.5 %all-reduce.9.cloned.1.call-done = f32[16,12,128]{2,0,1:T(8,128)} async-done(((f32[16,12,128]{2,0,1:T(8,128)}), f32[16,12,128]{2,0,1:T(8,128)}) %all-reduce.9.cloned.1.call-update) | async-done | bytes 98320
  337.8 1.4 multiply_convert_fusion
  339.2 13.1 %all_gather.7 = bf16[16,12,128]{2,1,0:T(8,128)(2,1)S(1)} all-gather(bf16[4,12,128]{2,1,0:T(8,128)(2,1)S(1)} %copy.168), channel_id=1, replica_groups=mesh['lat'=8,'dep'=4] {'dep'}, dimensions={0}, use_global_device_ids=true | all-gather | bytes 61440 | tf_op jit(solution)/shard_map/all_gather | solution.py:107
  352.4 24.9 %convolution_bitcast_fusion = f32[16,64,3,128]{3,0,2,1:T(8,128)S(1)} fusion(bf16[16,12,128,1,1]{2,1,0,4,3:T(8,128)(2,1)S(1)} %bitcast.196, bf16[12,64,3,128,128]{4,3,2,1,0:T(8,128)(2,1)} %bitcast.3, pred[12,64,3]{0,2,1:T(4,128)(4,1)S(1)} %compare_and_fusion), kind=kOutput, calls=%fused_computation.6 | convolution fusion | flops 1245708288 | bytes 77121792 | tf_op jit(solution)/shard_map/rfd,fzocd->rzoc/dot_general | solution.py:105
  377.4 1.3 collective-permute-start.6
  378.7 1.3 collective-permute-start.7
  380.2 4.0 collective-permute-done.7
  384.2 0.8 multiply_reduce_fusion
  385.0 47.6 %all-reduce.2 = (f32[]{:T(128)}, f32[]{:T(128)}) all-reduce(f32[]{:T(128)} %get-tuple-element.89, f32[]{:T(128)} %multiply_reduce_fusion), channel_id=1, replica_groups=mesh['lat'=8,'dep'=4] {'lat','dep'}, use_global_device_ids=true, to_apply=%region_7.8 | all-reduce | flops 2 | bytes 16 | tf_op jit(solution)/shard_map/psum | solution.py:104
  433.9 1.8 multiply_subtract_fusion
  435.6 1.0 copy.172
  436.6 3.7 all-to-all-start.2
  440.6 13.7 %all-to-all-done.2 = f32[16,64,128]{2,1,0:T(8,128)S(1)} async-done(((f32[16,64,128]{2,1,0:T(8,128)}), f32[16,64,128]{2,1,0:T(8,128)S(1)}, u32[]{:S(2)}, u32[]{:S(2)}) %all-to-all-start.2) | async-done | bytes 524320 | tf_op jit(solution)/shard_map/all_to_all | solution.py:118
  454.4 0.5 subtract_multiply_fusion.15
  455.1 0.6 add_multiply_fusion.13
  455.7 0.5 pad_maximum_fusion.15
  456.2 0.3 copy.176
  457.0 0.3 minimum_subtract_fusion
  457.4 0.5 subtract_multiply_fusion.7
  458.1 0.6 add_multiply_fusion.5
  458.7 0.5 pad_maximum_fusion.22
  459.2 0.3 copy.179
  460.4 16.4 %all_to_all.67 = f32[4,256,128]{2,0,1:T(4,128)S(1)} all-to-all(f32[4,256,128]{2,0,1:T(4,128)S(1)} %bitcast.185), channel_id=1, replica_groups=mesh['lat'=8,'dep'=4] {'dep'}, dimensions={1} | all-to-all | bytes 1048576 | tf_op jit(solution)/shard_map/all_to_all | solution.py:123
  477.3 1.0 copy.183
  478.3 1.0 copy.184
  (119 shorter events, 5.7 us)
Async XLA Ops:
  7.2 9.2 %copy-start = (bf16[64,128,128]{2,1,0:T(8,128)(2,1)S(1)}, bf16[64,128,128]{2,1,0:T(8,128)(2,1)}, u32[]{:S(2)}) copy-start(bf16[64,128,128]{2,1,0:T(8,128)(2,1)} %param.13) | copy-start | bytes 6291460
  7.2 123.2 %all-reduce.7.cloned.1.call-start = ((), (), s32[]{:S(2)}) async-start(), calls=%async_computation.4 | async-start | bytes 196608
  9.2 58.3 %collective-permute-start.1 = (bf16[16,64,128]{2,0,1:T(8,128)(2,1)S(1)}, bf16[16,64,128]{2,0,1:T(8,128)(2,1)S(1)}, u32[]{:S(2)}, u32[]{:S(2)}) collective-permute-start(bf16[16,64,128]{2,0,1:T(8,128)(2,1)S(1)} %fusion.19), channel_id=1, source_target_pairs={{4,0},{8,4},{12,8},{16,12},{20,16},{24,20},{28,24},{5,1},{9,5},{13... | collective-permute-start | bytes 786440 | tf_op jit(solution)/shard_map/ppermute | solution.py:26
  10.5 57.0 %collective-permute-start = (bf16[16,64,128]{2,0,1:T(8,128)(2,1)S(1)}, bf16[16,64,128]{2,0,1:T(8,128)(2,1)S(1)}, u32[]{:S(2)}, u32[]{:S(2)}) collective-permute-start(bf16[16,64,128]{2,0,1:T(8,128)(2,1)S(1)} %fusion.19), channel_id=1, source_target_pairs={{0,4},{4,8},{8,12},{12,16},{16,20},{20,24},{24,28},{1,5},{5,9},{9,... | collective-permute-start | bytes 786440 | tf_op jit(solution)/shard_map/ppermute | solution.py:24
  67.5 0.7 copy-start.11
  68.2 24.4 %copy-start.12 = (f32[16,128]{1,0:T(8,128)S(1)}, f32[16,128]{1,0:T(8,128)}, u32[]{:S(2)}) copy-start(f32[16,128]{1,0:T(8,128)} %param.17) | copy-start | bytes 24580
  68.2 24.4 %copy-start.13 = (s32[12,1]{0,1:T(1,128)S(1)}, s32[12,1]{0,1:T(1,128)}, u32[]{:S(2)}) copy-start(s32[12,1]{0,1:T(1,128)} %param.18) | copy-start | bytes 148
  68.2 24.6 %copy-start.14 = (u32[32]{0:T(128)S(1)}, u32[32]{0:T(128)}, u32[]{:S(2)}) copy-start(u32[32]{0:T(128)} %constant.36) | copy-start | bytes 388
  68.2 62.2 %copy-start.9 = (f32[4,12,128]{2,0,1:T(4,128)S(1)}, f32[4,12,128]{2,0,1:T(4,128)}, u32[]{:S(2)}) copy-start(f32[4,12,128]{2,0,1:T(4,128)} %param.12) | copy-start | bytes 73732
  131.8 94.9 %copy-start.1 = (f32[16,64,128]{2,1,0:T(8,128)S(1)}, f32[16,64,128]{2,1,0:T(8,128)}, u32[]{:S(2)}) copy-start(f32[16,64,128]{2,1,0:T(8,128)} %param.10) | copy-start | bytes 1572868
  131.8 94.9 %copy-start.4 = (f32[16,64,128]{2,1,0:T(8,128)S(1)}, f32[16,64,128]{2,1,0:T(8,128)}, u32[]{:S(2)}) copy-start(f32[16,64,128]{2,1,0:T(8,128)} %param.11) | copy-start | bytes 1572868
  145.1 88.3 %copy-start.10 = (f32[256]{0:T(256)S(1)}, f32[256]{0:T(256)}, u32[]{:S(2)}) copy-start(f32[256]{0:T(256)} %param.19) | copy-start | bytes 3076
  170.0 6.9 %copy-start.3 = (f32[16,64,3,128]{3,0,2,1:T(8,128)}, f32[16,64,3,128]{3,0,2,1:T(8,128)S(1)}, u32[]{:S(2)}) copy-start(f32[16,64,3,128]{3,0,2,1:T(8,128)S(1)} %convolution_bitcast_fusion.1) | copy-start | bytes 4718596
  170.1 2.8 collective-permute-start.2
  171.4 5.5 %collective-permute-start.3 = (f32[16,64,128]{2,0,1:T(8,128)S(1)}, f32[16,64,128]{2,0,1:T(8,128)S(1)}, u32[]{:S(2)}, u32[]{:S(2)}) collective-permute-start(f32[16,64,128]{2,0,1:T(8,128)S(1)} %get-tuple-element.23), channel_id=1, source_target_pairs={{4,0},{8,4},{12,8},{16,12},{20,16},{24,20},{28,24},{5,1},{9,5},{13... | collective-permute-start | bytes 1572872 | tf_op jit(solution)/shard_map/ppermute | solution.py:36
  172.9 4.8 copy-start.6
  176.9 0.8 copy-start.8
  229.7 17.7 %all-to-all-start = ((f32[16,64,128]{2,1,0:T(8,128)}), f32[16,64,128]{2,1,0:T(8,128)S(1)}, u32[]{:S(2)}, u32[]{:S(2)}) async-start(f32[16,64,128]{2,1,0:T(8,128)} %copy.153), calls=%async_computation | async-start | bytes 1048576 | tf_op jit(solution)/shard_map/all_to_all | solution.py:118
  233.4 104.4 %all-reduce.9.cloned.1.call-start = ((), (), s32[]{:S(2)}) async-start(), calls=%async_computation.5 | async-start | bytes 196608
  270.6 4.4 collective-permute-start.5
  271.9 4.2 collective-permute-start.4
  377.3 6.9 %copy-start.2 = (f32[16,64,3,128]{3,0,2,1:T(8,128)}, f32[16,64,3,128]{3,0,2,1:T(8,128)S(1)}, u32[]{:S(2)}) copy-start(f32[16,64,3,128]{3,0,2,1:T(8,128)S(1)} %convolution_bitcast_fusion) | copy-start | bytes 4718596
  377.4 2.8 collective-permute-start.6
  378.7 5.5 %collective-permute-start.7 = (f32[16,64,128]{2,0,1:T(8,128)S(1)}, f32[16,64,128]{2,0,1:T(8,128)S(1)}, u32[]{:S(2)}, u32[]{:S(2)}) collective-permute-start(f32[16,64,128]{2,0,1:T(8,128)S(1)} %get-tuple-element.21), channel_id=1, source_target_pairs={{4,0},{8,4},{12,8},{16,12},{20,16},{24,20},{28,24},{5,1},{9,5},{13... | collective-permute-start | bytes 1572872 | tf_op jit(solution)/shard_map/ppermute | solution.py:36
  380.2 4.8 copy-start.5
  384.2 0.8 copy-start.7
  436.6 17.7 %all-to-all-start.2 = ((f32[16,64,128]{2,1,0:T(8,128)}), f32[16,64,128]{2,1,0:T(8,128)S(1)}, u32[]{:S(2)}, u32[]{:S(2)}) async-start(f32[16,64,128]{2,1,0:T(8,128)} %copy.172), calls=%async_computation.2 | async-start | bytes 1048576 | tf_op jit(solution)/shard_map/all_to_all | solution.py:118
Sparse Core Ops, SparseCore 0:
  92.7 37.6 all-reduce.6
  300.4 37.3 all-reduce.8
where the time goes:
time: 487 us; the launch traced here: 486 us
  blocking collectives  155 us (32%)
  waiting for transfers between devices  111 us (23%)
  matrix products  98.5 us (20%)
  local copies, waits for them, and re-layouts  61.2 us (13%)
  other arithmetic  21.6 us (4%)
  starting transfers between devices  21.4 us (4%)
  between operations  18.1 us (4%)
    psum x2, blocking collectives, local(): misfit = lax.psum(misfit_local, ('lat', 'dep'))  95.3 us
    unnamed x4, waiting for transfers between devices  73.9 us
    gather x1, local copies, waits for them, and re-layouts, local(): foot_table[foot_id[0]]  51 us
    dot_general x2, matrix products, local(): jnp.einsum('rfd,fzocd->rzoc', lax.all_gather(weighted, 'dep', axis=0, til...  49.8 us
    dot_general x2, matrix products, local(): jnp.einsum('rzoc,fzocd->rfd', widened, chosen, preferred_element_type=jnp...  48.5 us
    all_to_all x2, blocking collectives, local(): lax.all_to_all(walsh(shrunk, local_bits + device_bits), 'dep', split_axis...  32.8 us
    all_to_all x2, waiting for transfers between devices, local(): lax.all_to_all(moved, 'dep', split_axis=0, concat_axis=1, tiled=True)  27.3 us
    all_gather x2, blocking collectives, local(): lax.all_gather(weighted, 'dep', axis=0, tiled=True)  26.4 us
  transfers between devices with their start and end apart: 12, of which 9 were waited for; matrix products, arithmetic and copies ran while one was open for 11% of the time, Pallas kernels for 0%

commit v1 on v0

v1 whole, which is shorter than its diff:
```python
import functools
import math

import jax
import jax.numpy as jnp
import numpy as np
from jax import lax
from jax.experimental import pallas as pl
from jax.experimental.pallas import tpu as pltpu
from jax.sharding import PartitionSpec as P

ITERS = 2
KSTART = 8

tiny_eps = 1e-06
f32 = jnp.float32
bf16 = jnp.bfloat16

SLOTS = 3


def momentum_list():
    ratio_now = 1.0
    ratios = [ratio_now]
    for iteration in range(KSTART + ITERS + 3):
        ratio_now = (1.0 + math.sqrt(1.0 + 4.0 * ratio_now * ratio_now)) / 2.0
        ratios.append(ratio_now)
    return [
        (ratios[KSTART - 1 + iteration] - 1.0) / ratios[KSTART + iteration]
        for iteration in range(ITERS + 1)
    ]


def signs(length):
    index = np.arange(length)
    both = index[:, None] & index[None]
    parity = np.zeros_like(both)
    while both.any():
        parity ^= both & 1
        both >>= 1
    return np.where(parity == 1, -1.0, 1.0)


def dot(a, b):
    return jnp.dot(a, b, preferred_element_type=f32)


def split_dot(matrix, values):
    upper = values.astype(bf16)
    lower = (values - upper.astype(f32)).astype(bf16)
    return dot(matrix, upper) + dot(matrix, lower)


def call(body, outs, args, prefetch=(), scratch=(), flops=0, limit=28):
    vmem = pl.BlockSpec(memory_space=pltpu.VMEM)
    size = sum(math.prod(a.shape) * a.dtype.itemsize for a in (*args, *outs))
    return pl.pallas_call(
        body,
        out_shape=tuple(outs),
        in_specs=[pl.BlockSpec(memory_space=pltpu.SMEM)] * len(prefetch) + [vmem] * len(args),
        out_specs=tuple([vmem] * len(outs)),
        scratch_shapes=list(scratch),
        compiler_params=pltpu.CompilerParams(vmem_limit_bytes=limit * 2**20),
        cost_estimate=pl.CostEstimate(flops=flops, bytes_accessed=size, transcendentals=0),
    )(*prefetch, *args)


def shape(dims, dtype):
    return jax.ShapeDtypeStruct(tuple(dims), dtype)


def prepare_kernel(count, rows, momentum, me_ref, est_ref, prev_ref, *outs):
    heads, rests = outs[:count], outs[count:]
    for slot in range(count):
        group = pl.ds((me_ref[0] ^ slot) * rows, rows)
        est = est_ref[group]
        current = est + momentum * (est - prev_ref[group])
        head = current.astype(bf16)
        heads[slot][...] = head
        rests[slot][0] = (current - head.astype(f32)).astype(bf16)
        upper = est.astype(bf16)
        rests[slot][1] = upper
        rests[slot][2] = (est - upper.astype(f32)).astype(bf16)


def choose_kernel(count, block, prints, *refs):
    ids, choose_ref = refs[:count], refs[count]
    wide = jnp.concatenate([r[...] for r in ids], axis=1)
    for pair in range(prints // 2):
        both = jnp.concatenate(
            [jnp.where(wide == 2 * pair + k, 1.0, 0.0).astype(f32) for k in (0, 1)], axis=0
        )
        choose_ref[pl.ds(pair * 2 * block, 2 * block)] = both.astype(bf16)


def choose_t_kernel(count, block, prints, spread_ref, number_ref, *refs):
    ids, choose_ref = refs[:count], refs[count]
    wide = jnp.concatenate([r[...] for r in ids], axis=1).astype(f32)
    tall = wide.T.astype(bf16)
    step = 5 * 128
    width = prints * block
    for start in range(0, width, step):
        stop = min(start + step, width)
        lanes = dot(tall, spread_ref[:, start:stop])
        choose_ref[:, start:stop] = jnp.where(lanes == number_ref[0:1, start:stop], 1.0, 0.0).astype(bf16)


def project(rows, block, frames, prints, lifted, choose_ref, table_ref, acc_ref, outs):
    per = 8 if prints % 8 == 0 else 2
    tile = table_ref.shape[1]
    total = jnp.zeros((rows * block, tile), f32)
    for start in range(0, prints, per):
        summed = dot(choose_ref[pl.ds(start * block, per * block)], lifted)
        for pair in range(per // 2):
            base = 2 * pair * block
            left = jnp.concatenate(
                [
                    jnp.concatenate(
                        [
                            summed[base + k * block : base + (k + 1) * block, r * tile : (r + 1) * tile]
                            for k in (0, 1)
                        ],
                        axis=1,
                    )
                    for r in range(rows)
                ],
                axis=0,
            )
            upper = left.astype(bf16)
            lower = (left - upper.astype(f32)).astype(bf16)
            weights = table_ref[pl.ds(start + 2 * pair, 2)].reshape(2 * tile, tile)
            total = total + dot(upper, weights) + dot(lower, weights)
    acc_ref[...] = total
    for slot in range(SLOTS):
        for r in range(rows):
            outs[slot][r] = acc_ref[pl.ds(r * block + slot * frames, frames)]


def project_kernel(count, rows, block, frames, prints, *refs):
    heads = refs[:count]
    choose_ref, table_ref = refs[count : count + 2]
    outs = refs[count + 2 : count + 2 + SLOTS]
    acc_ref = refs[count + 2 + SLOTS]
    lifted = jnp.concatenate(
        [jnp.concatenate([h[r] for r in range(rows)], axis=1) for h in heads], axis=0
    )
    project(rows, block, frames, prints, lifted, choose_ref, table_ref, acc_ref, outs)


def residual_kernel(frames, id_ref, own_ref, a_ref, b_ref, measured_ref, masks_ref, w_ref, misfit_ref, mask_ref):
    for f in range(frames):
        mask_ref[pl.ds(f, 1)] = masks_ref[pl.ds(id_ref[f], 1)]
    mask = mask_ref[...]
    total = jnp.zeros((1, mask.shape[1]), f32)
    for r in range(own_ref.shape[0]):
        projected = own_ref[r] + (a_ref[r] + b_ref[r])
        residual = mask * projected - measured_ref[r]
        total = total + jnp.sum(residual * residual, axis=0, keepdims=True)
        w_ref[r] = (mask * residual).astype(bf16)
    misfit_ref[...] = total


def back_kernel(
    rows, block, frames, prints, own_ref, a_ref, b_ref, choose_ref, table_ref, misfit_ref,
    grad_ref, sums_ref, left_ref, upper_ref, lower_ref,
):
    tile = table_ref.shape[1]
    left_ref[...] = jnp.zeros_like(left_ref)
    for slot, ref in enumerate((own_ref, a_ref, b_ref)):
        for r in range(rows):
            left_ref[pl.ds(r * block + slot * frames, frames)] = ref[r].astype(f32)
    left = left_ref[...].astype(bf16)
    per = 8 if prints % 8 == 0 else 2
    for start in range(0, prints, per):
        weights = table_ref[pl.ds(start, per)].reshape(per * tile, tile)
        spread = lax.dot_general(left, weights, (((1,), (1,)), ((), ())), preferred_element_type=f32)
        for pair in range(per // 2):
            both = jnp.concatenate(
                [
                    jnp.concatenate(
                        [
                            spread[r * block : (r + 1) * block, k * tile : (k + 1) * tile]
                            for r in range(rows)
                        ],
                        axis=1,
                    )
                    for k in (2 * pair, 2 * pair + 1)
                ],
                axis=0,
            )
            upper = both.astype(bf16)
            where = pl.ds((start + 2 * pair) * block, 2 * block)
            upper_ref[where] = upper
            lower_ref[where] = (both - upper.astype(f32)).astype(bf16)
    choose = choose_ref[...]
    gradient = dot(choose, upper_ref[...]) + dot(choose, lower_ref[...])
    grad_ref[...] = gradient
    grad_sum = jnp.sum(jnp.sum(gradient * gradient, axis=0, keepdims=True), axis=1, keepdims=True)
    misfit_sum = jnp.sum(misfit_ref[...], axis=1, keepdims=True)
    lane = lax.broadcasted_iota(jnp.int32, sums_ref.shape, 1)
    sums_ref[...] = jnp.where(lane < sums_ref.shape[1] // 2, misfit_sum, grad_sum)


def shrink(scale, sums_ref, current, grad, had_ref, limits_ref):
    total = jnp.sum(sums_ref[...], axis=0, keepdims=True)
    half = total.shape[1] // 2
    step = 0.5 * total[:, 0:1] / (total[:, half : half + 1] + tiny_eps)
    moved = current - step * grad
    coefficients = split_dot(had_ref[...], moved) * scale
    limit = step * limits_ref[...]
    limit = jnp.concatenate([limit] * (moved.shape[1] // limit.shape[1]), axis=1)
    clipped = jnp.clip(coefficients, -limit, limit)
    return moved - split_dot(had_ref[...], clipped) * scale


def first_kernel(count, rows, block, frames, prints, scale, momentum, *refs):
    heads, refs = refs[:count], refs[count:]
    rests, refs = refs[:count], refs[count:]
    sums_ref, grad_ref, had_ref, limits_ref, choose_ref, table_ref = refs[:6]
    outs, refs = refs[6 : 6 + SLOTS], refs[6 + SLOTS :]
    current_ref, refs = refs[0], refs[1:]
    fresh_refs, acc_ref = refs[:count], refs[count]

    def whole(piece):
        return jnp.concatenate(
            [jnp.concatenate([piece(s, r) for r in range(rows)], axis=1) for s in range(count)], axis=0
        )

    current = whole(lambda s, r: heads[s][r].astype(f32) + rests[s][0, r].astype(f32))
    state = whole(lambda s, r: rests[s][1, r].astype(f32) + rests[s][2, r].astype(f32))
    fresh = shrink(scale, sums_ref, current, grad_ref[...], had_ref, limits_ref)
    put_slots(fresh, fresh_refs, rows)
    current = fresh + momentum * (fresh - state)
    current_ref[...] = current
    project(rows, block, frames, prints, current.astype(bf16), choose_ref, table_ref, acc_ref, outs)


def put_slots(fresh, refs, rows):
    depth, tile = refs[0].shape[1:]
    for slot, ref in enumerate(refs):
        for r in range(rows):
            ref[r] = fresh[slot * depth : (slot + 1) * depth, r * tile : (r + 1) * tile]


def last_kernel(count, rows, scale, sums_ref, current_ref, grad_ref, had_ref, limits_ref, *fresh_refs):
    fresh = shrink(scale, sums_ref, current_ref[...], grad_ref[...], had_ref, limits_ref)
    put_slots(fresh, fresh_refs, rows)


def finish_kernel(count, rows, momentum, me_ref, *refs):
    states, fresh, (refined_ref, ahead_ref) = refs[:count], refs[count : 2 * count], refs[2 * count :]
    for slot in range(count):
        group = pl.ds((me_ref[0] ^ slot) * rows, rows)
        now = fresh[slot][...]
        refined_ref[group] = now
        ahead_ref[group] = now + momentum * (now - states[slot][...])


def depth_exchange(parts):
    count = len(parts)
    return [parts[0]] + [
        lax.ppermute(parts[s], "dep", [(i, i ^ s) for i in range(count)]) for s in range(1, count)
    ]


def partner_exchange(to_a, to_b):
    count = lax.axis_size("lat")
    pairs_a = [(i, i ^ 1) for i in range(count)]
    pairs_b = [(i, (i + 1 if i % 2 else i - 1) % count) for i in range(count)]
    return lax.ppermute(to_a, "lat", pairs_a), lax.ppermute(to_b, "lat", pairs_b)


def local(
    estimate,
    previous,
    measured,
    foot_table,
    foot_id,
    foot_lo,
    foot_count,
    mask_table,
    mask_id,
    thresholds,
):
    row_total, depth_local, tile = estimate.shape
    count = lax.axis_size("dep")
    lat_count = lax.axis_size("lat")
    rows = row_total // count
    depth = depth_local * count
    frames = measured.shape[1]
    prints = foot_table.shape[0]
    block = -(-SLOTS * frames // 8) * 8
    width = rows * tile
    momenta = momentum_list()
    scale = float(0.7071067811865476 ** (depth.bit_length() - 1))
    had = jnp.asarray(signs(depth), bf16)
    limits = jnp.broadcast_to(thresholds[:, None], (depth, tile))
    place = lax.axis_index("lat")
    me = lax.axis_index("dep").astype(jnp.int32).reshape(1)
    volume = shape((rows, depth_local, tile), f32)

    offsets = (jnp.arange(3, dtype=jnp.int32) - 1)[None, :, None]
    first = foot_lo[0][:, None]
    live = (offsets >= first) & (offsets < first + foot_count[0][:, None])
    ids = jnp.where(live, jnp.transpose(foot_id[0], (0, 2, 1)), -1)
    odd = place % 2 == 1
    lower, upper = ids[:, 0], ids[:, 2]
    ids_a, ids_b = partner_exchange(jnp.where(odd, lower, upper), jnp.where(odd, upper, lower))
    ids_b = jnp.where((place == 0) | (place == lat_count - 1), -1, ids_b)
    pad = jnp.full((block - SLOTS * frames, depth_local), -1, jnp.int32)
    ids = depth_exchange([jnp.concatenate([ids[:, 1], ids_a, ids_b, pad], axis=0)] * count)

    prepared = call(
        functools.partial(prepare_kernel, count, rows, momenta[0]),
        [shape((rows, depth_local, tile), bf16)] * count + [shape((3, rows, depth_local, tile), bf16)] * count,
        [estimate, previous],
        prefetch=[me],
    )
    heads = depth_exchange(prepared[:count])
    rests = depth_exchange(prepared[count:])

    (choose,) = call(
        functools.partial(choose_kernel, count, block, prints), [shape((prints * block, depth), bf16)], ids
    )
    lanes = np.arange(prints * block)
    spread = jnp.asarray(lanes[None] % block == np.arange(block)[:, None], bf16)
    number = jnp.asarray(np.broadcast_to(lanes // block, (8, prints * block)), f32)
    (choose_t,) = call(
        functools.partial(choose_t_kernel, count, block, prints),
        [shape((depth, prints * block), bf16)],
        [spread, number, *ids],
    )
    sizes = (count, rows, block, frames, prints)
    acc = pltpu.VMEM((rows * block, tile), f32)
    part = shape((rows, frames, tile), f32)
    work = 2 * prints * block * width * (depth + tile)
    parts = call(
        functools.partial(project_kernel, *sizes),
        [part] * SLOTS,
        [*heads, choose, foot_table],
        scratch=[acc],
        flops=work,
    )

    def step_sums(parts):
        part_a, part_b = partner_exchange(parts[1], parts[2])
        weighted, misfit = call(
            functools.partial(residual_kernel, frames),
            [shape((rows, frames, tile), bf16), shape((1, tile), f32)],
            [parts[0], part_a, part_b, measured, mask_table],
            prefetch=[mask_id[:, 0]],
            scratch=[pltpu.VMEM((frames, tile), f32)],
        )
        weighted_a, weighted_b = partner_exchange(weighted, weighted)
        gradient, sums = call(
            functools.partial(back_kernel, *sizes[1:]),
            [shape((depth, width), f32), shape((count * lat_count, tile), f32)],
            [weighted, weighted_a, weighted_b, choose_t, foot_table, misfit],
            scratch=[
                pltpu.VMEM((rows * block, tile), f32),
                pltpu.VMEM((prints * block, width), bf16),
                pltpu.VMEM((prints * block, width), bf16),
            ],
            flops=2 * work,
        )
        return gradient, lax.all_to_all(sums, ("lat", "dep"), split_axis=0, concat_axis=0, tiled=True)

    gradient, sums = step_sums(parts)
    done = call(
        functools.partial(first_kernel, *sizes, scale, momenta[1]),
        [part] * SLOTS + [shape((depth, width), f32)] + [volume] * count,
        [*heads, *rests, sums, gradient, had, limits, choose, foot_table],
        scratch=[acc],
        flops=work,
    )
    parts, current, states = done[:SLOTS], done[SLOTS], depth_exchange(done[SLOTS + 1 :])
    gradient, sums = step_sums(parts)
    fresh = depth_exchange(
        call(
            functools.partial(last_kernel, count, rows, scale),
            [volume] * count,
            [sums, current, gradient, had, limits],
        )
    )
    return call(
        functools.partial(finish_kernel, count, rows, momenta[2]),
        [shape(estimate.shape, f32)] * 2,
        [*states, *fresh],
        prefetch=[me],
    )


def solution(mesh):
    in_specs = (
        P(None, "dep", "lat"),
        P(None, "dep", "lat"),
        P("dep", None, "lat"),
        P(),
        P("lat", None, "dep", None),
        P("lat", None, "dep"),
        P("lat", None, "dep"),
        P(),
        P(None, "lat"),
        P(),
    )
    out_specs = (P(None, "dep", "lat"), P(None, "dep", "lat"))
    return jax.shard_map(local, mesh=mesh, in_specs=in_specs, out_specs=out_specs, check_vma=False)
```

time: 487 us -> 104 us (0.21)
  blocking collectives: 155 us -> 17 us
  matrix products: 98.5 us -> 0 us
  waiting for transfers between devices: 111 us -> 29.1 us
  local copies, waits for them, and re-layouts: 61.2 us -> 3 us
  other arithmetic: 21.6 us -> 1.75 us
  between operations: 18.1 us -> 0.88 us
  Pallas kernels: 0 us -> 17 us
  starting transfers between devices: 21.4 us -> 34 us
    dot_general x5 -> x0, matrix products: 98.5 us -> none  [the longest x2 49.8 us: local(): jnp.einsum('rfd,fzocd->rzoc', lax.all_gather(weighted, 'dep', axis=0, til...]
    psum x2 -> x0, blocking collectives: 95.3 us -> none  [local(): misfit = lax.psum(misfit_local, ('lat', 'dep'))]
    unnamed x4 -> x0, waiting for transfers between devices: 73.9 us -> none
    gather x1 -> x0, local copies, waits for them, and re-layouts: 51 us -> none  [local(): foot_table[foot_id[0]]]
    all_gather x2 -> x0, blocking collectives: 26.4 us -> none  [local(): lax.all_gather(weighted, 'dep', axis=0, tiled=True)]
    all_to_all x2 -> x1, waiting for transfers between devices: 27.3 us -> 3.05 us  [step_sums(): lax.all_to_all(sums, ('lat', 'dep'), split_axis=0, concat_axis=0, tiled=T...]
    pallas_call x0 -> x11, Pallas kernels: none -> 17 us  [call(): pl.pallas_call(body, out_shape=tuple(outs), in_specs=[pl.BlockSpec(memory...]
    ppermute x8 -> x25, starting transfers between devices: 13.9 us -> 30.9 us  [the longest x15 24.1 us: depth_exchange(): lax.ppermute(parts[s], 'dep', [(i, i ^ s) for i in range(count)])]
  transfers between devices with their start and end apart: 12 -> 26, of which waited for: 9 -> 11; matrix products, arithmetic and copies ran while one was open for 11% -> 0% of each run, Pallas kernels for 0% -> 7%
where the time goes in v1:
time: 104 us; the launch traced here: 103 us
  starting transfers between devices  34 us (33%)
  waiting for transfers between devices  29.1 us (28%)
  Pallas kernels  17 us (16%)
  blocking collectives  17 us (16%)
  local copies, waits for them, and re-layouts  3 us (3%)
  other arithmetic  1.75 us (2%)
    ppermute x15, starting transfers between devices, depth_exchange(): lax.ppermute(parts[s], 'dep', [(i, i ^ s) for i in range(count)])  24.1 us
    all_to_all x1, blocking collectives, step_sums(): lax.all_to_all(sums, ('lat', 'dep'), split_axis=0, concat_axis=0, tiled=T...  17 us
    pallas_call x11, Pallas kernels, call(): pl.pallas_call(body, out_shape=tuple(outs), in_specs=[pl.BlockSpec(memory...  17 us
    ppermute x15, waiting for transfers between devices, depth_exchange(): lax.ppermute(parts[s], 'dep', [(i, i ^ s) for i in range(count)])  16.3 us
    ppermute x5, waiting for transfers between devices, partner_exchange(): lax.ppermute(to_b, 'lat', pairs_b)  9.15 us
    ppermute x5, starting transfers between devices, partner_exchange(): lax.ppermute(to_b, 'lat', pairs_b)  6.64 us
    all_to_all x1, starting transfers between devices, step_sums(): lax.all_to_all(sums, ('lat', 'dep'), split_axis=0, concat_axis=0, tiled=T...  3.15 us
    all_to_all x1, waiting for transfers between devices, step_sums(): lax.all_to_all(sums, ('lat', 'dep'), split_axis=0, concat_axis=0, tiled=T...  3.05 us
  transfers between devices with their start and end apart: 26, of which 11 were waited for; matrix products, arithmetic and copies ran while one was open for 0% of the time, Pallas kernels for 7%

profile of v1, /device:TPU:0, one launch (start us, length us, event | category | flops | bytes accessed | tf_op | source)
XLA Modules:
  0.0 102.7 jit_solution(17671391915755332778)
XLA Ops:
  0.7 0.7 copy.30
  1.4 0.7 bitcast_add_fusion
  2.1 0.9 bitcast_select_fusion
  3.0 3.4 %collective-permute-start.7 = (s32[12,64]{1,0:T(8,128)S(1)}, s32[12,64]{1,0:T(8,128)S(1)}, u32[]{:S(2)}, u32[]{:S(2)}) collective-permute-start(s32[12,64]{1,0:T(8,128)S(1)} %get-tuple-element.66), channel_id=1, source_target_pairs={{0,28},{4,8},{8,4},{12,16},{16,12},{20,24},{24,20},{28,0},{1,29},{... | collective-permute-start | bytes 9224 | tf_op jit(solution)/shard_map/ppermute | solution.py:270
  6.4 0.0 collective-permute-start.6
  6.4 1.0 %copy-done.1 = f32[16,64,128]{2,1,0:T(8,128)S(1)} copy-done((f32[16,64,128]{2,1,0:T(8,128)S(1)}, f32[16,64,128]{2,1,0:T(8,128)}, u32[]{:S(2)}) %copy-start.1) | copy-done | bytes 524312
  7.5 1.0 %copy-done.2 = f32[16,64,128]{2,1,0:T(8,128)S(1)} copy-done((f32[16,64,128]{2,1,0:T(8,128)S(1)}, f32[16,64,128]{2,1,0:T(8,128)}, u32[]{:S(2)}) %copy-start.2) | copy-done | bytes 524312
  8.5 0.2 shard_map.140
  8.7 1.6 %collective-permute-start = (bf16[4,64,128]{2,1,0:T(8,128)(2,1)S(1)}, bf16[4,64,128]{2,1,0:T(8,128)(2,1)S(1)}, u32[]{:S(2)}, u32[]{:S(2)}) collective-permute-start(bf16[4,64,128]{2,1,0:T(8,128)(2,1)S(1)} %get-tuple-element.34), channel_id=1, source_target_pairs={{0,1},{1,0},{2,3},{3,2},{4,5},{5,4},{6,7},{7,6},{8,9},{9,8},{10,11... | collective-permute-start | bytes 196616 | tf_op jit(solution)/shard_map/ppermute | solution.py:262
  10.3 2.6 %collective-permute-start.1 = (bf16[4,64,128]{2,1,0:T(8,128)(2,1)S(1)}, bf16[4,64,128]{2,1,0:T(8,128)(2,1)S(1)}, u32[]{:S(2)}, u32[]{:S(2)}) collective-permute-start(bf16[4,64,128]{2,1,0:T(8,128)(2,1)S(1)} %get-tuple-element.35), channel_id=1, source_target_pairs={{0,2},{1,3},{2,0},{3,1},{4,6},{5,7},{6,4},{7,5},{8,10},{9,11},{10,... | collective-permute-start | bytes 196616 | tf_op jit(solution)/shard_map/ppermute | solution.py:262
  12.9 0.2 collective-permute-start.2
  13.1 0.1 pad.3.clone
  13.2 0.0 collective-permute-done.6
  13.2 0.1 add_add_fusion.refs_0_
  13.3 3.6 %collective-permute-start.10 = (s32[40,64]{1,0:T(8,128)S(1)}, s32[40,64]{1,0:T(8,128)S(1)}, u32[]{:S(2)}, u32[]{:S(2)}) collective-permute-start(s32[40,64]{1,0:T(8,128)S(1)} %add_add_fusion.refs_0_), channel_id=1, source_target_pairs={{0,3},{1,2},{2,1},{3,0},{4,7},{5,6},{6,5},{7,4},{8,11},{9,10},{10,... | collective-permute-start | bytes 30728 | tf_op jit(solution)/shard_map/ppermute | solution.py:262
  16.9 2.5 %collective-permute-done.10.refs_3_ = s32[40,64]{1,0:T(8,128)S(1)} collective-permute-done((s32[40,64]{1,0:T(8,128)S(1)}, s32[40,64]{1,0:T(8,128)S(1)}, u32[]{:S(2)}, u32[]{:S(2)}) %collective-permute-start.10) | collective-permute-done | bytes 10272 | tf_op jit(solution)/shard_map/ppermute | solution.py:262
  19.4 2.4 %collective-permute-start.8 = (s32[40,64]{1,0:T(8,128)S(1)}, s32[40,64]{1,0:T(8,128)S(1)}, u32[]{:S(2)}, u32[]{:S(2)}) collective-permute-start(s32[40,64]{1,0:T(8,128)S(1)} %add_add_fusion.refs_0_), channel_id=1, source_target_pairs={{0,1},{1,0},{2,3},{3,2},{4,5},{5,4},{6,7},{7,6},{8,9},{9,8},{10,11... | collective-permute-start | bytes 30728 | tf_op jit(solution)/shard_map/ppermute | solution.py:262
  21.8 0.0 collective-permute-done.9.refs_2_
  21.8 1.8 %collective-permute-done.8.refs_1_ = s32[40,64]{1,0:T(8,128)S(1)} collective-permute-done((s32[40,64]{1,0:T(8,128)S(1)}, s32[40,64]{1,0:T(8,128)S(1)}, u32[]{:S(2)}, u32[]{:S(2)}) %collective-permute-start.8) | collective-permute-done | bytes 10272 | tf_op jit(solution)/shard_map/ppermute | solution.py:262
  23.6 0.3 shard_map.141.refs_4_.refs_12_
  23.8 0.0 collective-permute-done.1.refs_2_
  23.9 0.0 collective-permute-done.2.refs_3_
  23.9 0.0 copy-start.10
  23.9 0.0 copy-start.6
  23.9 0.0 copy-start.7
  23.9 0.0 copy-start.4
  23.9 0.0 copy-start.5
  23.9 2.8 %shard_map.142 = (f32[4,12,128]{2,1,0:T(8,128)S(1)}, f32[4,12,128]{2,1,0:T(8,128)S(1)}, f32[4,12,128]{2,1,0:T(8,128)S(1)}) custom-call(bf16[4,64,128]{2,1,0:T(8,128)(2,1)S(1)} %get-tuple-element.33.refs_0_, bf16[4,64,128]{2,1,0:T(8,128)(2,1)S(1)} %collective-permute-done.refs_1_, bf16[4,64,128]{2,1,0:T(8,128)(2,1)S(1)} %collective-permute-done.1.refs_2_, ...), custom_call_target="tpu_custom_call" | custom-call | flops 1006632960 | bytes 3743744 | tf_op jit(solution)/shard_map/pallas_call | solution.py:57
  26.7 0.1 collective-permute-start.11
  26.8 0.8 collective-permute-start.12
  27.6 0.4 collective-permute-done.11.a_ref
  28.0 3.4 %collective-permute-done.12.b_ref = f32[4,12,128]{2,1,0:T(8,128)S(1)} collective-permute-done((f32[4,12,128]{2,1,0:T(8,128)S(1)}, f32[4,12,128]{2,1,0:T(8,128)S(1)}, u32[]{:S(2)}, u32[]{:S(2)}) %collective-permute-start.12) | collective-permute-done | bytes 24608 | tf_op jit(solution)/shard_map/ppermute | solution.py:270
  31.4 0.6 shard_map.143
  31.9 0.5 collective-permute-start.14
  32.5 2.0 %collective-permute-start.3 = (bf16[3,4,64,128]{3,2,1,0:T(8,128)(2,1)S(1)}, bf16[3,4,64,128]{3,2,1,0:T(8,128)(2,1)S(1)}, u32[]{:S(2)}, u32[]{:S(2)}) collective-permute-start(bf16[3,4,64,128]{3,2,1,0:T(8,128)(2,1)S(1)} %get-tuple-element.38), channel_id=1, source_target_pairs={{0,1},{1,0},{2,3},{3,2},{4,5},{5,4},{6,7},{7,6},{8,9},{9,8},{10,11... | collective-permute-start | bytes 589832 | tf_op jit(solution)/shard_map/ppermute | solution.py:262
  34.5 1.8 %collective-permute-start.4 = (bf16[3,4,64,128]{3,2,1,0:T(8,128)(2,1)S(1)}, bf16[3,4,64,128]{3,2,1,0:T(8,128)(2,1)S(1)}, u32[]{:S(2)}, u32[]{:S(2)}) collective-permute-start(bf16[3,4,64,128]{3,2,1,0:T(8,128)(2,1)S(1)} %get-tuple-element.39), channel_id=1, source_target_pairs={{0,2},{1,3},{2,0},{3,1},{4,6},{5,7},{6,4},{7,5},{8,10},{9,11},{10,... | collective-permute-start | bytes 589832 | tf_op jit(solution)/shard_map/ppermute | solution.py:262
  36.3 0.6 collective-permute-start.5
  36.9 0.6 shard_map.144.choose_ref
  37.6 0.0 copy-start.11
  37.6 0.0 copy-start.3
  37.6 2.3 %shard_map.145 = (f32[256,512]{1,0:T(8,128)S(1)}, f32[32,128]{1,0:T(8,128)S(1)}) custom-call(bf16[4,12,128]{2,1,0:T(8,128)(2,1)S(1)} %get-tuple-element.44.own_ref, bf16[4,12,128]{2,1,0:T(8,128)(2,1)S(1)} %collective-permute-done.13.a_ref, bf16[4,12,128]{2,1,0:T(8,128)(2,1)S(1)} %collective-permute-done.14.b_ref, ...), custom_call_target="tpu_custom_call" | custom-call | flops 2013265920 | bytes 3985920 | tf_op jit(solution)/shard_map/pallas_call | solution.py:57
  39.9 17.0 %all_to_all.22 = f32[32,1,128]{2,1,0:T(1,128)S(1)} all-to-all(f32[32,1,128]{2,1,0:T(1,128)S(1)} %bitcast.29), channel_id=1, replica_groups=mesh['lat'=8,'dep'=4] {'lat','dep'}, dimensions={0} | all-to-all | bytes 32768 | tf_op jit(solution)/shard_map/all_to_all | solution.py:366
  56.9 0.1 broadcast_in_dim.21.refs_11_.limits_ref
  57.0 4.1 %shard_map.146 = (f32[4,12,128]{2,1,0:T(8,128)S(1)}, f32[4,12,128]{2,1,0:T(8,128)S(1)}, f32[4,12,128]{2,1,0:T(8,128)S(1)}, f32[256,512]{1,0:T(8,128)S(1)}, f32[4...) custom-call(bf16[4,64,128]{2,1,0:T(8,128)(2,1)S(1)} %get-tuple-element.33.r, ...), custom_call_target="tpu_custom_call" | custom-call | flops 1006632960 | bytes 6381568 | tf_op jit(solution)/shard_map/pallas_call | solution.py:57
  61.1 1.0 collective-permute-start.19
  62.1 0.2 collective-permute-done.18.a_ref
  62.3 3.2 %collective-permute-done.19.b_ref = f32[4,12,128]{2,1,0:T(8,128)S(1)} collective-permute-done((f32[4,12,128]{2,1,0:T(8,128)S(1)}, f32[4,12,128]{2,1,0:T(8,128)S(1)}, u32[]{:S(2)}, u32[]{:S(2)}) %collective-permute-start.19) | collective-permute-done | bytes 24608 | tf_op jit(solution)/shard_map/ppermute | solution.py:270
  65.5 0.6 shard_map.147
  66.1 0.9 collective-permute-start.21
  67.0 0.6 collective-permute-start.15
  67.6 2.6 %collective-permute-done.21.b_ref = bf16[4,12,128]{2,1,0:T(8,128)(2,1)S(1)} collective-permute-done((bf16[4,12,128]{2,1,0:T(8,128)(2,1)S(1)}, bf16[4,12,128]{2,1,0:T(8,128)(2,1)S(1)}, u32[]{:S(2)}, u32[]{:S(2)}) %collective-permute-start.21) | collective-permute-done | bytes 12320 | tf_op jit(solution)/shard_map/ppermute | solution.py:270
  70.2 2.9 %shard_map.148 = (f32[256,512]{1,0:T(8,128)S(1)}, f32[32,128]{1,0:T(8,128)}) custom-call(bf16[4,12,128]{2,1,0:T(8,128)(2,1)S(1)} %get-tuple-element.55.own_ref, bf16[4,12,128]{2,1,0:T(8,128)(2,1)S(1)} %collective-permute-done.20.a_ref, bf16[4,12,128]{2,1,0:T(8,128)(2,1)S(1)} %collective-permute-done.21.b_ref, bf16[256,2560]{1,0:T(8,128)(2,1)S(1)} %shard_map.144.choose_ref, ...), custom_call_target="tpu_custom_call" | custom-call | flops 2013265920 | bytes 3985920 | tf_op jit(solution)/shard_map/pallas_call | solution.py:57
  73.1 3.1 %all-to-all-start.1 = ((f32[32,1,128]{2,1,0:T(1,128)}), f32[32,1,128]{2,1,0:T(1,128)S(1)}, u32[]{:S(2)}, u32[]{:S(2)}) async-start(f32[32,1,128]{2,1,0:T(1,128)} %bitcast.11), calls=%async_computation.1 | async-start | bytes 32768 | tf_op jit(solution)/shard_map/all_to_all | solution.py:366
  76.2 2.7 %collective-permute-start.16 = (f32[4,64,128]{2,1,0:T(8,128)}, f32[4,64,128]{2,1,0:T(8,128)S(1)}, u32[]{:S(2)}, u32[]{:S(2)}) collective-permute-start(f32[4,64,128]{2,1,0:T(8,128)} %copy-done.9), channel_id=1, source_target_pairs={{0,2},{1,3},{2,0},{3,1},{4,6},{5,7},{6,4},{7,5},{8,10},{9,11},{10,... | collective-permute-start | bytes 393224 | tf_op jit(solution)/shard_map/ppermute | solution.py:262
  79.0 1.5 %collective-permute-start.17 = (f32[4,64,128]{2,1,0:T(8,128)}, f32[4,64,128]{2,1,0:T(8,128)S(1)}, u32[]{:S(2)}, u32[]{:S(2)}) collective-permute-start(f32[4,64,128]{2,1,0:T(8,128)} %copy-done.8), channel_id=1, source_target_pairs={{0,3},{1,2},{2,1},{3,0},{4,7},{5,6},{6,5},{7,4},{8,11},{9,10},{10,... | collective-permute-start | bytes 393224 | tf_op jit(solution)/shard_map/ppermute | solution.py:262
  80.4 3.1 %all-to-all-done.1 = f32[32,1,128]{2,1,0:T(1,128)S(1)} async-done(((f32[32,1,128]{2,1,0:T(1,128)}), f32[32,1,128]{2,1,0:T(1,128)S(1)}, u32[]{:S(2)}, u32[]{:S(2)}) %all-to-all-start.1) | async-done | bytes 16416 | tf_op jit(solution)/shard_map/all_to_all | solution.py:366
  83.5 0.8 shard_map.149
  84.3 0.5 collective-permute-start.22
  84.8 0.6 collective-permute-start.23
  85.4 3.4 %collective-permute-start.24 = (f32[4,64,128]{2,1,0:T(8,128)S(1)}, f32[4,64,128]{2,1,0:T(8,128)S(1)}, u32[]{:S(2)}, u32[]{:S(2)}) collective-permute-start(f32[4,64,128]{2,1,0:T(8,128)S(1)} %get-tuple-element.63), channel_id=1, source_target_pairs={{0,3},{1,2},{2,1},{3,0},{4,7},{5,6},{6,5},{7,4},{8,11},{9,10},{10,... | collective-permute-start | bytes 393224 | tf_op jit(solution)/shard_map/ppermute | solution.py:262
  88.8 1.2 %collective-permute-done.16.refs_2_ = f32[4,64,128]{2,1,0:T(8,128)S(1)} collective-permute-done((f32[4,64,128]{2,1,0:T(8,128)}, f32[4,64,128]{2,1,0:T(8,128)S(1)}, u32[]{:S(2)}, u32[]{:S(2)}) %collective-permute-start.16) | collective-permute-done | bytes 131104 | tf_op jit(solution)/shard_map/ppermute | solution.py:262
  90.0 1.8 %collective-permute-done.22.refs_5_ = f32[4,64,128]{2,1,0:T(8,128)S(1)} collective-permute-done((f32[4,64,128]{2,1,0:T(8,128)S(1)}, f32[4,64,128]{2,1,0:T(8,128)S(1)}, u32[]{:S(2)}, u32[]{:S(2)}) %collective-permute-start.22) | collective-permute-done | bytes 131104 | tf_op jit(solution)/shard_map/ppermute | solution.py:262
  91.8 9.0 %collective-permute-done.23.refs_6_ = f32[4,64,128]{2,1,0:T(8,128)S(1)} collective-permute-done((f32[4,64,128]{2,1,0:T(8,128)S(1)}, f32[4,64,128]{2,1,0:T(8,128)S(1)}, u32[]{:S(2)}, u32[]{:S(2)}) %collective-permute-start.23) | collective-permute-done | bytes 131104 | tf_op jit(solution)/shard_map/ppermute | solution.py:262
  100.8 1.9 %shard_map.150 = (f32[16,64,128]{2,1,0:T(8,128)}, f32[16,64,128]{2,1,0:T(8,128)}) custom-call(s32[1]{0:T(128)} %bitcast.me_ref, f32[4,64,128]{2,1,0:T(8,128)S(1)} %get-tuple-element.48.refs_0_, f32[4,64,128]{2,1,0:T(8,128)} %collective-permute-done.15.refs_1_, f32[4,64,128]{2,1,0:T(8,128)S(1)} %collective-permute-done.16.refs_2_, ...), custom_call_target="tpu_custom_call" | custom-call | bytes 2097152 | tf_op jit(solution)/shard_map/pallas_call | solution.py:57
  (35 shorter events, 0.1 us)
Async XLA Ops:
  2.1 21.8 %copy-start = (bf16[64,128,128]{2,1,0:T(8,128)(2,1)S(1)}, bf16[64,128,128]{2,1,0:T(8,128)(2,1)}, u32[]{:S(2)}) copy-start(bf16[64,128,128]{2,1,0:T(8,128)(2,1)} %table_ref.3) | copy-start | bytes 6291460
  3.0 10.2 %collective-permute-start.7 = (s32[12,64]{1,0:T(8,128)S(1)}, s32[12,64]{1,0:T(8,128)S(1)}, u32[]{:S(2)}, u32[]{:S(2)}) collective-permute-start(s32[12,64]{1,0:T(8,128)S(1)} %get-tuple-element.66), channel_id=1, source_target_pairs={{0,28},{4,8},{8,4},{12,16},{16,12},{20,24},{24,20},{28,0},{1,29},{... | collective-permute-start | bytes 9224 | tf_op jit(solution)/shard_map/ppermute | solution.py:270
  6.4 6.8 %collective-permute-start.6 = (s32[12,64]{1,0:T(8,128)S(1)}, s32[12,64]{1,0:T(8,128)S(1)}, u32[]{:S(2)}, u32[]{:S(2)}) collective-permute-start(s32[12,64]{1,0:T(8,128)S(1)} %get-tuple-element.65), channel_id=1, source_target_pairs={{0,4},{4,0},{8,12},{12,8},{16,20},{20,16},{24,28},{28,24},{1,5},{5... | collective-permute-start | bytes 9224 | tf_op jit(solution)/shard_map/ppermute | solution.py:270
  6.4 1.0 %copy-start.1 = (f32[16,64,128]{2,1,0:T(8,128)S(1)}, f32[16,64,128]{2,1,0:T(8,128)}, u32[]{:S(2)}) copy-start(f32[16,64,128]{2,1,0:T(8,128)} %est_ref.1) | copy-start | bytes 1572868
  7.5 1.0 %copy-start.2 = (f32[16,64,128]{2,1,0:T(8,128)S(1)}, f32[16,64,128]{2,1,0:T(8,128)}, u32[]{:S(2)}) copy-start(f32[16,64,128]{2,1,0:T(8,128)} %prev_ref.1) | copy-start | bytes 1572868
  8.7 15.2 %collective-permute-start = (bf16[4,64,128]{2,1,0:T(8,128)(2,1)S(1)}, bf16[4,64,128]{2,1,0:T(8,128)(2,1)S(1)}, u32[]{:S(2)}, u32[]{:S(2)}) collective-permute-start(bf16[4,64,128]{2,1,0:T(8,128)(2,1)S(1)} %get-tuple-element.34), channel_id=1, source_target_pairs={{0,1},{1,0},{2,3},{3,2},{4,5},{5,4},{6,7},{7,6},{8,9},{9,8},{10,11... | collective-permute-start | bytes 196616 | tf_op jit(solution)/shard_map/ppermute | solution.py:262
  10.3 13.5 %collective-permute-start.1 = (bf16[4,64,128]{2,1,0:T(8,128)(2,1)S(1)}, bf16[4,64,128]{2,1,0:T(8,128)(2,1)S(1)}, u32[]{:S(2)}, u32[]{:S(2)}) collective-permute-start(bf16[4,64,128]{2,1,0:T(8,128)(2,1)S(1)} %get-tuple-element.35), channel_id=1, source_target_pairs={{0,2},{1,3},{2,0},{3,1},{4,6},{5,7},{6,4},{7,5},{8,10},{9,11},{10,... | collective-permute-start | bytes 196616 | tf_op jit(solution)/shard_map/ppermute | solution.py:262
  12.9 11.0 %collective-permute-start.2 = (bf16[4,64,128]{2,1,0:T(8,128)(2,1)S(1)}, bf16[4,64,128]{2,1,0:T(8,128)(2,1)S(1)}, u32[]{:S(2)}, u32[]{:S(2)}) collective-permute-start(bf16[4,64,128]{2,1,0:T(8,128)(2,1)S(1)} %get-tuple-element.36), channel_id=1, source_target_pairs={{0,3},{1,2},{2,1},{3,0},{4,7},{5,6},{6,5},{7,4},{8,11},{9,10},{10,... | collective-permute-start | bytes 196616 | tf_op jit(solution)/shard_map/ppermute | solution.py:262
  13.3 6.1 %collective-permute-start.10 = (s32[40,64]{1,0:T(8,128)S(1)}, s32[40,64]{1,0:T(8,128)S(1)}, u32[]{:S(2)}, u32[]{:S(2)}) collective-permute-start(s32[40,64]{1,0:T(8,128)S(1)} %add_add_fusion.refs_0_), channel_id=1, source_target_pairs={{0,3},{1,2},{2,1},{3,0},{4,7},{5,6},{6,5},{7,4},{8,11},{9,10},{10,... | collective-permute-start | bytes 30728 | tf_op jit(solution)/shard_map/ppermute | solution.py:262
  16.9 4.9 %collective-permute-start.9 = (s32[40,64]{1,0:T(8,128)S(1)}, s32[40,64]{1,0:T(8,128)S(1)}, u32[]{:S(2)}, u32[]{:S(2)}) collective-permute-start(s32[40,64]{1,0:T(8,128)S(1)} %add_add_fusion.refs_0_), channel_id=1, source_target_pairs={{0,2},{1,3},{2,0},{3,1},{4,6},{5,7},{6,4},{7,5},{8,10},{9,11},{10,... | collective-permute-start | bytes 30728 | tf_op jit(solution)/shard_map/ppermute | solution.py:262
  19.4 4.1 %collective-permute-start.8 = (s32[40,64]{1,0:T(8,128)S(1)}, s32[40,64]{1,0:T(8,128)S(1)}, u32[]{:S(2)}, u32[]{:S(2)}) collective-permute-start(s32[40,64]{1,0:T(8,128)S(1)} %add_add_fusion.refs_0_), channel_id=1, source_target_pairs={{0,1},{1,0},{2,3},{3,2},{4,5},{5,4},{6,7},{7,6},{8,9},{9,8},{10,11... | collective-permute-start | bytes 30728 | tf_op jit(solution)/shard_map/ppermute | solution.py:262
  23.9 3.7 %copy-start.10 = (f32[4,12,128]{2,0,1:T(4,128)S(1)}, f32[4,12,128]{2,0,1:T(4,128)}, u32[]{:S(2)}) copy-start(f32[4,12,128]{2,0,1:T(4,128)} %param.15) | copy-start | bytes 73732
  23.9 7.5 %copy-start.6 = (f32[16,128]{1,0:T(8,128)S(1)}, f32[16,128]{1,0:T(8,128)}, u32[]{:S(2)}) copy-start(f32[16,128]{1,0:T(8,128)} %masks_ref.3) | copy-start | bytes 24580
  23.9 7.5 %copy-start.7 = (s32[12,1]{0,1:T(1,128)S(1)}, s32[12,1]{0,1:T(1,128)}, u32[]{:S(2)}) copy-start(s32[12,1]{0,1:T(1,128)} %param.21) | copy-start | bytes 148
  23.9 13.0 %copy-start.4 = (bf16[40,2560]{1,0:T(8,128)(2,1)S(1)}, bf16[40,2560]{1,0:T(8,128)(2,1)}, u32[]{:S(2)}) copy-start(bf16[40,2560]{1,0:T(8,128)(2,1)} %constant.38.clone.spread_ref) | copy-start | bytes 614404
  23.9 13.0 %copy-start.5 = (f32[8,2560]{1,0:T(8,128)S(1)}, f32[8,2560]{1,0:T(8,128)}, u32[]{:S(2)}) copy-start(f32[8,2560]{1,0:T(8,128)} %constant.39.clone.number_ref) | copy-start | bytes 245764
  26.7 1.3 %collective-permute-start.11 = (f32[4,12,128]{2,1,0:T(8,128)S(1)}, f32[4,12,128]{2,1,0:T(8,128)S(1)}, u32[]{:S(2)}, u32[]{:S(2)}) collective-permute-start(f32[4,12,128]{2,1,0:T(8,128)S(1)} %get-tuple-element.42), channel_id=1, source_target_pairs={{0,4},{4,0},{8,12},{12,8},{16,20},{20,16},{24,28},{28,24},{1,5},{5... | collective-permute-start | bytes 73736 | tf_op jit(solution)/shard_map/ppermute | solution.py:270
  26.8 4.6 %collective-permute-start.12 = (f32[4,12,128]{2,1,0:T(8,128)S(1)}, f32[4,12,128]{2,1,0:T(8,128)S(1)}, u32[]{:S(2)}, u32[]{:S(2)}) collective-permute-start(f32[4,12,128]{2,1,0:T(8,128)S(1)} %get-tuple-element.43), channel_id=1, source_target_pairs={{0,28},{4,8},{8,4},{12,16},{16,12},{20,24},{24,20},{28,0},{1,29},{... | collective-permute-start | bytes 73736 | tf_op jit(solution)/shard_map/ppermute | solution.py:270
  31.9 5.6 %collective-permute-start.14 = (bf16[4,12,128]{2,1,0:T(8,128)(2,1)S(1)}, bf16[4,12,128]{2,1,0:T(8,128)(2,1)S(1)}, u32[]{:S(2)}, u32[]{:S(2)}) collective-permute-start(bf16[4,12,128]{2,1,0:T(8,128)(2,1)S(1)} %get-tuple-element.44.own_ref), channel_id=1, source_target_pairs={{0,28},{4,8},{8,4},{12,16},{16,12},{20,24},{24,20},{28,0},{1,29},{... | collective-permute-start | bytes 36872 | tf_op jit(solution)/shard_map/ppermute | solution.py:270
  32.5 5.1 %collective-permute-start.13 = (bf16[4,12,128]{2,1,0:T(8,128)(2,1)S(1)}, bf16[4,12,128]{2,1,0:T(8,128)(2,1)S(1)}, u32[]{:S(2)}, u32[]{:S(2)}) collective-permute-start(bf16[4,12,128]{2,1,0:T(8,128)(2,1)S(1)} %get-tuple-element.44.own_ref), channel_id=1, source_target_pairs={{0,4},{4,0},{8,12},{12,8},{16,20},{20,16},{24,28},{28,24},{1,5},{5... | collective-permute-start | bytes 36872 | tf_op jit(solution)/shard_map/ppermute | solution.py:270
  32.5 24.4 %collective-permute-start.3 = (bf16[3,4,64,128]{3,2,1,0:T(8,128)(2,1)S(1)}, bf16[3,4,64,128]{3,2,1,0:T(8,128)(2,1)S(1)}, u32[]{:S(2)}, u32[]{:S(2)}) collective-permute-start(bf16[3,4,64,128]{3,2,1,0:T(8,128)(2,1)S(1)} %get-tuple-element.38), channel_id=1, source_target_pairs={{0,1},{1,0},{2,3},{3,2},{4,5},{5,4},{6,7},{7,6},{8,9},{9,8},{10,11... | collective-permute-start | bytes 589832 | tf_op jit(solution)/shard_map/ppermute | solution.py:262
  34.5 22.4 %collective-permute-start.4 = (bf16[3,4,64,128]{3,2,1,0:T(8,128)(2,1)S(1)}, bf16[3,4,64,128]{3,2,1,0:T(8,128)(2,1)S(1)}, u32[]{:S(2)}, u32[]{:S(2)}) collective-permute-start(bf16[3,4,64,128]{3,2,1,0:T(8,128)(2,1)S(1)} %get-tuple-element.39), channel_id=1, source_target_pairs={{0,2},{1,3},{2,0},{3,1},{4,6},{5,7},{6,4},{7,5},{8,10},{9,11},{10,... | collective-permute-start | bytes 589832 | tf_op jit(solution)/shard_map/ppermute | solution.py:262
  36.3 20.6 %collective-permute-start.5 = (bf16[3,4,64,128]{3,2,1,0:T(8,128)(2,1)S(1)}, bf16[3,4,64,128]{3,2,1,0:T(8,128)(2,1)S(1)}, u32[]{:S(2)}, u32[]{:S(2)}) collective-permute-start(bf16[3,4,64,128]{3,2,1,0:T(8,128)(2,1)S(1)} %get-tuple-element.40), channel_id=1, source_target_pairs={{0,3},{1,2},{2,1},{3,0},{4,7},{5,6},{6,5},{7,4},{8,11},{9,10},{10,... | collective-permute-start | bytes 589832 | tf_op jit(solution)/shard_map/ppermute | solution.py:262
  37.6 19.3 %copy-start.11 = (f32[256]{0:T(256)S(1)}, f32[256]{0:T(256)}, u32[]{:S(2)}) copy-start(f32[256]{0:T(256)} %param.22) | copy-start | bytes 3076
  37.6 19.4 %copy-start.3 = (bf16[256,256]{1,0:T(8,128)(2,1)S(1)}, bf16[256,256]{1,0:T(8,128)(2,1)}, u32[]{:S(2)}) copy-start(bf16[256,256]{1,0:T(8,128)(2,1)} %constant.37.clone.refs_10_.had_ref) | copy-start | bytes 393220
  61.1 12.0 %copy-start.8 = (f32[4,64,128]{2,1,0:T(8,128)}, f32[4,64,128]{2,1,0:T(8,128)S(1)}, u32[]{:S(2)}) copy-start(f32[4,64,128]{2,1,0:T(8,128)S(1)} %get-tuple-element.51) | copy-start | bytes 393220
  61.1 12.0 %copy-start.9 = (f32[4,64,128]{2,1,0:T(8,128)}, f32[4,64,128]{2,1,0:T(8,128)S(1)}, u32[]{:S(2)}) copy-start(f32[4,64,128]{2,1,0:T(8,128)S(1)} %get-tuple-element.50) | copy-start | bytes 393220
  61.1 1.2 %collective-permute-start.18 = (f32[4,12,128]{2,1,0:T(8,128)S(1)}, f32[4,12,128]{2,1,0:T(8,128)S(1)}, u32[]{:S(2)}, u32[]{:S(2)}) collective-permute-start(f32[4,12,128]{2,1,0:T(8,128)S(1)} %get-tuple-element.53), channel_id=1, source_target_pairs={{0,4},{4,0},{8,12},{12,8},{16,20},{20,16},{24,28},{28,24},{1,5},{5... | collective-permute-start | bytes 73736 | tf_op jit(solution)/shard_map/ppermute | solution.py:270
  61.1 4.4 %collective-permute-start.19 = (f32[4,12,128]{2,1,0:T(8,128)S(1)}, f32[4,12,128]{2,1,0:T(8,128)S(1)}, u32[]{:S(2)}, u32[]{:S(2)}) collective-permute-start(f32[4,12,128]{2,1,0:T(8,128)S(1)} %get-tuple-element.54), channel_id=1, source_target_pairs={{0,28},{4,8},{8,4},{12,16},{16,12},{20,24},{24,20},{28,0},{1,29},{... | collective-permute-start | bytes 73736 | tf_op jit(solution)/shard_map/ppermute | solution.py:270
  66.1 4.1 %collective-permute-start.21 = (bf16[4,12,128]{2,1,0:T(8,128)(2,1)S(1)}, bf16[4,12,128]{2,1,0:T(8,128)(2,1)S(1)}, u32[]{:S(2)}, u32[]{:S(2)}) collective-permute-start(bf16[4,12,128]{2,1,0:T(8,128)(2,1)S(1)} %get-tuple-element.55.own_ref), channel_id=1, source_target_pairs={{0,28},{4,8},{8,4},{12,16},{16,12},{20,24},{24,20},{28,0},{1,29},{... | collective-permute-start | bytes 36872 | tf_op jit(solution)/shard_map/ppermute | solution.py:270
  67.0 3.2 %collective-permute-start.20 = (bf16[4,12,128]{2,1,0:T(8,128)(2,1)S(1)}, bf16[4,12,128]{2,1,0:T(8,128)(2,1)S(1)}, u32[]{:S(2)}, u32[]{:S(2)}) collective-permute-start(bf16[4,12,128]{2,1,0:T(8,128)(2,1)S(1)} %get-tuple-element.55.own_ref), channel_id=1, source_target_pairs={{0,4},{4,0},{8,12},{12,8},{16,20},{20,16},{24,28},{28,24},{1,5},{5... | collective-permute-start | bytes 36872 | tf_op jit(solution)/shard_map/ppermute | solution.py:270
  67.0 18.4 %collective-permute-start.15 = (f32[4,64,128]{2,1,0:T(8,128)}, f32[4,64,128]{2,1,0:T(8,128)}, u32[]{:S(2)}, u32[]{:S(2)}) collective-permute-start(f32[4,64,128]{2,1,0:T(8,128)} %get-tuple-element.49), channel_id=1, source_target_pairs={{0,1},{1,0},{2,3},{3,2},{4,5},{5,4},{6,7},{7,6},{8,9},{9,8},{10,11... | collective-permute-start | bytes 393224 | tf_op jit(solution)/shard_map/ppermute | solution.py:262
  73.1 10.4 %all-to-all-start.1 = ((f32[32,1,128]{2,1,0:T(1,128)}), f32[32,1,128]{2,1,0:T(1,128)S(1)}, u32[]{:S(2)}, u32[]{:S(2)}) async-start(f32[32,1,128]{2,1,0:T(1,128)} %bitcast.11), calls=%async_computation.1 | async-start | bytes 32768 | tf_op jit(solution)/shard_map/all_to_all | solution.py:366
  76.2 13.7 %collective-permute-start.16 = (f32[4,64,128]{2,1,0:T(8,128)}, f32[4,64,128]{2,1,0:T(8,128)S(1)}, u32[]{:S(2)}, u32[]{:S(2)}) collective-permute-start(f32[4,64,128]{2,1,0:T(8,128)} %copy-done.9), channel_id=1, source_target_pairs={{0,2},{1,3},{2,0},{3,1},{4,6},{5,7},{6,4},{7,5},{8,10},{9,11},{10,... | collective-permute-start | bytes 393224 | tf_op jit(solution)/shard_map/ppermute | solution.py:262
  79.0 11.0 %collective-permute-start.17 = (f32[4,64,128]{2,1,0:T(8,128)}, f32[4,64,128]{2,1,0:T(8,128)S(1)}, u32[]{:S(2)}, u32[]{:S(2)}) collective-permute-start(f32[4,64,128]{2,1,0:T(8,128)} %copy-done.8), channel_id=1, source_target_pairs={{0,3},{1,2},{2,1},{3,0},{4,7},{5,6},{6,5},{7,4},{8,11},{9,10},{10,... | collective-permute-start | bytes 393224 | tf_op jit(solution)/shard_map/ppermute | solution.py:262
  84.3 7.5 %collective-permute-start.22 = (f32[4,64,128]{2,1,0:T(8,128)S(1)}, f32[4,64,128]{2,1,0:T(8,128)S(1)}, u32[]{:S(2)}, u32[]{:S(2)}) collective-permute-start(f32[4,64,128]{2,1,0:T(8,128)S(1)} %get-tuple-element.61), channel_id=1, source_target_pairs={{0,1},{1,0},{2,3},{3,2},{4,5},{5,4},{6,7},{7,6},{8,9},{9,8},{10,11... | collective-permute-start | bytes 393224 | tf_op jit(solution)/shard_map/ppermute | solution.py:262
  84.8 16.0 %collective-permute-start.23 = (f32[4,64,128]{2,1,0:T(8,128)S(1)}, f32[4,64,128]{2,1,0:T(8,128)S(1)}, u32[]{:S(2)}, u32[]{:S(2)}) collective-permute-start(f32[4,64,128]{2,1,0:T(8,128)S(1)} %get-tuple-element.62), channel_id=1, source_target_pairs={{0,2},{1,3},{2,0},{3,1},{4,6},{5,7},{6,4},{7,5},{8,10},{9,11},{10,... | collective-permute-start | bytes 393224 | tf_op jit(solution)/shard_map/ppermute | solution.py:262
  85.4 15.4 %collective-permute-start.24 = (f32[4,64,128]{2,1,0:T(8,128)S(1)}, f32[4,64,128]{2,1,0:T(8,128)S(1)}, u32[]{:S(2)}, u32[]{:S(2)}) collective-permute-start(f32[4,64,128]{2,1,0:T(8,128)S(1)} %get-tuple-element.63), channel_id=1, source_target_pairs={{0,3},{1,2},{2,1},{3,0},{4,7},{5,6},{6,5},{7,4},{8,11},{9,10},{10,... | collective-permute-start | bytes 393224 | tf_op jit(solution)/shard_map/ppermute | solution.py:262

commit v2 on v1

v2 whole, which is shorter than its diff:
```python
import functools
import math

import jax
import jax.numpy as jnp
import numpy as np
from jax import lax
from jax.experimental import pallas as pl
from jax.experimental.pallas import tpu as pltpu
from jax.sharding import PartitionSpec as P

ITERS = 2
KSTART = 8

tiny_eps = 1e-06
f32 = jnp.float32
bf16 = jnp.bfloat16

SLOTS = 3
LEVELS = 32700.0


def momentum_list():
    ratio_now = 1.0
    ratios = [ratio_now]
    for iteration in range(KSTART + ITERS + 3):
        ratio_now = (1.0 + math.sqrt(1.0 + 4.0 * ratio_now * ratio_now)) / 2.0
        ratios.append(ratio_now)
    return [
        (ratios[KSTART - 1 + iteration] - 1.0) / ratios[KSTART + iteration]
        for iteration in range(ITERS + 1)
    ]


def signs(length):
    index = np.arange(length)
    both = index[:, None] & index[None]
    parity = np.zeros_like(both)
    while both.any():
        parity ^= both & 1
        both >>= 1
    return np.where(parity == 1, -1.0, 1.0)


def dot(a, b):
    return jnp.dot(a, b, preferred_element_type=f32)


def split_dot(matrix, values):
    upper = values.astype(bf16)
    lower = (values - upper.astype(f32)).astype(bf16)
    return dot(matrix, upper) + dot(matrix, lower)


def call(body, outs, args, prefetch=(), scratch=(), flops=0, limit=28, far=(), far_outs=False, anchors=()):
    vmem = pl.BlockSpec(memory_space=pltpu.VMEM)
    hbm = pl.BlockSpec(memory_space=pltpu.HBM)
    ahead = [pl.BlockSpec(memory_space=pl.ANY)] * len(anchors)
    size = sum(math.prod(a.shape) * a.dtype.itemsize for a in (*args, *outs, *far))
    return pl.pallas_call(
        body,
        out_shape=tuple(outs),
        in_specs=[pl.BlockSpec(memory_space=pltpu.SMEM)] * len(prefetch) + ahead + [vmem] * len(args) + [hbm] * len(far),
        out_specs=tuple([hbm if far_outs else vmem] * len(outs)),
        scratch_shapes=list(scratch),
        compiler_params=pltpu.CompilerParams(vmem_limit_bytes=limit * 2**20),
        cost_estimate=pl.CostEstimate(flops=flops, bytes_accessed=size, transcendentals=0),
    )(*prefetch, *anchors, *args, *far)


def shape(dims, dtype):
    return jax.ShapeDtypeStruct(tuple(dims), dtype)


def encode(ref, values):
    rows, depth, tile = values.shape
    flat = jnp.concatenate([values[r] for r in range(rows)], axis=0)
    bound = jnp.max(jnp.max(jnp.abs(flat), axis=0, keepdims=True), axis=1, keepdims=True)
    exponent = jnp.floor(jnp.log2(jnp.maximum(bound, 1e-30))) + 1.0
    coded = jnp.clip(jnp.round(flat * (LEVELS * jnp.exp2(-exponent))), -32767.0, 32767.0)
    ref[pl.ds(0, rows * depth)] = coded.astype(jnp.int32).astype(jnp.int16)
    ref[pl.ds(rows * depth, 16)] = jnp.broadcast_to(exponent, (16, tile)).astype(jnp.int32).astype(jnp.int16)


def decode(ref, size):
    coded = ref[pl.ds(0, size + 16)].astype(jnp.int32).astype(f32)
    return coded[:size] * (jnp.exp2(coded[size : size + 1, 0:1]) * (1.0 / LEVELS))


def decode_wide(refs, rows, depth):
    pieces = [decode(ref, rows * depth) for ref in refs]
    return jnp.concatenate(
        [jnp.concatenate([p[r * depth : (r + 1) * depth] for r in range(rows)], axis=1) for p in pieces],
        axis=0,
    )


def lateral_kernel(rows, frames, mask_ref, *refs):
    outs, held, sems = refs[5:8], refs[8:13], refs[13]
    copies = [pltpu.make_async_copy(a, b, sems.at[i]) for i, (a, b) in enumerate(zip(refs[:5], held))]
    for copy in copies:
        copy.start()
    id_ref, lo_ref, live_ref, measured_ref, masks_ref = held
    odd = lax.axis_index("lat") % 2 == 1
    own_ref = outs[0]
    depth = id_ref.shape[3]
    for ref in outs:
        ref[rows + 1] = jnp.full(ref.shape[1:], -1.0, f32)
    for copy in copies:
        copy.wait()
    for f in range(frames):
        first = lo_ref[f]
        end = first + live_ref[f]
        ids = [jnp.where((o - 1 >= first) & (o - 1 < end), id_ref[f, o], -1).astype(f32) for o in range(3)]
        for ref, row in zip(outs, (ids[1], jnp.where(odd, ids[0], ids[2]), jnp.where(odd, ids[2], ids[0]))):
            ref[rows + 1, pl.ds(f, 1), pl.ds(0, depth)] = row
        own_ref[rows, pl.ds(f, 1)] = masks_ref[pl.ds(mask_ref[f], 1)]
        for r in range(rows):
            own_ref[r, pl.ds(f, 1)] = measured_ref[f, pl.ds(r, 1)]
    for ref in outs[1:]:
        ref[pl.ds(0, rows + 1)] = own_ref[pl.ds(0, rows + 1)]


def prepare_kernel(count, rows, momentum, est_ref, prev_ref, *refs):
    me = lax.axis_index("dep")
    for slot in range(count):
        group = pl.ds((me ^ slot) * rows, rows)
        est = est_ref[group]
        encode(refs[slot], est + momentum * (est - prev_ref[group]))
        encode(refs[count + slot], est)


def fill_kernel(count, rows, frames, own_ref, a_ref, b_ref, *refs):
    ids_ref = refs[2 * count]
    place, last = lax.axis_index("lat"), lax.axis_size("lat") - 1
    ids_ref[...] = jnp.full(ids_ref.shape, -1.0, f32)
    ids_ref[pl.ds(0, frames)] = own_ref[rows + 1]
    ids_ref[pl.ds(frames, frames)] = a_ref[rows + 1]
    ids_ref[pl.ds(2 * frames, frames)] = jnp.where((place == 0) | (place == last), -1.0, b_ref[rows + 1])
    ids = ids_ref[...].astype(jnp.int32).astype(jnp.int16)
    for coded, out in zip(refs[:count], refs[count : 2 * count]):
        size = coded.shape[0]
        out[pl.ds(0, size)] = coded[...]
        out[pl.ds(size, ids.shape[0])] = ids


def table_kernel(anchor_ref, table_ref, out_ref):
    out_ref[...] = table_ref[...]


def state_kernel(rows, tile, fresh_ref, *refs):
    put_slots(fresh_ref[...], refs, rows, tile)


def choose_t_kernel(block, prints, spread_ref, number_ref, ids_ref, choose_ref):
    tall = ids_ref[...].T.astype(bf16)
    step = 5 * 128
    width = prints * block
    for start in range(0, width, step):
        stop = min(start + step, width)
        lanes = dot(tall, spread_ref[:, start:stop])
        choose_ref[:, start:stop] = jnp.where(lanes == number_ref[0:1, start:stop], 1.0, 0.0).astype(bf16)


def project(rows, block, frames, prints, lifted, choose_ref, table_ref, acc_ref, outs):
    per = 8 if prints % 8 == 0 else 2
    tile = table_ref.shape[1]
    total = jnp.zeros((rows * block, tile), f32)
    for start in range(0, prints, per):
        summed = dot(choose_ref[pl.ds(start * block, per * block)], lifted)
        for pair in range(per // 2):
            base = 2 * pair * block
            left = jnp.concatenate(
                [
                    jnp.concatenate(
                        [
                            summed[base + k * block : base + (k + 1) * block, r * tile : (r + 1) * tile]
                            for k in (0, 1)
                        ],
                        axis=1,
                    )
                    for r in range(rows)
                ],
                axis=0,
            )
            upper = left.astype(bf16)
            lower = (left - upper.astype(f32)).astype(bf16)
            weights = table_ref[pl.ds(start + 2 * pair, 2)].reshape(2 * tile, tile)
            total = total + dot(upper, weights) + dot(lower, weights)
    acc_ref[...] = total
    to_a_ref, to_b_ref, part_a_ref, part_b_ref = outs
    for r in range(rows):
        own, part_a, part_b = (acc_ref[pl.ds(r * block + slot * frames, frames)] for slot in range(SLOTS))
        to_a_ref[r] = own
        to_a_ref[rows + r] = part_a
        part_a_ref[r] = part_a
        to_b_ref[r] = own
        to_b_ref[rows + r] = part_b
        part_b_ref[r] = part_b


def project_kernel(count, rows, block, frames, prints, depth, *refs):
    currents, table_ref, outs = refs[:count], refs[count], refs[count + 1 : count + 5]
    choose_ref, ids_ref, acc_ref = refs[count + 5 :]
    top = rows * depth + 16
    rest = currents[0].shape[0] - top
    wide = jnp.concatenate(
        [c[pl.ds(top, rest)].astype(jnp.int32).astype(f32)[:block, :depth] for c in currents], axis=1
    )
    ids_ref[...] = wide
    for pair in range(prints // 2):
        both = jnp.concatenate(
            [jnp.where(wide == float(2 * pair + k), 1.0, 0.0).astype(f32) for k in (0, 1)], axis=0
        )
        choose_ref[pl.ds(pair * 2 * block, 2 * block)] = both.astype(bf16)
    lifted = decode_wide(currents, rows, depth).astype(bf16)
    project(rows, block, frames, prints, lifted, choose_ref, table_ref, acc_ref, outs)


def back_kernel(
    skip, rows, block, frames, prints, *refs
):
    own_ref, a_ref, b_ref, to_a_ref, part_b_ref, from_a_ref, from_b_ref, past_a_ref, past_b_ref = refs[skip : skip + 9]
    choose_ref, table_ref, grad_ref, sums_ref, left_ref, upper_ref, lower_ref = refs[skip + 9 :]
    tile = table_ref.shape[1]
    left_ref[...] = jnp.zeros_like(left_ref)
    misfit = jnp.zeros((1, tile), f32)
    for r in range(rows):
        projected = (
            to_a_ref[r] + (from_a_ref[rows + r] + from_b_ref[rows + r]),
            from_a_ref[r] + (to_a_ref[rows + r] + past_a_ref[r]),
            from_b_ref[r] + (part_b_ref[r] + past_b_ref[r]),
        )
        for slot, ref in enumerate((own_ref, a_ref, b_ref)):
            mask = ref[rows]
            residual = mask * projected[slot] - ref[r]
            if slot == 0:
                misfit = misfit + jnp.sum(residual * residual, axis=0, keepdims=True)
            weighted = (mask * residual).astype(bf16).astype(f32)
            left_ref[pl.ds(r * block + slot * frames, frames)] = weighted
    left = left_ref[...].astype(bf16)
    per = 8 if prints % 8 == 0 else 2
    for start in range(0, prints, per):
        weights = table_ref[pl.ds(start, per)].reshape(per * tile, tile)
        spread = lax.dot_general(left, weights, (((1,), (1,)), ((), ())), preferred_element_type=f32)
        for pair in range(per // 2):
            both = jnp.concatenate(
                [
                    jnp.concatenate(
                        [
                            spread[r * block : (r + 1) * block, k * tile : (k + 1) * tile]
                            for r in range(rows)
                        ],
                        axis=1,
                    )
                    for k in (2 * pair, 2 * pair + 1)
                ],
                axis=0,
            )
            upper = both.astype(bf16)
            where = pl.ds((start + 2 * pair) * block, 2 * block)
            upper_ref[where] = upper
            lower_ref[where] = (both - upper.astype(f32)).astype(bf16)
    choose = choose_ref[...]
    gradient = dot(choose, upper_ref[...]) + dot(choose, lower_ref[...])
    grad_ref[...] = gradient
    grad_sum = jnp.sum(jnp.sum(gradient * gradient, axis=0, keepdims=True), axis=1, keepdims=True)
    misfit_sum = jnp.sum(misfit, axis=1, keepdims=True)
    lane = lax.broadcasted_iota(jnp.int32, sums_ref.shape, 1)
    sums_ref[...] = jnp.where(lane < sums_ref.shape[1] // 2, misfit_sum, grad_sum)


def shrink(scale, sums_ref, current, grad, had_ref, limits_ref):
    total = jnp.sum(sums_ref[...], axis=0, keepdims=True)
    half = total.shape[1] // 2
    step = 0.5 * total[:, 0:1] / (total[:, half : half + 1] + tiny_eps)
    moved = current - step * grad
    coefficients = split_dot(had_ref[...], moved) * scale
    limit = step * limits_ref[...]
    limit = jnp.concatenate([limit] * (moved.shape[1] // limit.shape[1]), axis=1)
    clipped = jnp.clip(coefficients, -limit, limit)
    return moved - split_dot(had_ref[...], clipped) * scale


def first_kernel(count, rows, block, frames, prints, depth, scale, momentum, *refs):
    currents, refs = refs[:count], refs[count:]
    states, refs = refs[:count], refs[count:]
    sums_ref, grad_ref, had_ref, limits_ref, choose_ref, table_ref = refs[:6]
    outs, refs = refs[6:10], refs[10:]
    current_ref, fresh_ref, acc_ref = refs

    current, state = decode_wide(currents, rows, depth), decode_wide(states, rows, depth)
    fresh = shrink(scale, sums_ref, current, grad_ref[...], had_ref, limits_ref)
    fresh_ref[...] = fresh
    current = fresh + momentum * (fresh - state)
    current_ref[...] = current
    project(rows, block, frames, prints, current.astype(bf16), choose_ref, table_ref, acc_ref, outs)


def put_slots(fresh, refs, rows, tile):
    depth = fresh.shape[0] // len(refs)
    for slot in [*range(1, len(refs)), 0]:
        piece = fresh[slot * depth : (slot + 1) * depth]
        encode(refs[slot], jnp.stack([piece[:, r * tile : (r + 1) * tile] for r in range(rows)]))


def last_kernel(count, rows, scale, sums_ref, current_ref, grad_ref, had_ref, limits_ref, *fresh_refs):
    tile = limits_ref.shape[1]
    fresh = shrink(scale, sums_ref, current_ref[...], grad_ref[...], had_ref, limits_ref)
    put_slots(fresh, fresh_refs, rows, tile)


def finish_kernel(count, rows, momentum, *refs):
    states, fresh = refs[:count], refs[count : 2 * count]
    refined_hbm, ahead_hbm, refined_ref, ahead_ref, sems = refs[2 * count :]
    me = lax.axis_index("dep")
    copies = []
    for slot in range(count):
        group = pl.ds((me ^ slot) * rows, rows)
        size = math.prod(refined_ref.shape[1:3])
        now, before = decode(fresh[slot], size), decode(states[slot], size)
        refined_ref[slot] = now.reshape(refined_ref.shape[1:])
        ahead_ref[slot] = (now + momentum * (now - before)).reshape(ahead_ref.shape[1:])
        copies.append(pltpu.make_async_copy(refined_ref.at[slot], refined_hbm.at[group], sems.at[0, slot]))
        copies.append(pltpu.make_async_copy(ahead_ref.at[slot], ahead_hbm.at[group], sems.at[1, slot]))
        copies[-2].start()
        copies[-1].start()
    for copy in copies:
        copy.wait()


def depth_exchange(parts):
    count = len(parts)
    return [parts[0]] + [
        lax.ppermute(parts[s], "dep", [(i, i ^ s) for i in range(count)]) for s in range(1, count)
    ]


def partner_exchange(to_a, to_b):
    count = lax.axis_size("lat")
    pairs_a = [(i, i ^ 1) for i in range(count)]
    pairs_b = [(i, (i + 1 if i % 2 else i - 1) % count) for i in range(count)]
    return lax.ppermute(to_a, "lat", pairs_a), lax.ppermute(to_b, "lat", pairs_b)


def past_exchange(part_a, part_b):
    count = lax.axis_size("lat")
    past_a = [(i, (i + 2 if i % 2 else i - 2) % count) for i in range(count)]
    past_b = [(i, (i - 2 if i % 2 else i + 2) % count) for i in range(count)]
    return lax.ppermute(part_b, "lat", past_a), lax.ppermute(part_a, "lat", past_b)


def local(
    estimate,
    previous,
    measured,
    foot_table,
    foot_id,
    foot_lo,
    foot_count,
    mask_table,
    mask_id,
    thresholds,
):
    row_total, depth_local, tile = estimate.shape
    count = lax.axis_size("dep")
    lat_count = lax.axis_size("lat")
    rows = row_total // count
    depth = depth_local * count
    frames = measured.shape[1]
    prints = foot_table.shape[0]
    block = -(-SLOTS * frames // 8) * 8
    width = rows * tile
    momenta = momentum_list()
    scale = float(0.7071067811865476 ** (depth.bit_length() - 1))
    had = jnp.asarray(signs(depth), bf16)
    limits = jnp.broadcast_to(thresholds[:, None], (depth, tile))
    volume = (rows, depth_local, tile)
    coded = shape((rows * depth_local + 16, tile), jnp.int16)

    small = [
        jnp.transpose(foot_id, (1, 3, 0, 2)),
        jnp.transpose(foot_lo, (1, 0, 2)),
        jnp.transpose(foot_count, (1, 0, 2)),
        jnp.transpose(measured, (1, 0, 2)),
        mask_table,
    ]
    pack = shape((rows + 2, frames, tile), f32)
    own, to_a, to_b = call(
        functools.partial(lateral_kernel, rows, frames),
        [pack] * 3,
        [],
        far=small,
        scratch=[*(pltpu.VMEM(a.shape, a.dtype) for a in small), pltpu.SemaphoreType.DMA((len(small),))],
        prefetch=[mask_id[:, 0]],
        limit=56,
    )
    packs = [own, *partner_exchange(to_a, to_b)]

    more = -(-block // 16) * 16
    prepared = call(
        functools.partial(prepare_kernel, count, rows, momenta[0]), [coded] * (2 * count), [estimate, previous]
    )
    currents = call(
        functools.partial(fill_kernel, count, rows, frames),
        [shape((rows * depth_local + 16 + more, tile), jnp.int16)] * count,
        [*packs, *prepared[:count]],
        scratch=[pltpu.VMEM((more, tile), f32)],
    )
    (table,) = call(
        table_kernel,
        [shape(foot_table.shape, foot_table.dtype)],
        [foot_table],
        anchors=currents[:1],
    )
    currents = depth_exchange(currents)
    states = depth_exchange(prepared[count:])
    lanes = np.arange(prints * block)
    spread = jnp.asarray(lanes[None] % block == np.arange(block)[:, None], bf16)
    number = jnp.asarray(np.broadcast_to(lanes // block, (8, prints * block)), f32)
    sizes = (rows, block, frames, prints)
    acc = pltpu.VMEM((rows * block, tile), f32)
    part, double = shape((rows, frames, tile), f32), shape((2 * rows, frames, tile), f32)
    work = 2 * prints * block * width * (depth + tile)
    *parts, choose, ids = call(
        functools.partial(project_kernel, count, *sizes, depth_local),
        [double, double, part, part, shape((prints * block, depth), bf16), shape((block, depth), f32)],
        [*currents, table],
        scratch=[acc],
        flops=work,
    )
    (choose_t,) = call(
        functools.partial(choose_t_kernel, block, prints),
        [shape((depth, prints * block), bf16)],
        [spread, number, ids],
    )

    def step_sums(parts, hidden):
        to_a, to_b, part_a, part_b = parts
        gradient, sums = call(
            functools.partial(back_kernel, len(hidden), *sizes),
            [shape((depth, width), f32), shape((count * lat_count, tile), f32)],
            [
                *packs,
                to_a,
                part_b,
                *partner_exchange(to_a, to_b),
                *past_exchange(part_a, part_b),
                choose_t,
                table,
            ],
            scratch=[
                pltpu.VMEM((rows * block, tile), f32),
                pltpu.VMEM((prints * block, width), bf16),
                pltpu.VMEM((prints * block, width), bf16),
            ],
            flops=2 * work,
            anchors=hidden,
        )
        return gradient, lax.all_to_all(sums, ("lat", "dep"), split_axis=0, concat_axis=0, tiled=True)

    gradient, sums = step_sums(parts, states[1:])
    done = call(
        functools.partial(first_kernel, count, *sizes, depth_local, scale, momenta[1]),
        [double, double, part, part] + [shape((depth, width), f32)] * 2,
        [*currents, *states, sums, gradient, had, limits, choose, table],
        scratch=[acc],
        flops=work,
    )
    parts, current = done[:4], done[4]
    states = depth_exchange(
        call(functools.partial(state_kernel, rows, tile), [coded] * count, [done[5]])
    )
    gradient, sums = step_sums(parts, [])
    fresh = depth_exchange(
        call(
            functools.partial(last_kernel, count, rows, scale),
            [coded] * count,
            [sums, current, gradient, had, limits],
        )
    )
    return call(
        functools.partial(finish_kernel, count, rows, momenta[2]),
        [shape(estimate.shape, f32)] * 2,
        [*states, *fresh],
        far_outs=True,
        scratch=[
            pltpu.VMEM((count, *volume), f32),
            pltpu.VMEM((count, *volume), f32),
            pltpu.SemaphoreType.DMA((2, count)),
        ],
    )


def solution(mesh):
    in_specs = (
        P(None, "dep", "lat"),
        P(None, "dep", "lat"),
        P("dep", None, "lat"),
        P(),
        P("lat", None, "dep", None),
        P("lat", None, "dep"),
        P("lat", None, "dep"),
        P(),
        P(None, "lat"),
        P(),
    )
    out_specs = (P(None, "dep", "lat"), P(None, "dep", "lat"))
    return jax.shard_map(local, mesh=mesh, in_specs=in_specs, out_specs=out_specs, check_vma=False)
```

time: 104 us -> 82.9 us (0.80)
  waiting for transfers between devices: 29.1 us -> 11.9 us
  blocking collectives: 17 us -> 14.8 us
  other arithmetic: 1.75 us -> 0 us
  local copies, waits for them, and re-layouts: 3 us -> 4.59 us
  starting transfers between devices: 34 us -> 32.9 us
    ppermute x15 -> x12, waiting for transfers between devices: 16.3 us -> 5.27 us  [depth_exchange(): lax.ppermute(parts[s], 'dep', [(i, i ^ s) for i in range(count)])]
    ppermute x5 -> x3, waiting for transfers between devices: 9.15 us -> 0.01 us  [partner_exchange(): lax.ppermute(to_b, 'lat', pairs_b)]
    ppermute x0 -> x4, starting transfers between devices: none -> 6.46 us  [the longest x2 3.63 us: past_exchange(): lax.ppermute(part_a, 'lat', past_b)]
    ppermute x15 -> x12, starting transfers between devices: 24.1 us -> 18.1 us  [depth_exchange(): lax.ppermute(parts[s], 'dep', [(i, i ^ s) for i in range(count)])]
    ppermute x0 -> x4, waiting for transfers between devices: none -> 3.65 us  [the longest x2 1.84 us: past_exchange(): lax.ppermute(part_b, 'lat', past_a)]
    all_to_all x1, blocking collectives: 17 us -> 14.8 us  [step_sums(): lax.all_to_all(sums, ('lat', 'dep'), split_axis=0, concat_axis=0, tiled=T...]
    ppermute x5 -> x3, starting transfers between devices: 6.64 us -> 4.45 us  [partner_exchange(): lax.ppermute(to_b, 'lat', pairs_b)]
    unnamed x26 -> x18, local copies, waits for them, and re-layouts: 2.84 us -> 4.5 us
  transfers between devices with their start and end apart: 26 -> 23, of which waited for: 11 -> 8; matrix products, arithmetic and copies ran while one was open for 0% -> 0% of each run, Pallas kernels for 7% -> 10%
where the time goes in v2:
time: 82.9 us; the launch traced here: 82.5 us
  starting transfers between devices  32.9 us (40%)
  Pallas kernels  17.2 us (21%)
  blocking collectives  14.8 us (18%)
  waiting for transfers between devices  11.9 us (14%)
  local copies, waits for them, and re-layouts  4.59 us (6%)
  between operations  0.97 us (1%)
    ppermute x12, starting transfers between devices, depth_exchange(): lax.ppermute(parts[s], 'dep', [(i, i ^ s) for i in range(count)])  18.1 us
    pallas_call x12, Pallas kernels, call(): pl.pallas_call(body, out_shape=tuple(outs), in_specs=[pl.BlockSpec(memory...  17.2 us
    all_to_all x1, blocking collectives, step_sums(): lax.all_to_all(sums, ('lat', 'dep'), split_axis=0, concat_axis=0, tiled=T...  14.8 us
    ppermute x12, waiting for transfers between devices, depth_exchange(): lax.ppermute(parts[s], 'dep', [(i, i ^ s) for i in range(count)])  5.27 us
    unnamed x18, local copies, waits for them, and re-layouts  4.5 us
    ppermute x3, starting transfers between devices, partner_exchange(): lax.ppermute(to_b, 'lat', pairs_b)  4.45 us
    ppermute x2, starting transfers between devices, past_exchange(): lax.ppermute(part_a, 'lat', past_b)  3.63 us
    all_to_all x1, waiting for transfers between devices, step_sums(): lax.all_to_all(sums, ('lat', 'dep'), split_axis=0, concat_axis=0, tiled=T...  2.99 us
  transfers between devices with their start and end apart: 23, of which 8 were waited for; matrix products, arithmetic and copies ran while one was open for 0% of the time, Pallas kernels for 10%

profile of v2, /device:TPU:0, one launch (start us, length us, event | category | flops | bytes accessed | tf_op | source)
XLA Modules:
  0.0 82.5 jit_solution(1321136247383953347)
XLA Ops:
  0.6 2.2 %shard_map.140 = (f32[6,12,128]{2,1,0:T(8,128)}, f32[6,12,128]{2,1,0:T(8,128)}, f32[6,12,128]{2,1,0:T(8,128)}) custom-call(s32[12]{0:T(128)} %bitcast.20, s32[12,3,1,64]{3,2,1,0:T(1,128)} %bitcast.17, s32[12,1,64]{2,1,0:T(1,128)} %bitcast.18, s32[12,1,64]{2,1,0:T(1,128)} %bitcast.19, f32[12,4,128]{2,1,0:T(4,128)} %bitcast.16, f32[16,128]{1,0:T(8,128)} %refs_4_.1), custom_call_target="tpu_custom_call" | custom-call | bytes 158720 | tf_op jit(solution)/shard_map/pallas_call | solution.py:60
  2.8 0.5 collective-permute-start
  3.4 3.6 %collective-permute-start.1 = (f32[6,12,128]{2,1,0:T(8,128)}, f32[6,12,128]{2,1,0:T(8,128)S(1)}, u32[]{:S(2)}, u32[]{:S(2)}) collective-permute-start(f32[6,12,128]{2,1,0:T(8,128)} %get-tuple-element.43), channel_id=1, source_target_pairs={{0,28},{4,8},{8,4},{12,16},{16,12},{20,24},{24,20},{28,0},{1,29},{... | collective-permute-start | bytes 110600 | tf_op jit(solution)/shard_map/ppermute | solution.py:343
  6.9 1.0 %copy-done.1 = f32[16,64,128]{2,1,0:T(8,128)S(1)} copy-done((f32[16,64,128]{2,1,0:T(8,128)S(1)}, f32[16,64,128]{2,1,0:T(8,128)}, u32[]{:S(2)}) %copy-start.1) | copy-done | bytes 524312
  8.0 1.0 %copy-done.2 = f32[16,64,128]{2,1,0:T(8,128)S(1)} copy-done((f32[16,64,128]{2,1,0:T(8,128)S(1)}, f32[16,64,128]{2,1,0:T(8,128)}, u32[]{:S(2)}) %copy-start.2) | copy-done | bytes 524312
  9.0 0.3 shard_map.141
  9.3 0.0 collective-permute-done.a_ref.refs_4_.refs_1_
  9.4 0.0 collective-permute-done.1.b_ref.refs_5_.refs_2_
  9.4 0.0 copy-start.6
  9.4 0.8 copy-done.6
  10.2 1.6 %collective-permute-start.2 = (s16[320,128]{1,0:T(8,128)(2,1)S(1)}, s16[320,128]{1,0:T(8,128)(2,1)S(1)}, u32[]{:S(2)}, u32[]{:S(2)}) collective-permute-start(s16[320,128]{1,0:T(8,128)(2,1)S(1)} %get-tuple-element.49), channel_id=1, source_target_pairs={{0,1},{1,0},{2,3},{3,2},{4,5},{5,4},{6,7},{7,6},{8,9},{9,8},{10,11... | collective-permute-start | bytes 245768 | tf_op jit(solution)/shard_map/ppermute | solution.py:335
  11.8 2.6 %collective-permute-start.3 = (s16[320,128]{1,0:T(8,128)(2,1)S(1)}, s16[320,128]{1,0:T(8,128)(2,1)S(1)}, u32[]{:S(2)}, u32[]{:S(2)}) collective-permute-start(s16[320,128]{1,0:T(8,128)(2,1)S(1)} %get-tuple-element.50), channel_id=1, source_target_pairs={{0,2},{1,3},{2,0},{3,1},{4,6},{5,7},{6,4},{7,5},{8,10},{9,11},{10,... | collective-permute-start | bytes 245768 | tf_op jit(solution)/shard_map/ppermute | solution.py:335
  14.4 0.2 collective-permute-start.4
  14.7 0.7 collective-permute-start.5
  15.3 3.5 %collective-permute-start.6 = (s16[272,128]{1,0:T(8,128)(2,1)S(1)}, s16[272,128]{1,0:T(8,128)(2,1)S(1)}, u32[]{:S(2)}, u32[]{:S(2)}) collective-permute-start(s16[272,128]{1,0:T(8,128)(2,1)S(1)} %get-tuple-element.54), channel_id=1, source_target_pairs={{0,2},{1,3},{2,0},{3,1},{4,6},{5,7},{6,4},{7,5},{8,10},{9,11},{10,... | collective-permute-start | bytes 208904 | tf_op jit(solution)/shard_map/ppermute | solution.py:335
  18.8 1.6 %copy-done = bf16[64,128,128]{2,1,0:T(8,128)(2,1)S(1)} copy-done((bf16[64,128,128]{2,1,0:T(8,128)(2,1)S(1)}, bf16[64,128,128]{2,1,0:T(8,128)(2,1)}, u32[]{:S(2)}) %copy-start) | copy-done | bytes 2097176
  20.4 0.1 shard_map.143.refs_4_.refs_13_.refs_10_
  20.6 0.0 copy-start.4
  20.6 0.0 copy-start.5
  20.6 0.0 collective-permute-done.2.refs_1_
  20.6 0.0 copy-start.7
  20.6 0.3 collective-permute-start.7
  20.9 0.9 %collective-permute-done.3.refs_2_ = s16[320,128]{1,0:T(8,128)(2,1)S(1)} collective-permute-done((s16[320,128]{1,0:T(8,128)(2,1)S(1)}, s16[320,128]{1,0:T(8,128)(2,1)S(1)}, u32[]{:S(2)}, u32[]{:S(2)}) %collective-permute-start.3) | collective-permute-done | bytes 81952 | tf_op jit(solution)/shard_map/ppermute | solution.py:335
  21.7 0.0 collective-permute-done.4.refs_3_
  21.7 2.8 %shard_map.144 = (f32[8,12,128]{2,1,0:T(8,128)S(1)}, f32[8,12,128]{2,1,0:T(8,128)S(1)}, f32[4,12,128]{2,1,0:T(8,128)S(1)}, f32[4,12,128]{2,1,0:T(8,128)S(1)}, bf...) custom-call(s16[320,128]{1,0:T(8,128)(2,1)S(1)} %get-tuple-element.48.anchor_ref.refs_0_, ...), custom_call_target="tpu_custom_call" | custom-call | flops 1006632960 | bytes 3923968 | tf_op jit(solution)/shard_map/pallas_call | solution.py:60
  24.6 0.8 collective-permute-start.9
  25.4 0.0 collective-permute-start.8
  25.4 0.0 collective-permute-done.5.refs_0_.refs_5_
  25.4 2.2 %collective-permute-start.11 = (f32[4,12,128]{2,1,0:T(8,128)S(1)}, f32[4,12,128]{2,1,0:T(8,128)S(1)}, u32[]{:S(2)}, u32[]{:S(2)}) collective-permute-start(f32[4,12,128]{2,1,0:T(8,128)S(1)} %get-tuple-element.59), channel_id=1, source_target_pairs={{0,8},{4,28},{8,16},{12,4},{16,24},{20,12},{24,0},{28,20},{1,9},{5... | collective-permute-start | bytes 73736 | tf_op jit(solution)/shard_map/ppermute | solution.py:350
  27.6 0.0 collective-permute-done.6.refs_1_.refs_6_
  27.6 1.4 %collective-permute-start.10 = (f32[4,12,128]{2,1,0:T(8,128)S(1)}, f32[4,12,128]{2,1,0:T(8,128)S(1)}, u32[]{:S(2)}, u32[]{:S(2)}) collective-permute-start(f32[4,12,128]{2,1,0:T(8,128)S(1)} %get-tuple-element.57.refs_7_), channel_id=1, source_target_pairs={{0,24},{4,12},{8,0},{12,20},{16,8},{20,28},{24,16},{28,4},{1,25},{... | collective-permute-start | bytes 73736 | tf_op jit(solution)/shard_map/ppermute | solution.py:350
  29.0 0.5 shard_map.145.refs_12_.refs_9_
  29.5 0.0 copy-start.8
  29.5 0.0 copy-start.3
  29.6 0.7 collective-permute-done.11.refs_11_
  30.2 1.3 %collective-permute-done.10.refs_10_ = f32[4,12,128]{2,1,0:T(8,128)S(1)} collective-permute-done((f32[4,12,128]{2,1,0:T(8,128)S(1)}, f32[4,12,128]{2,1,0:T(8,128)S(1)}, u32[]{:S(2)}, u32[]{:S(2)}) %collective-permute-start.10) | collective-permute-done | bytes 24608 | tf_op jit(solution)/shard_map/ppermute | solution.py:350
  31.5 0.0 collective-permute-done.8.refs_8_
  31.5 2.3 %shard_map.146 = (f32[256,512]{1,0:T(8,128)S(1)}, f32[32,128]{1,0:T(8,128)S(1)}) custom-call(s16[272,128]{1,0:T(8,128)(2,1)S(1)} %collective-permute-done.5.refs_0_.refs_5_, s16[272,128]{1,0:T(8,128)(2,1)S(1)} %collective-permute-done.6.refs_1_.refs_6_, s16[272,128]{1,0:T(8,128)(2,1)S(1)} %collective-permute-done.7.refs_2_.refs_7_, ...), custom_call_target="tpu_custom_call" | custom-call | flops 2013265920 | bytes 4280320 | tf_op jit(solution)/shard_map/pallas_call | solution.py:60
  33.8 14.8 %all_to_all.22 = f32[32,1,128]{2,1,0:T(1,128)S(1)} all-to-all(f32[32,1,128]{2,1,0:T(1,128)S(1)} %bitcast.15), channel_id=1, replica_groups=mesh['lat'=8,'dep'=4] {'lat','dep'}, dimensions={0} | all-to-all | bytes 32768 | tf_op jit(solution)/shard_map/all_to_all | solution.py:460
  48.6 0.1 broadcast_in_dim.2.refs_11_.limits_ref
  48.7 3.6 %shard_map.147 = (f32[8,12,128]{2,1,0:T(8,128)S(1)}, f32[8,12,128]{2,1,0:T(8,128)S(1)}, f32[4,12,128]{2,1,0:T(8,128)S(1)}, f32[4,12,128]{2,1,0:T(8,128)S(1)}, f3...) custom-call(s16[320,128]{1,0:T(8,128)(2,1)S(1)} %get-tuple-element.48.anchor_ref.refs_0_, ...), custom_call_target="tpu_custom_call" | custom-call | flops 1006632960 | bytes 6012928 | tf_op jit(solution)/shard_map/pallas_call | solution.py:60
  52.3 0.1 collective-permute-start.16
  52.4 0.7 collective-permute-start.15
  53.1 1.5 %collective-permute-start.18 = (f32[4,12,128]{2,1,0:T(8,128)S(1)}, f32[4,12,128]{2,1,0:T(8,128)S(1)}, u32[]{:S(2)}, u32[]{:S(2)}) collective-permute-start(f32[4,12,128]{2,1,0:T(8,128)S(1)} %get-tuple-element.72), channel_id=1, source_target_pairs={{0,8},{4,28},{8,16},{12,4},{16,24},{20,12},{24,0},{28,20},{1,9},{5... | collective-permute-start | bytes 73736 | tf_op jit(solution)/shard_map/ppermute | solution.py:350
  54.6 1.4 %collective-permute-start.17 = (f32[4,12,128]{2,1,0:T(8,128)S(1)}, f32[4,12,128]{2,1,0:T(8,128)S(1)}, u32[]{:S(2)}, u32[]{:S(2)}) collective-permute-start(f32[4,12,128]{2,1,0:T(8,128)S(1)} %get-tuple-element.70.refs_4_), channel_id=1, source_target_pairs={{0,24},{4,12},{8,0},{12,20},{16,8},{20,28},{24,16},{28,4},{1,25},{... | collective-permute-start | bytes 73736 | tf_op jit(solution)/shard_map/ppermute | solution.py:350
  56.0 0.2 shard_map.148
  56.2 0.6 collective-permute-start.12
  56.8 1.1 %collective-permute-done.18.refs_8_ = f32[4,12,128]{2,1,0:T(8,128)S(1)} collective-permute-done((f32[4,12,128]{2,1,0:T(8,128)S(1)}, f32[4,12,128]{2,1,0:T(8,128)S(1)}, u32[]{:S(2)}, u32[]{:S(2)}) %collective-permute-start.18) | collective-permute-done | bytes 24608 | tf_op jit(solution)/shard_map/ppermute | solution.py:350
  57.9 0.6 collective-permute-done.17.refs_7_
  58.5 0.0 collective-permute-done.15.refs_5_
  58.5 2.9 %shard_map.149 = (f32[256,512]{1,0:T(8,128)S(1)}, f32[32,128]{1,0:T(8,128)}) custom-call(f32[6,12,128]{2,1,0:T(8,128)S(1)} %copy-done.7, f32[6,12,128]{2,1,0:T(8,128)S(1)} %collective-permute-done.a_ref.refs_4_.refs_1_, f32[6,12,128]{2,1,0:T(8,128)S(1)} %collective-permute-done.1.b_ref.refs_5_.refs_2_, f32[8,12,128]{2,1,0:T(8,128)S(1)} %get-tuple-element.69.refs_3_, ...), custom_call_target="tpu_custom_call" | custom-call | flops 2013265920 | bytes 4280320 | tf_op jit(solution)/shard_map/pallas_call | solution.py:60
  61.4 2.7 %all-to-all-start.1 = ((f32[32,1,128]{2,1,0:T(1,128)}), f32[32,1,128]{2,1,0:T(1,128)S(1)}, u32[]{:S(2)}, u32[]{:S(2)}) async-start(f32[32,1,128]{2,1,0:T(1,128)} %bitcast.9), calls=%async_computation.1 | async-start | bytes 32768 | tf_op jit(solution)/shard_map/all_to_all | solution.py:460
  64.1 2.7 %collective-permute-start.13 = (s16[272,128]{1,0:T(8,128)(2,1)S(1)}, s16[272,128]{1,0:T(8,128)(2,1)S(1)}, u32[]{:S(2)}, u32[]{:S(2)}) collective-permute-start(s16[272,128]{1,0:T(8,128)(2,1)S(1)} %get-tuple-element.67), channel_id=1, source_target_pairs={{0,2},{1,3},{2,0},{3,1},{4,6},{5,7},{6,4},{7,5},{8,10},{9,11},{10,... | collective-permute-start | bytes 208904 | tf_op jit(solution)/shard_map/ppermute | solution.py:335
  66.9 1.5 %collective-permute-start.14 = (s16[272,128]{1,0:T(8,128)(2,1)S(1)}, s16[272,128]{1,0:T(8,128)(2,1)S(1)}, u32[]{:S(2)}, u32[]{:S(2)}) collective-permute-start(s16[272,128]{1,0:T(8,128)(2,1)S(1)} %get-tuple-element.68), channel_id=1, source_target_pairs={{0,3},{1,2},{2,1},{3,0},{4,7},{5,6},{6,5},{7,4},{8,11},{9,10},{10,... | collective-permute-start | bytes 208904 | tf_op jit(solution)/shard_map/ppermute | solution.py:335
  68.3 3.0 %all-to-all-done.1 = f32[32,1,128]{2,1,0:T(1,128)S(1)} async-done(((f32[32,1,128]{2,1,0:T(1,128)}), f32[32,1,128]{2,1,0:T(1,128)S(1)}, u32[]{:S(2)}, u32[]{:S(2)}) %all-to-all-start.1) | async-done | bytes 16416 | tf_op jit(solution)/shard_map/all_to_all | solution.py:460
  71.3 1.0 %shard_map.150 = (s16[272,128]{1,0:T(8,128)(2,1)S(1)}, s16[272,128]{1,0:T(8,128)(2,1)S(1)}, s16[272,128]{1,0:T(8,128)(2,1)S(1)}, s16[272,128]{1,0:T(8,128)(2,1)S(1)}) custom-call(f32[32,128]{1,0:T(8,128)S(1)} %bitcast.14, f32[256,512]{1,0:T(8,128)S(1)} %get-tuple-element.74.current_ref, f32[256,512]{1,0:T(8,128)S(1)} %get-tuple-element.75.grad_ref, ...), custom_call_target="tpu_custom_call" | custom-call | bytes 1605632 | tf_op jit(solution)/shard_map/pallas_call | solution.py:60
  72.3 0.5 collective-permute-start.19
  72.7 0.6 collective-permute-start.20
  73.4 0.0 collective-permute-done.12.refs_1_
  73.4 3.4 %collective-permute-start.21 = (s16[272,128]{1,0:T(8,128)(2,1)S(1)}, s16[272,128]{1,0:T(8,128)(2,1)S(1)}, u32[]{:S(2)}, u32[]{:S(2)}) collective-permute-start(s16[272,128]{1,0:T(8,128)(2,1)S(1)} %get-tuple-element.79), channel_id=1, source_target_pairs={{0,3},{1,2},{2,1},{3,0},{4,7},{5,6},{6,5},{7,4},{8,11},{9,10},{10,... | collective-permute-start | bytes 208904 | tf_op jit(solution)/shard_map/ppermute | solution.py:335
  76.7 0.0 collective-permute-done.14.refs_3_
  76.7 0.7 collective-permute-done.19.refs_5_
  77.4 3.7 %collective-permute-done.20.refs_6_ = s16[272,128]{1,0:T(8,128)(2,1)S(1)} collective-permute-done((s16[272,128]{1,0:T(8,128)(2,1)S(1)}, s16[272,128]{1,0:T(8,128)(2,1)S(1)}, u32[]{:S(2)}, u32[]{:S(2)}) %collective-permute-start.20) | collective-permute-done | bytes 69664 | tf_op jit(solution)/shard_map/ppermute | solution.py:335
  81.1 1.2 %shard_map.151 = (f32[16,64,128]{2,1,0:T(8,128)}, f32[16,64,128]{2,1,0:T(8,128)}) custom-call(s16[272,128]{1,0:T(8,128)(2,1)S(1)} %get-tuple-element.65.refs_0_, s16[272,128]{1,0:T(8,128)(2,1)S(1)} %collective-permute-done.12.refs_1_, s16[272,128]{1,0:T(8,128)(2,1)S(1)} %collective-permute-done.13.refs_2_, ...), custom_call_target="tpu_custom_call" | custom-call | bytes 1605632 | tf_op jit(solution)/shard_map/pallas_call | solution.py:60
  (14 shorter events, 0.1 us)
Async XLA Ops:
  2.8 6.5 %collective-permute-start = (f32[6,12,128]{2,1,0:T(8,128)}, f32[6,12,128]{2,1,0:T(8,128)S(1)}, u32[]{:S(2)}, u32[]{:S(2)}) collective-permute-start(f32[6,12,128]{2,1,0:T(8,128)} %get-tuple-element.42), channel_id=1, source_target_pairs={{0,4},{4,0},{8,12},{12,8},{16,20},{20,16},{24,28},{28,24},{1,5},{5... | collective-permute-start | bytes 110600 | tf_op jit(solution)/shard_map/ppermute | solution.py:343
  3.4 6.0 %collective-permute-start.1 = (f32[6,12,128]{2,1,0:T(8,128)}, f32[6,12,128]{2,1,0:T(8,128)S(1)}, u32[]{:S(2)}, u32[]{:S(2)}) collective-permute-start(f32[6,12,128]{2,1,0:T(8,128)} %get-tuple-element.43), channel_id=1, source_target_pairs={{0,28},{4,8},{8,4},{12,16},{16,12},{20,24},{24,20},{28,0},{1,29},{... | collective-permute-start | bytes 110600 | tf_op jit(solution)/shard_map/ppermute | solution.py:343
  6.9 1.0 %copy-start.1 = (f32[16,64,128]{2,1,0:T(8,128)S(1)}, f32[16,64,128]{2,1,0:T(8,128)}, u32[]{:S(2)}) copy-start(f32[16,64,128]{2,1,0:T(8,128)} %est_ref.1) | copy-start | bytes 1572868
  8.0 1.0 %copy-start.2 = (f32[16,64,128]{2,1,0:T(8,128)S(1)}, f32[16,64,128]{2,1,0:T(8,128)}, u32[]{:S(2)}) copy-start(f32[16,64,128]{2,1,0:T(8,128)} %prev_ref.1) | copy-start | bytes 1572868
  9.4 0.8 copy-start.6
  10.2 10.4 %collective-permute-start.2 = (s16[320,128]{1,0:T(8,128)(2,1)S(1)}, s16[320,128]{1,0:T(8,128)(2,1)S(1)}, u32[]{:S(2)}, u32[]{:S(2)}) collective-permute-start(s16[320,128]{1,0:T(8,128)(2,1)S(1)} %get-tuple-element.49), channel_id=1, source_target_pairs={{0,1},{1,0},{2,3},{3,2},{4,5},{5,4},{6,7},{7,6},{8,9},{9,8},{10,11... | collective-permute-start | bytes 245768 | tf_op jit(solution)/shard_map/ppermute | solution.py:335
  11.8 9.9 %collective-permute-start.3 = (s16[320,128]{1,0:T(8,128)(2,1)S(1)}, s16[320,128]{1,0:T(8,128)(2,1)S(1)}, u32[]{:S(2)}, u32[]{:S(2)}) collective-permute-start(s16[320,128]{1,0:T(8,128)(2,1)S(1)} %get-tuple-element.50), channel_id=1, source_target_pairs={{0,2},{1,3},{2,0},{3,1},{4,6},{5,7},{6,4},{7,5},{8,10},{9,11},{10,... | collective-permute-start | bytes 245768 | tf_op jit(solution)/shard_map/ppermute | solution.py:335
  14.4 7.3 %collective-permute-start.4 = (s16[320,128]{1,0:T(8,128)(2,1)S(1)}, s16[320,128]{1,0:T(8,128)(2,1)S(1)}, u32[]{:S(2)}, u32[]{:S(2)}) collective-permute-start(s16[320,128]{1,0:T(8,128)(2,1)S(1)} %get-tuple-element.51), channel_id=1, source_target_pairs={{0,3},{1,2},{2,1},{3,0},{4,7},{5,6},{6,5},{7,4},{8,11},{9,10},{10,... | collective-permute-start | bytes 245768 | tf_op jit(solution)/shard_map/ppermute | solution.py:335
  14.7 10.8 %collective-permute-start.5 = (s16[272,128]{1,0:T(8,128)(2,1)S(1)}, s16[272,128]{1,0:T(8,128)(2,1)S(1)}, u32[]{:S(2)}, u32[]{:S(2)}) collective-permute-start(s16[272,128]{1,0:T(8,128)(2,1)S(1)} %get-tuple-element.53), channel_id=1, source_target_pairs={{0,1},{1,0},{2,3},{3,2},{4,5},{5,4},{6,7},{7,6},{8,9},{9,8},{10,11... | collective-permute-start | bytes 208904 | tf_op jit(solution)/shard_map/ppermute | solution.py:335
  15.3 12.2 %collective-permute-start.6 = (s16[272,128]{1,0:T(8,128)(2,1)S(1)}, s16[272,128]{1,0:T(8,128)(2,1)S(1)}, u32[]{:S(2)}, u32[]{:S(2)}) collective-permute-start(s16[272,128]{1,0:T(8,128)(2,1)S(1)} %get-tuple-element.54), channel_id=1, source_target_pairs={{0,2},{1,3},{2,0},{3,1},{4,6},{5,7},{6,4},{7,5},{8,10},{9,11},{10,... | collective-permute-start | bytes 208904 | tf_op jit(solution)/shard_map/ppermute | solution.py:335
  18.8 1.6 %copy-start = (bf16[64,128,128]{2,1,0:T(8,128)(2,1)S(1)}, bf16[64,128,128]{2,1,0:T(8,128)(2,1)}, u32[]{:S(2)}) copy-start(bf16[64,128,128]{2,1,0:T(8,128)(2,1)} %table_ref.1) | copy-start | bytes 6291460
  20.6 8.4 %copy-start.4 = (bf16[40,2560]{1,0:T(8,128)(2,1)S(1)}, bf16[40,2560]{1,0:T(8,128)(2,1)}, u32[]{:S(2)}) copy-start(bf16[40,2560]{1,0:T(8,128)(2,1)} %constant.7.clone.spread_ref) | copy-start | bytes 614404
  20.6 8.4 %copy-start.5 = (f32[8,2560]{1,0:T(8,128)S(1)}, f32[8,2560]{1,0:T(8,128)}, u32[]{:S(2)}) copy-start(f32[8,2560]{1,0:T(8,128)} %constant.8.clone.number_ref) | copy-start | bytes 245764
  20.6 10.9 %copy-start.7 = (f32[6,12,128]{2,1,0:T(8,128)S(1)}, f32[6,12,128]{2,1,0:T(8,128)}, u32[]{:S(2)}) copy-start(f32[6,12,128]{2,1,0:T(8,128)} %get-tuple-element.41.own_ref.refs_3_.refs_0_) | copy-start | bytes 110596
  20.6 8.9 %collective-permute-start.7 = (s16[272,128]{1,0:T(8,128)(2,1)S(1)}, s16[272,128]{1,0:T(8,128)(2,1)S(1)}, u32[]{:S(2)}, u32[]{:S(2)}) collective-permute-start(s16[272,128]{1,0:T(8,128)(2,1)S(1)} %get-tuple-element.55), channel_id=1, source_target_pairs={{0,3},{1,2},{2,1},{3,0},{4,7},{5,6},{6,5},{7,4},{8,11},{9,10},{10,... | collective-permute-start | bytes 208904 | tf_op jit(solution)/shard_map/ppermute | solution.py:335
  24.6 6.9 %collective-permute-start.9 = (f32[8,12,128]{2,1,0:T(8,128)S(1)}, f32[8,12,128]{2,1,0:T(8,128)S(1)}, u32[]{:S(2)}, u32[]{:S(2)}) collective-permute-start(f32[8,12,128]{2,1,0:T(8,128)S(1)} %get-tuple-element.58), channel_id=1, source_target_pairs={{0,28},{4,8},{8,4},{12,16},{16,12},{20,24},{24,20},{28,0},{1,29},{... | collective-permute-start | bytes 147464 | tf_op jit(solution)/shard_map/ppermute | solution.py:343
  25.4 6.1 %collective-permute-start.8 = (f32[8,12,128]{2,1,0:T(8,128)S(1)}, f32[8,12,128]{2,1,0:T(8,128)S(1)}, u32[]{:S(2)}, u32[]{:S(2)}) collective-permute-start(f32[8,12,128]{2,1,0:T(8,128)S(1)} %get-tuple-element.56.refs_6_), channel_id=1, source_target_pairs={{0,4},{4,0},{8,12},{12,8},{16,20},{20,16},{24,28},{28,24},{1,5},{5... | collective-permute-start | bytes 147464 | tf_op jit(solution)/shard_map/ppermute | solution.py:343
  25.4 4.8 %collective-permute-start.11 = (f32[4,12,128]{2,1,0:T(8,128)S(1)}, f32[4,12,128]{2,1,0:T(8,128)S(1)}, u32[]{:S(2)}, u32[]{:S(2)}) collective-permute-start(f32[4,12,128]{2,1,0:T(8,128)S(1)} %get-tuple-element.59), channel_id=1, source_target_pairs={{0,8},{4,28},{8,16},{12,4},{16,24},{20,12},{24,0},{28,20},{1,9},{5... | collective-permute-start | bytes 73736 | tf_op jit(solution)/shard_map/ppermute | solution.py:350
  27.6 3.9 %collective-permute-start.10 = (f32[4,12,128]{2,1,0:T(8,128)S(1)}, f32[4,12,128]{2,1,0:T(8,128)S(1)}, u32[]{:S(2)}, u32[]{:S(2)}) collective-permute-start(f32[4,12,128]{2,1,0:T(8,128)S(1)} %get-tuple-element.57.refs_7_), channel_id=1, source_target_pairs={{0,24},{4,12},{8,0},{12,20},{16,8},{20,28},{24,16},{28,4},{1,25},{... | collective-permute-start | bytes 73736 | tf_op jit(solution)/shard_map/ppermute | solution.py:350
  29.5 19.1 %copy-start.8 = (f32[256]{0:T(256)S(1)}, f32[256]{0:T(256)}, u32[]{:S(2)}) copy-start(f32[256]{0:T(256)} %param.22) | copy-start | bytes 3076
  29.5 19.2 %copy-start.3 = (bf16[256,256]{1,0:T(8,128)(2,1)S(1)}, bf16[256,256]{1,0:T(8,128)(2,1)}, u32[]{:S(2)}) copy-start(bf16[256,256]{1,0:T(8,128)(2,1)} %constant.6.clone.refs_10_.had_ref) | copy-start | bytes 393220
  52.3 6.2 %collective-permute-start.16 = (f32[8,12,128]{2,1,0:T(8,128)S(1)}, f32[8,12,128]{2,1,0:T(8,128)S(1)}, u32[]{:S(2)}, u32[]{:S(2)}) collective-permute-start(f32[8,12,128]{2,1,0:T(8,128)S(1)} %get-tuple-element.71), channel_id=1, source_target_pairs={{0,28},{4,8},{8,4},{12,16},{16,12},{20,24},{24,20},{28,0},{1,29},{... | collective-permute-start | bytes 147464 | tf_op jit(solution)/shard_map/ppermute | solution.py:343
  52.4 6.1 %collective-permute-start.15 = (f32[8,12,128]{2,1,0:T(8,128)S(1)}, f32[8,12,128]{2,1,0:T(8,128)S(1)}, u32[]{:S(2)}, u32[]{:S(2)}) collective-permute-start(f32[8,12,128]{2,1,0:T(8,128)S(1)} %get-tuple-element.69.refs_3_), channel_id=1, source_target_pairs={{0,4},{4,0},{8,12},{12,8},{16,20},{20,16},{24,28},{28,24},{1,5},{5... | collective-permute-start | bytes 147464 | tf_op jit(solution)/shard_map/ppermute | solution.py:343
  53.1 4.8 %collective-permute-start.18 = (f32[4,12,128]{2,1,0:T(8,128)S(1)}, f32[4,12,128]{2,1,0:T(8,128)S(1)}, u32[]{:S(2)}, u32[]{:S(2)}) collective-permute-start(f32[4,12,128]{2,1,0:T(8,128)S(1)} %get-tuple-element.72), channel_id=1, source_target_pairs={{0,8},{4,28},{8,16},{12,4},{16,24},{20,12},{24,0},{28,20},{1,9},{5... | collective-permute-start | bytes 73736 | tf_op jit(solution)/shard_map/ppermute | solution.py:350
  54.6 3.9 %collective-permute-start.17 = (f32[4,12,128]{2,1,0:T(8,128)S(1)}, f32[4,12,128]{2,1,0:T(8,128)S(1)}, u32[]{:S(2)}, u32[]{:S(2)}) collective-permute-start(f32[4,12,128]{2,1,0:T(8,128)S(1)} %get-tuple-element.70.refs_4_), channel_id=1, source_target_pairs={{0,24},{4,12},{8,0},{12,20},{16,8},{20,28},{24,16},{28,4},{1,25},{... | collective-permute-start | bytes 73736 | tf_op jit(solution)/shard_map/ppermute | solution.py:350
  56.2 17.1 %collective-permute-start.12 = (s16[272,128]{1,0:T(8,128)(2,1)S(1)}, s16[272,128]{1,0:T(8,128)(2,1)S(1)}, u32[]{:S(2)}, u32[]{:S(2)}) collective-permute-start(s16[272,128]{1,0:T(8,128)(2,1)S(1)} %get-tuple-element.66), channel_id=1, source_target_pairs={{0,1},{1,0},{2,3},{3,2},{4,5},{5,4},{6,7},{7,6},{8,9},{9,8},{10,11... | collective-permute-start | bytes 208904 | tf_op jit(solution)/shard_map/ppermute | solution.py:335
  61.4 9.9 %all-to-all-start.1 = ((f32[32,1,128]{2,1,0:T(1,128)}), f32[32,1,128]{2,1,0:T(1,128)S(1)}, u32[]{:S(2)}, u32[]{:S(2)}) async-start(f32[32,1,128]{2,1,0:T(1,128)} %bitcast.9), calls=%async_computation.1 | async-start | bytes 32768 | tf_op jit(solution)/shard_map/all_to_all | solution.py:460
  64.1 12.6 %collective-permute-start.13 = (s16[272,128]{1,0:T(8,128)(2,1)S(1)}, s16[272,128]{1,0:T(8,128)(2,1)S(1)}, u32[]{:S(2)}, u32[]{:S(2)}) collective-permute-start(s16[272,128]{1,0:T(8,128)(2,1)S(1)} %get-tuple-element.67), channel_id=1, source_target_pairs={{0,2},{1,3},{2,0},{3,1},{4,6},{5,7},{6,4},{7,5},{8,10},{9,11},{10,... | collective-permute-start | bytes 208904 | tf_op jit(solution)/shard_map/ppermute | solution.py:335
  66.9 9.9 %collective-permute-start.14 = (s16[272,128]{1,0:T(8,128)(2,1)S(1)}, s16[272,128]{1,0:T(8,128)(2,1)S(1)}, u32[]{:S(2)}, u32[]{:S(2)}) collective-permute-start(s16[272,128]{1,0:T(8,128)(2,1)S(1)} %get-tuple-element.68), channel_id=1, source_target_pairs={{0,3},{1,2},{2,1},{3,0},{4,7},{5,6},{6,5},{7,4},{8,11},{9,10},{10,... | collective-permute-start | bytes 208904 | tf_op jit(solution)/shard_map/ppermute | solution.py:335
  72.3 5.1 %collective-permute-start.19 = (s16[272,128]{1,0:T(8,128)(2,1)S(1)}, s16[272,128]{1,0:T(8,128)(2,1)S(1)}, u32[]{:S(2)}, u32[]{:S(2)}) collective-permute-start(s16[272,128]{1,0:T(8,128)(2,1)S(1)} %get-tuple-element.77), channel_id=1, source_target_pairs={{0,1},{1,0},{2,3},{3,2},{4,5},{5,4},{6,7},{7,6},{8,9},{9,8},{10,11... | collective-permute-start | bytes 208904 | tf_op jit(solution)/shard_map/ppermute | solution.py:335
  72.7 8.4 %collective-permute-start.20 = (s16[272,128]{1,0:T(8,128)(2,1)S(1)}, s16[272,128]{1,0:T(8,128)(2,1)S(1)}, u32[]{:S(2)}, u32[]{:S(2)}) collective-permute-start(s16[272,128]{1,0:T(8,128)(2,1)S(1)} %get-tuple-element.78), channel_id=1, source_target_pairs={{0,2},{1,3},{2,0},{3,1},{4,6},{5,7},{6,4},{7,5},{8,10},{9,11},{10,... | collective-permute-start | bytes 208904 | tf_op jit(solution)/shard_map/ppermute | solution.py:335
  73.4 7.8 %collective-permute-start.21 = (s16[272,128]{1,0:T(8,128)(2,1)S(1)}, s16[272,128]{1,0:T(8,128)(2,1)S(1)}, u32[]{:S(2)}, u32[]{:S(2)}) collective-permute-start(s16[272,128]{1,0:T(8,128)(2,1)S(1)} %get-tuple-element.79), channel_id=1, source_target_pairs={{0,3},{1,2},{2,1},{3,0},{4,7},{5,6},{6,5},{7,4},{8,11},{9,10},{10,... | collective-permute-start | bytes 208904 | tf_op jit(solution)/shard_map/ppermute | solution.py:335

commit v3 on v2

--- a/solution.py
+++ b/solution.py
@@ -121,13 +121,29 @@
         ref[pl.ds(0, rows + 1)] = own_ref[pl.ds(0, rows + 1)]
 
 
-def prepare_kernel(count, rows, momentum, est_ref, prev_ref, *refs):
+def prepare_kernel(count, rows, momentum, est_ref, prev_ref, own_ref, *refs):
+    refs[2 * count][...] = own_ref[...]
     me = lax.axis_index("dep")
     for slot in range(count):
         group = pl.ds((me ^ slot) * rows, rows)
         est = est_ref[group]
         encode(refs[slot], est + momentum * (est - prev_ref[group]))
         encode(refs[count + slot], est)
+
+
+def pack_ids(ids, height):
+    if ids.shape[0] > height:
+        half = ids.shape[1] // 2
+        ids = jnp.concatenate([ids[:height, :half], ids[height:, :half]], axis=1)
+    return ids.astype(jnp.int32).astype(jnp.int16)
+
+
+def unpack_ids(packed, block, depth):
+    ids = packed.astype(jnp.int32).astype(f32)
+    if ids.shape[0] < block:
+        half = ids.shape[1] // 2
+        ids = jnp.concatenate([ids[:, :half], ids[:, half:]], axis=0)
+    return ids[:block, :depth]
 
 
 def fill_kernel(count, rows, frames, own_ref, a_ref, b_ref, *refs):
@@ -137,7 +153,7 @@
     ids_ref[pl.ds(0, frames)] = own_ref[rows + 1]
     ids_ref[pl.ds(frames, frames)] = a_ref[rows + 1]
     ids_ref[pl.ds(2 * frames, frames)] = jnp.where((place == 0) | (place == last), -1.0, b_ref[rows + 1])
-    ids = ids_ref[...].astype(jnp.int32).astype(jnp.int16)
+    ids = pack_ids(ids_ref[...], refs[count].shape[0] - refs[0].shape[0])
     for coded, out in zip(refs[:count], refs[count : 2 * count]):
         size = coded.shape[0]
         out[pl.ds(0, size)] = coded[...]
@@ -183,10 +199,8 @@
                 ],
                 axis=0,
             )
-            upper = left.astype(bf16)
-            lower = (left - upper.astype(f32)).astype(bf16)
             weights = table_ref[pl.ds(start + 2 * pair, 2)].reshape(2 * tile, tile)
-            total = total + dot(upper, weights) + dot(lower, weights)
+            total = total + dot(left.astype(bf16), weights)
     acc_ref[...] = total
     to_a_ref, to_b_ref, part_a_ref, part_b_ref = outs
     for r in range(rows):
@@ -205,7 +219,7 @@
     top = rows * depth + 16
     rest = currents[0].shape[0] - top
     wide = jnp.concatenate(
-        [c[pl.ds(top, rest)].astype(jnp.int32).astype(f32)[:block, :depth] for c in currents], axis=1
+        [unpack_ids(c[pl.ds(top, rest)], block, depth) for c in currents], axis=1
     )
     ids_ref[...] = wide
     for pair in range(prints // 2):
@@ -397,15 +411,17 @@
     )
     packs = [own, *partner_exchange(to_a, to_b)]
 
-    more = -(-block // 16) * 16
+    fold = 2 if 2 * depth_local <= tile else 1
+    more = -(-block // (16 * fold)) * 16
     prepared = call(
-        functools.partial(prepare_kernel, count, rows, momenta[0]), [coded] * (2 * count), [estimate, previous]
-    )
+        functools.partial(prepare_kernel, count, rows, momenta[0]), [coded] * (2 * count) + [pack], [estimate, previous, own]
+    )
+    packs[0] = prepared[-1]
     currents = call(
         functools.partial(fill_kernel, count, rows, frames),
         [shape((rows * depth_local + 16 + more, tile), jnp.int16)] * count,
         [*packs, *prepared[:count]],
-        scratch=[pltpu.VMEM((more, tile), f32)],
+        scratch=[pltpu.VMEM((fold * more, tile), f32)],
     )
     (table,) = call(
         table_kernel,
@@ -414,7 +430,7 @@
         anchors=currents[:1],
     )
     currents = depth_exchange(currents)
-    states = depth_exchange(prepared[count:])
+    states = depth_exchange(prepared[count : 2 * count])
     lanes = np.arange(prints * block)
     spread = jnp.asarray(lanes[None] % block == np.arange(block)[:, None], bf16)
     number = jnp.asarray(np.broadcast_to(lanes // block, (8, prints * block)), f32)

time: 82.9 us -> 80.3 us (0.969)
  Pallas kernels: 17.2 us -> 15.8 us
  waiting for transfers between devices: 11.9 us -> 11 us
    pallas_call x12, Pallas kernels: 17.2 us -> 15.8 us  [call(): pl.pallas_call(body, out_shape=tuple(outs), in_specs=[pl.BlockSpec(memory...]
    unnamed x18 -> x16, local copies, waits for them, and re-layouts: 4.5 us -> 4.5 us
  transfers between devices with their start and end apart: 23 -> 23, of which waited for: 8 -> 8; matrix products, arithmetic and copies ran while one was open for 0% -> 0% of each run, Pallas kernels for 10% -> 9%
where the time goes in v3:
time: 80.3 us; the launch traced here: 79.8 us
  starting transfers between devices  33.1 us (41%)
  Pallas kernels  15.8 us (20%)
  blocking collectives  14.6 us (18%)
  waiting for transfers between devices  11 us (14%)
  local copies, waits for them, and re-layouts  4.58 us (6%)
  between operations  0.81 us (1%)
    ppermute x12, starting transfers between devices, depth_exchange(): lax.ppermute(parts[s], 'dep', [(i, i ^ s) for i in range(count)])  18.1 us
    pallas_call x12, Pallas kernels, call(): pl.pallas_call(body, out_shape=tuple(outs), in_specs=[pl.BlockSpec(memory...  15.8 us
    all_to_all x1, blocking collectives, step_sums(): lax.all_to_all(sums, ('lat', 'dep'), split_axis=0, concat_axis=0, tiled=T...  14.6 us
    ppermute x12, waiting for transfers between devices, depth_exchange(): lax.ppermute(parts[s], 'dep', [(i, i ^ s) for i in range(count)])  4.82 us
    unnamed x16, local copies, waits for them, and re-layouts  4.5 us
    ppermute x2, starting transfers between devices, past_exchange(): lax.ppermute(part_a, 'lat', past_b)  3.96 us
    ppermute x3, starting transfers between devices, partner_exchange(): lax.ppermute(to_b, 'lat', pairs_b)  3.73 us
    ppermute x2, starting transfers between devices, past_exchange(): lax.ppermute(part_b, 'lat', past_a)  3.36 us
  transfers between devices with their start and end apart: 23, of which 8 were waited for; matrix products, arithmetic and copies ran while one was open for 0% of the time, Pallas kernels for 9%

profile of v3, /device:TPU:0, one launch (start us, length us, event | category | flops | bytes accessed | tf_op | source)
XLA Modules:
  0.0 79.8 jit_solution(10591950171394680539)
XLA Ops:
  0.6 2.2 %shard_map.140 = (f32[6,12,128]{2,1,0:T(8,128)}, f32[6,12,128]{2,1,0:T(8,128)}, f32[6,12,128]{2,1,0:T(8,128)}) custom-call(s32[12]{0:T(128)} %bitcast.20, s32[12,3,1,64]{3,2,1,0:T(1,128)} %bitcast.17, s32[12,1,64]{2,1,0:T(1,128)} %bitcast.18, s32[12,1,64]{2,1,0:T(1,128)} %bitcast.19, f32[12,4,128]{2,1,0:T(4,128)} %bitcast.16, f32[16,128]{1,0:T(8,128)} %refs_4_.1), custom_call_target="tpu_custom_call" | custom-call | bytes 158720 | tf_op jit(solution)/shard_map/pallas_call | solution.py:60
  2.8 0.5 collective-permute-start
  3.4 3.6 %collective-permute-start.1 = (f32[6,12,128]{2,1,0:T(8,128)}, f32[6,12,128]{2,1,0:T(8,128)S(1)}, u32[]{:S(2)}, u32[]{:S(2)}) collective-permute-start(f32[6,12,128]{2,1,0:T(8,128)} %get-tuple-element.45), channel_id=1, source_target_pairs={{0,28},{4,8},{8,4},{12,16},{16,12},{20,24},{24,20},{28,0},{1,29},{... | collective-permute-start | bytes 110600 | tf_op jit(solution)/shard_map/ppermute | solution.py:357
  6.9 1.0 %copy-done.1 = f32[16,64,128]{2,1,0:T(8,128)S(1)} copy-done((f32[16,64,128]{2,1,0:T(8,128)S(1)}, f32[16,64,128]{2,1,0:T(8,128)}, u32[]{:S(2)}) %copy-start.1) | copy-done | bytes 524312
  8.0 1.0 %copy-done.2 = f32[16,64,128]{2,1,0:T(8,128)S(1)} copy-done((f32[16,64,128]{2,1,0:T(8,128)S(1)}, f32[16,64,128]{2,1,0:T(8,128)}, u32[]{:S(2)}) %copy-start.2) | copy-done | bytes 524312
  9.0 0.8 copy-done.6
  9.8 0.3 shard_map.141
  10.1 0.0 collective-permute-done.a_ref.refs_4_.refs_1_
  10.2 0.0 collective-permute-done.1.b_ref.refs_5_.refs_2_
  10.2 0.1 shard_map.142
  10.3 1.6 %collective-permute-start.2 = (s16[304,128]{1,0:T(8,128)(2,1)S(1)}, s16[304,128]{1,0:T(8,128)(2,1)S(1)}, u32[]{:S(2)}, u32[]{:S(2)}) collective-permute-start(s16[304,128]{1,0:T(8,128)(2,1)S(1)} %get-tuple-element.51), channel_id=1, source_target_pairs={{0,1},{1,0},{2,3},{3,2},{4,5},{5,4},{6,7},{7,6},{8,9},{9,8},{10,11... | collective-permute-start | bytes 233480 | tf_op jit(solution)/shard_map/ppermute | solution.py:349
  11.9 2.6 %collective-permute-start.3 = (s16[304,128]{1,0:T(8,128)(2,1)S(1)}, s16[304,128]{1,0:T(8,128)(2,1)S(1)}, u32[]{:S(2)}, u32[]{:S(2)}) collective-permute-start(s16[304,128]{1,0:T(8,128)(2,1)S(1)} %get-tuple-element.52), channel_id=1, source_target_pairs={{0,2},{1,3},{2,0},{3,1},{4,6},{5,7},{6,4},{7,5},{8,10},{9,11},{10,... | collective-permute-start | bytes 233480 | tf_op jit(solution)/shard_map/ppermute | solution.py:349
  14.5 0.2 collective-permute-start.4
  14.7 0.7 collective-permute-start.5
  15.4 3.5 %collective-permute-start.6 = (s16[272,128]{1,0:T(8,128)(2,1)S(1)}, s16[272,128]{1,0:T(8,128)(2,1)S(1)}, u32[]{:S(2)}, u32[]{:S(2)}) collective-permute-start(s16[272,128]{1,0:T(8,128)(2,1)S(1)} %get-tuple-element.56), channel_id=1, source_target_pairs={{0,2},{1,3},{2,0},{3,1},{4,6},{5,7},{6,4},{7,5},{8,10},{9,11},{10,... | collective-permute-start | bytes 208904 | tf_op jit(solution)/shard_map/ppermute | solution.py:349
  18.9 1.6 %copy-done = bf16[64,128,128]{2,1,0:T(8,128)(2,1)S(1)} copy-done((bf16[64,128,128]{2,1,0:T(8,128)(2,1)S(1)}, bf16[64,128,128]{2,1,0:T(8,128)(2,1)}, u32[]{:S(2)}) %copy-start) | copy-done | bytes 2097176
  20.5 0.1 shard_map.143.refs_4_.refs_13_.refs_10_
  20.6 0.0 copy-start.4
  20.6 0.0 copy-start.5
  20.6 0.0 collective-permute-done.2.refs_1_
  20.6 0.3 collective-permute-start.7
  20.9 0.4 collective-permute-done.3.refs_2_
  21.3 0.0 collective-permute-done.4.refs_3_
  21.3 2.1 %shard_map.144 = (f32[8,12,128]{2,1,0:T(8,128)S(1)}, f32[8,12,128]{2,1,0:T(8,128)S(1)}, f32[4,12,128]{2,1,0:T(8,128)S(1)}, f32[4,12,128]{2,1,0:T(8,128)S(1)}, bf...) custom-call(s16[304,128]{1,0:T(8,128)(2,1)S(1)} %get-tuple-element.50.anchor_ref.refs_0_, ...), custom_call_target="tpu_custom_call" | custom-call | flops 1006632960 | bytes 3907584 | tf_op jit(solution)/shard_map/pallas_call | solution.py:60
  23.5 0.1 collective-permute-start.9
  23.6 0.0 collective-permute-start.8
  23.6 0.0 collective-permute-done.5.refs_0_.refs_5_
  23.6 2.5 %collective-permute-start.11 = (f32[4,12,128]{2,1,0:T(8,128)S(1)}, f32[4,12,128]{2,1,0:T(8,128)S(1)}, u32[]{:S(2)}, u32[]{:S(2)}) collective-permute-start(f32[4,12,128]{2,1,0:T(8,128)S(1)} %get-tuple-element.61), channel_id=1, source_target_pairs={{0,8},{4,28},{8,16},{12,4},{16,24},{20,12},{24,0},{28,20},{1,9},{5... | collective-permute-start | bytes 73736 | tf_op jit(solution)/shard_map/ppermute | solution.py:364
  26.1 0.0 collective-permute-done.6.refs_1_.refs_6_
  26.1 1.9 %collective-permute-start.10 = (f32[4,12,128]{2,1,0:T(8,128)S(1)}, f32[4,12,128]{2,1,0:T(8,128)S(1)}, u32[]{:S(2)}, u32[]{:S(2)}) collective-permute-start(f32[4,12,128]{2,1,0:T(8,128)S(1)} %get-tuple-element.59.refs_7_), channel_id=1, source_target_pairs={{0,24},{4,12},{8,0},{12,20},{16,8},{20,28},{24,16},{28,4},{1,25},{... | collective-permute-start | bytes 73736 | tf_op jit(solution)/shard_map/ppermute | solution.py:364
  28.1 0.5 shard_map.145.refs_12_.refs_9_
  28.6 0.0 copy-start.7
  28.6 0.0 copy-start.3
  28.6 0.2 collective-permute-done.11.refs_11_
  28.8 1.2 %collective-permute-done.10.refs_10_ = f32[4,12,128]{2,1,0:T(8,128)S(1)} collective-permute-done((f32[4,12,128]{2,1,0:T(8,128)S(1)}, f32[4,12,128]{2,1,0:T(8,128)S(1)}, u32[]{:S(2)}, u32[]{:S(2)}) %collective-permute-start.10) | collective-permute-done | bytes 24608 | tf_op jit(solution)/shard_map/ppermute | solution.py:364
  30.1 2.3 %shard_map.146 = (f32[256,512]{1,0:T(8,128)S(1)}, f32[32,128]{1,0:T(8,128)S(1)}) custom-call(s16[272,128]{1,0:T(8,128)(2,1)S(1)} %collective-permute-done.5.refs_0_.refs_5_, s16[272,128]{1,0:T(8,128)(2,1)S(1)} %collective-permute-done.6.refs_1_.refs_6_, s16[272,128]{1,0:T(8,128)(2,1)S(1)} %collective-permute-done.7.refs_2_.refs_7_, ...), custom_call_target="tpu_custom_call" | custom-call | flops 2013265920 | bytes 4280320 | tf_op jit(solution)/shard_map/pallas_call | solution.py:60
  32.4 14.6 %all_to_all.22 = f32[32,1,128]{2,1,0:T(1,128)S(1)} all-to-all(f32[32,1,128]{2,1,0:T(1,128)S(1)} %bitcast.15), channel_id=1, replica_groups=mesh['lat'=8,'dep'=4] {'lat','dep'}, dimensions={0} | all-to-all | bytes 32768 | tf_op jit(solution)/shard_map/all_to_all | solution.py:476
  46.9 0.1 broadcast_in_dim.2.refs_11_.limits_ref
  47.1 2.8 %shard_map.147 = (f32[8,12,128]{2,1,0:T(8,128)S(1)}, f32[8,12,128]{2,1,0:T(8,128)S(1)}, f32[4,12,128]{2,1,0:T(8,128)S(1)}, f32[4,12,128]{2,1,0:T(8,128)S(1)}, f3...) custom-call(s16[304,128]{1,0:T(8,128)(2,1)S(1)} %get-tuple-element.50.anchor_ref.refs_0_, ...), custom_call_target="tpu_custom_call" | custom-call | flops 1006632960 | bytes 5996544 | tf_op jit(solution)/shard_map/pallas_call | solution.py:60
  49.9 0.1 collective-permute-start.16
  50.0 0.7 collective-permute-start.15
  50.6 1.5 %collective-permute-start.18 = (f32[4,12,128]{2,1,0:T(8,128)S(1)}, f32[4,12,128]{2,1,0:T(8,128)S(1)}, u32[]{:S(2)}, u32[]{:S(2)}) collective-permute-start(f32[4,12,128]{2,1,0:T(8,128)S(1)} %get-tuple-element.74), channel_id=1, source_target_pairs={{0,8},{4,28},{8,16},{12,4},{16,24},{20,12},{24,0},{28,20},{1,9},{5... | collective-permute-start | bytes 73736 | tf_op jit(solution)/shard_map/ppermute | solution.py:364
  52.1 1.5 %collective-permute-start.17 = (f32[4,12,128]{2,1,0:T(8,128)S(1)}, f32[4,12,128]{2,1,0:T(8,128)S(1)}, u32[]{:S(2)}, u32[]{:S(2)}) collective-permute-start(f32[4,12,128]{2,1,0:T(8,128)S(1)} %get-tuple-element.72.refs_4_), channel_id=1, source_target_pairs={{0,24},{4,12},{8,0},{12,20},{16,8},{20,28},{24,16},{28,4},{1,25},{... | collective-permute-start | bytes 73736 | tf_op jit(solution)/shard_map/ppermute | solution.py:364
  53.6 0.2 shard_map.148
  53.8 0.5 collective-permute-start.12
  54.3 1.1 %collective-permute-done.18.refs_8_ = f32[4,12,128]{2,1,0:T(8,128)S(1)} collective-permute-done((f32[4,12,128]{2,1,0:T(8,128)S(1)}, f32[4,12,128]{2,1,0:T(8,128)S(1)}, u32[]{:S(2)}, u32[]{:S(2)}) %collective-permute-start.18) | collective-permute-done | bytes 24608 | tf_op jit(solution)/shard_map/ppermute | solution.py:364
  55.4 0.6 collective-permute-done.17.refs_7_
  56.0 0.0 collective-permute-done.16.refs_6_
  56.0 0.0 collective-permute-done.15.refs_5_
  56.0 2.9 %shard_map.149 = (f32[256,512]{1,0:T(8,128)S(1)}, f32[32,128]{1,0:T(8,128)}) custom-call(f32[6,12,128]{2,1,0:T(8,128)S(1)} %get-tuple-element.43.own_ref.refs_3_.refs_0_, f32[6,12,128]{2,1,0:T(8,128)S(1)} %collective-permute-done.a_ref.refs_4_.refs_1_, f32[6,12,128]{2,1,0:T(8,128)S(1)} %collective-permute-done.1.b_ref.refs_5_.refs_2_, ...), custom_call_target="tpu_custom_call" | custom-call | flops 2013265920 | bytes 4280320 | tf_op jit(solution)/shard_map/pallas_call | solution.py:60
  58.9 2.7 %all-to-all-start.1 = ((f32[32,1,128]{2,1,0:T(1,128)}), f32[32,1,128]{2,1,0:T(1,128)S(1)}, u32[]{:S(2)}, u32[]{:S(2)}) async-start(f32[32,1,128]{2,1,0:T(1,128)} %bitcast.9), calls=%async_computation.1 | async-start | bytes 32768 | tf_op jit(solution)/shard_map/all_to_all | solution.py:476
  61.7 2.7 %collective-permute-start.13 = (s16[272,128]{1,0:T(8,128)(2,1)S(1)}, s16[272,128]{1,0:T(8,128)(2,1)S(1)}, u32[]{:S(2)}, u32[]{:S(2)}) collective-permute-start(s16[272,128]{1,0:T(8,128)(2,1)S(1)} %get-tuple-element.69), channel_id=1, source_target_pairs={{0,2},{1,3},{2,0},{3,1},{4,6},{5,7},{6,4},{7,5},{8,10},{9,11},{10,... | collective-permute-start | bytes 208904 | tf_op jit(solution)/shard_map/ppermute | solution.py:349
  64.4 1.5 %collective-permute-start.14 = (s16[272,128]{1,0:T(8,128)(2,1)S(1)}, s16[272,128]{1,0:T(8,128)(2,1)S(1)}, u32[]{:S(2)}, u32[]{:S(2)}) collective-permute-start(s16[272,128]{1,0:T(8,128)(2,1)S(1)} %get-tuple-element.70), channel_id=1, source_target_pairs={{0,3},{1,2},{2,1},{3,0},{4,7},{5,6},{6,5},{7,4},{8,11},{9,10},{10,... | collective-permute-start | bytes 208904 | tf_op jit(solution)/shard_map/ppermute | solution.py:349
  65.9 3.0 %all-to-all-done.1 = f32[32,1,128]{2,1,0:T(1,128)S(1)} async-done(((f32[32,1,128]{2,1,0:T(1,128)}), f32[32,1,128]{2,1,0:T(1,128)S(1)}, u32[]{:S(2)}, u32[]{:S(2)}) %all-to-all-start.1) | async-done | bytes 16416 | tf_op jit(solution)/shard_map/all_to_all | solution.py:476
  68.9 1.0 %shard_map.150 = (s16[272,128]{1,0:T(8,128)(2,1)S(1)}, s16[272,128]{1,0:T(8,128)(2,1)S(1)}, s16[272,128]{1,0:T(8,128)(2,1)S(1)}, s16[272,128]{1,0:T(8,128)(2,1)S(1)}) custom-call(f32[32,128]{1,0:T(8,128)S(1)} %bitcast.14, f32[256,512]{1,0:T(8,128)S(1)} %get-tuple-element.76.current_ref, f32[256,512]{1,0:T(8,128)S(1)} %get-tuple-element.77.grad_ref, ...), custom_call_target="tpu_custom_call" | custom-call | bytes 1605632 | tf_op jit(solution)/shard_map/pallas_call | solution.py:60
  69.8 0.5 collective-permute-start.19
  70.3 0.6 collective-permute-start.20
  70.9 3.4 %collective-permute-start.21 = (s16[272,128]{1,0:T(8,128)(2,1)S(1)}, s16[272,128]{1,0:T(8,128)(2,1)S(1)}, u32[]{:S(2)}, u32[]{:S(2)}) collective-permute-start(s16[272,128]{1,0:T(8,128)(2,1)S(1)} %get-tuple-element.81), channel_id=1, source_target_pairs={{0,3},{1,2},{2,1},{3,0},{4,7},{5,6},{6,5},{7,4},{8,11},{9,10},{10,... | collective-permute-start | bytes 208904 | tf_op jit(solution)/shard_map/ppermute | solution.py:349
  74.3 0.0 collective-permute-done.13.refs_2_
  74.3 0.0 collective-permute-done.14.refs_3_
  74.3 0.7 collective-permute-done.19.refs_5_
  74.9 3.7 %collective-permute-done.20.refs_6_ = s16[272,128]{1,0:T(8,128)(2,1)S(1)} collective-permute-done((s16[272,128]{1,0:T(8,128)(2,1)S(1)}, s16[272,128]{1,0:T(8,128)(2,1)S(1)}, u32[]{:S(2)}, u32[]{:S(2)}) %collective-permute-start.20) | collective-permute-done | bytes 69664 | tf_op jit(solution)/shard_map/ppermute | solution.py:349
  78.7 0.0 collective-permute-done.21.refs_7_
  78.7 1.2 %shard_map.151 = (f32[16,64,128]{2,1,0:T(8,128)}, f32[16,64,128]{2,1,0:T(8,128)}) custom-call(s16[272,128]{1,0:T(8,128)(2,1)S(1)} %get-tuple-element.67.refs_0_, s16[272,128]{1,0:T(8,128)(2,1)S(1)} %collective-permute-done.12.refs_1_, s16[272,128]{1,0:T(8,128)(2,1)S(1)} %collective-permute-done.13.refs_2_, ...), custom_call_target="tpu_custom_call" | custom-call | bytes 1605632 | tf_op jit(solution)/shard_map/pallas_call | solution.py:60
  (12 shorter events, 0.0 us)
Async XLA Ops:
  2.8 7.3 %collective-permute-start = (f32[6,12,128]{2,1,0:T(8,128)}, f32[6,12,128]{2,1,0:T(8,128)S(1)}, u32[]{:S(2)}, u32[]{:S(2)}) collective-permute-start(f32[6,12,128]{2,1,0:T(8,128)} %get-tuple-element.44), channel_id=1, source_target_pairs={{0,4},{4,0},{8,12},{12,8},{16,20},{20,16},{24,28},{28,24},{1,5},{5... | collective-permute-start | bytes 110600 | tf_op jit(solution)/shard_map/ppermute | solution.py:357
  3.4 6.8 %collective-permute-start.1 = (f32[6,12,128]{2,1,0:T(8,128)}, f32[6,12,128]{2,1,0:T(8,128)S(1)}, u32[]{:S(2)}, u32[]{:S(2)}) collective-permute-start(f32[6,12,128]{2,1,0:T(8,128)} %get-tuple-element.45), channel_id=1, source_target_pairs={{0,28},{4,8},{8,4},{12,16},{16,12},{20,24},{24,20},{28,0},{1,29},{... | collective-permute-start | bytes 110600 | tf_op jit(solution)/shard_map/ppermute | solution.py:357
  6.9 1.0 %copy-start.1 = (f32[16,64,128]{2,1,0:T(8,128)S(1)}, f32[16,64,128]{2,1,0:T(8,128)}, u32[]{:S(2)}) copy-start(f32[16,64,128]{2,1,0:T(8,128)} %est_ref.1) | copy-start | bytes 1572868
  8.0 1.0 %copy-start.2 = (f32[16,64,128]{2,1,0:T(8,128)S(1)}, f32[16,64,128]{2,1,0:T(8,128)}, u32[]{:S(2)}) copy-start(f32[16,64,128]{2,1,0:T(8,128)} %prev_ref.1) | copy-start | bytes 1572868
  9.0 0.8 copy-start.6
  10.3 10.4 %collective-permute-start.2 = (s16[304,128]{1,0:T(8,128)(2,1)S(1)}, s16[304,128]{1,0:T(8,128)(2,1)S(1)}, u32[]{:S(2)}, u32[]{:S(2)}) collective-permute-start(s16[304,128]{1,0:T(8,128)(2,1)S(1)} %get-tuple-element.51), channel_id=1, source_target_pairs={{0,1},{1,0},{2,3},{3,2},{4,5},{5,4},{6,7},{7,6},{8,9},{9,8},{10,11... | collective-permute-start | bytes 233480 | tf_op jit(solution)/shard_map/ppermute | solution.py:349
  11.9 9.4 %collective-permute-start.3 = (s16[304,128]{1,0:T(8,128)(2,1)S(1)}, s16[304,128]{1,0:T(8,128)(2,1)S(1)}, u32[]{:S(2)}, u32[]{:S(2)}) collective-permute-start(s16[304,128]{1,0:T(8,128)(2,1)S(1)} %get-tuple-element.52), channel_id=1, source_target_pairs={{0,2},{1,3},{2,0},{3,1},{4,6},{5,7},{6,4},{7,5},{8,10},{9,11},{10,... | collective-permute-start | bytes 233480 | tf_op jit(solution)/shard_map/ppermute | solution.py:349
  14.5 6.9 %collective-permute-start.4 = (s16[304,128]{1,0:T(8,128)(2,1)S(1)}, s16[304,128]{1,0:T(8,128)(2,1)S(1)}, u32[]{:S(2)}, u32[]{:S(2)}) collective-permute-start(s16[304,128]{1,0:T(8,128)(2,1)S(1)} %get-tuple-element.53), channel_id=1, source_target_pairs={{0,3},{1,2},{2,1},{3,0},{4,7},{5,6},{6,5},{7,4},{8,11},{9,10},{10,... | collective-permute-start | bytes 233480 | tf_op jit(solution)/shard_map/ppermute | solution.py:349
  14.7 8.9 %collective-permute-start.5 = (s16[272,128]{1,0:T(8,128)(2,1)S(1)}, s16[272,128]{1,0:T(8,128)(2,1)S(1)}, u32[]{:S(2)}, u32[]{:S(2)}) collective-permute-start(s16[272,128]{1,0:T(8,128)(2,1)S(1)} %get-tuple-element.55), channel_id=1, source_target_pairs={{0,1},{1,0},{2,3},{3,2},{4,5},{5,4},{6,7},{7,6},{8,9},{9,8},{10,11... | collective-permute-start | bytes 208904 | tf_op jit(solution)/shard_map/ppermute | solution.py:349
  15.4 10.7 %collective-permute-start.6 = (s16[272,128]{1,0:T(8,128)(2,1)S(1)}, s16[272,128]{1,0:T(8,128)(2,1)S(1)}, u32[]{:S(2)}, u32[]{:S(2)}) collective-permute-start(s16[272,128]{1,0:T(8,128)(2,1)S(1)} %get-tuple-element.56), channel_id=1, source_target_pairs={{0,2},{1,3},{2,0},{3,1},{4,6},{5,7},{6,4},{7,5},{8,10},{9,11},{10,... | collective-permute-start | bytes 208904 | tf_op jit(solution)/shard_map/ppermute | solution.py:349
  18.9 1.6 %copy-start = (bf16[64,128,128]{2,1,0:T(8,128)(2,1)S(1)}, bf16[64,128,128]{2,1,0:T(8,128)(2,1)}, u32[]{:S(2)}) copy-start(bf16[64,128,128]{2,1,0:T(8,128)(2,1)} %table_ref.1) | copy-start | bytes 6291460
  20.6 7.4 %copy-start.4 = (bf16[40,2560]{1,0:T(8,128)(2,1)S(1)}, bf16[40,2560]{1,0:T(8,128)(2,1)}, u32[]{:S(2)}) copy-start(bf16[40,2560]{1,0:T(8,128)(2,1)} %constant.7.clone.spread_ref) | copy-start | bytes 614404
  20.6 7.4 %copy-start.5 = (f32[8,2560]{1,0:T(8,128)S(1)}, f32[8,2560]{1,0:T(8,128)}, u32[]{:S(2)}) copy-start(f32[8,2560]{1,0:T(8,128)} %constant.8.clone.number_ref) | copy-start | bytes 245764
  20.6 8.0 %collective-permute-start.7 = (s16[272,128]{1,0:T(8,128)(2,1)S(1)}, s16[272,128]{1,0:T(8,128)(2,1)S(1)}, u32[]{:S(2)}, u32[]{:S(2)}) collective-permute-start(s16[272,128]{1,0:T(8,128)(2,1)S(1)} %get-tuple-element.57), channel_id=1, source_target_pairs={{0,3},{1,2},{2,1},{3,0},{4,7},{5,6},{6,5},{7,4},{8,11},{9,10},{10,... | collective-permute-start | bytes 208904 | tf_op jit(solution)/shard_map/ppermute | solution.py:349
  23.5 6.6 %collective-permute-start.9 = (f32[8,12,128]{2,1,0:T(8,128)S(1)}, f32[8,12,128]{2,1,0:T(8,128)S(1)}, u32[]{:S(2)}, u32[]{:S(2)}) collective-permute-start(f32[8,12,128]{2,1,0:T(8,128)S(1)} %get-tuple-element.60), channel_id=1, source_target_pairs={{0,28},{4,8},{8,4},{12,16},{16,12},{20,24},{24,20},{28,0},{1,29},{... | collective-permute-start | bytes 147464 | tf_op jit(solution)/shard_map/ppermute | solution.py:357
  23.6 6.5 %collective-permute-start.8 = (f32[8,12,128]{2,1,0:T(8,128)S(1)}, f32[8,12,128]{2,1,0:T(8,128)S(1)}, u32[]{:S(2)}, u32[]{:S(2)}) collective-permute-start(f32[8,12,128]{2,1,0:T(8,128)S(1)} %get-tuple-element.58.refs_6_), channel_id=1, source_target_pairs={{0,4},{4,0},{8,12},{12,8},{16,20},{20,16},{24,28},{28,24},{1,5},{5... | collective-permute-start | bytes 147464 | tf_op jit(solution)/shard_map/ppermute | solution.py:357
  23.6 5.2 %collective-permute-start.11 = (f32[4,12,128]{2,1,0:T(8,128)S(1)}, f32[4,12,128]{2,1,0:T(8,128)S(1)}, u32[]{:S(2)}, u32[]{:S(2)}) collective-permute-start(f32[4,12,128]{2,1,0:T(8,128)S(1)} %get-tuple-element.61), channel_id=1, source_target_pairs={{0,8},{4,28},{8,16},{12,4},{16,24},{20,12},{24,0},{28,20},{1,9},{5... | collective-permute-start | bytes 73736 | tf_op jit(solution)/shard_map/ppermute | solution.py:364
  26.1 3.9 %collective-permute-start.10 = (f32[4,12,128]{2,1,0:T(8,128)S(1)}, f32[4,12,128]{2,1,0:T(8,128)S(1)}, u32[]{:S(2)}, u32[]{:S(2)}) collective-permute-start(f32[4,12,128]{2,1,0:T(8,128)S(1)} %get-tuple-element.59.refs_7_), channel_id=1, source_target_pairs={{0,24},{4,12},{8,0},{12,20},{16,8},{20,28},{24,16},{28,4},{1,25},{... | collective-permute-start | bytes 73736 | tf_op jit(solution)/shard_map/ppermute | solution.py:364
  28.6 18.4 %copy-start.7 = (f32[256]{0:T(256)S(1)}, f32[256]{0:T(256)}, u32[]{:S(2)}) copy-start(f32[256]{0:T(256)} %param.22) | copy-start | bytes 3076
  28.6 18.4 %copy-start.3 = (bf16[256,256]{1,0:T(8,128)(2,1)S(1)}, bf16[256,256]{1,0:T(8,128)(2,1)}, u32[]{:S(2)}) copy-start(bf16[256,256]{1,0:T(8,128)(2,1)} %constant.6.clone.refs_10_.had_ref) | copy-start | bytes 393220
  49.9 6.2 %collective-permute-start.16 = (f32[8,12,128]{2,1,0:T(8,128)S(1)}, f32[8,12,128]{2,1,0:T(8,128)S(1)}, u32[]{:S(2)}, u32[]{:S(2)}) collective-permute-start(f32[8,12,128]{2,1,0:T(8,128)S(1)} %get-tuple-element.73), channel_id=1, source_target_pairs={{0,28},{4,8},{8,4},{12,16},{16,12},{20,24},{24,20},{28,0},{1,29},{... | collective-permute-start | bytes 147464 | tf_op jit(solution)/shard_map/ppermute | solution.py:357
  50.0 6.1 %collective-permute-start.15 = (f32[8,12,128]{2,1,0:T(8,128)S(1)}, f32[8,12,128]{2,1,0:T(8,128)S(1)}, u32[]{:S(2)}, u32[]{:S(2)}) collective-permute-start(f32[8,12,128]{2,1,0:T(8,128)S(1)} %get-tuple-element.71.refs_3_), channel_id=1, source_target_pairs={{0,4},{4,0},{8,12},{12,8},{16,20},{20,16},{24,28},{28,24},{1,5},{5... | collective-permute-start | bytes 147464 | tf_op jit(solution)/shard_map/ppermute | solution.py:357
  50.6 4.8 %collective-permute-start.18 = (f32[4,12,128]{2,1,0:T(8,128)S(1)}, f32[4,12,128]{2,1,0:T(8,128)S(1)}, u32[]{:S(2)}, u32[]{:S(2)}) collective-permute-start(f32[4,12,128]{2,1,0:T(8,128)S(1)} %get-tuple-element.74), channel_id=1, source_target_pairs={{0,8},{4,28},{8,16},{12,4},{16,24},{20,12},{24,0},{28,20},{1,9},{5... | collective-permute-start | bytes 73736 | tf_op jit(solution)/shard_map/ppermute | solution.py:364
  52.1 3.9 %collective-permute-start.17 = (f32[4,12,128]{2,1,0:T(8,128)S(1)}, f32[4,12,128]{2,1,0:T(8,128)S(1)}, u32[]{:S(2)}, u32[]{:S(2)}) collective-permute-start(f32[4,12,128]{2,1,0:T(8,128)S(1)} %get-tuple-element.72.refs_4_), channel_id=1, source_target_pairs={{0,24},{4,12},{8,0},{12,20},{16,8},{20,28},{24,16},{28,4},{1,25},{... | collective-permute-start | bytes 73736 | tf_op jit(solution)/shard_map/ppermute | solution.py:364
  53.8 17.1 %collective-permute-start.12 = (s16[272,128]{1,0:T(8,128)(2,1)S(1)}, s16[272,128]{1,0:T(8,128)(2,1)S(1)}, u32[]{:S(2)}, u32[]{:S(2)}) collective-permute-start(s16[272,128]{1,0:T(8,128)(2,1)S(1)} %get-tuple-element.68), channel_id=1, source_target_pairs={{0,1},{1,0},{2,3},{3,2},{4,5},{5,4},{6,7},{7,6},{8,9},{9,8},{10,11... | collective-permute-start | bytes 208904 | tf_op jit(solution)/shard_map/ppermute | solution.py:349
  58.9 9.9 %all-to-all-start.1 = ((f32[32,1,128]{2,1,0:T(1,128)}), f32[32,1,128]{2,1,0:T(1,128)S(1)}, u32[]{:S(2)}, u32[]{:S(2)}) async-start(f32[32,1,128]{2,1,0:T(1,128)} %bitcast.9), calls=%async_computation.1 | async-start | bytes 32768 | tf_op jit(solution)/shard_map/all_to_all | solution.py:476
  61.7 12.6 %collective-permute-start.13 = (s16[272,128]{1,0:T(8,128)(2,1)S(1)}, s16[272,128]{1,0:T(8,128)(2,1)S(1)}, u32[]{:S(2)}, u32[]{:S(2)}) collective-permute-start(s16[272,128]{1,0:T(8,128)(2,1)S(1)} %get-tuple-element.69), channel_id=1, source_target_pairs={{0,2},{1,3},{2,0},{3,1},{4,6},{5,7},{6,4},{7,5},{8,10},{9,11},{10,... | collective-permute-start | bytes 208904 | tf_op jit(solution)/shard_map/ppermute | solution.py:349
  64.4 9.9 %collective-permute-start.14 = (s16[272,128]{1,0:T(8,128)(2,1)S(1)}, s16[272,128]{1,0:T(8,128)(2,1)S(1)}, u32[]{:S(2)}, u32[]{:S(2)}) collective-permute-start(s16[272,128]{1,0:T(8,128)(2,1)S(1)} %get-tuple-element.70), channel_id=1, source_target_pairs={{0,3},{1,2},{2,1},{3,0},{4,7},{5,6},{6,5},{7,4},{8,11},{9,10},{10,... | collective-permute-start | bytes 208904 | tf_op jit(solution)/shard_map/ppermute | solution.py:349
  69.8 5.1 %collective-permute-start.19 = (s16[272,128]{1,0:T(8,128)(2,1)S(1)}, s16[272,128]{1,0:T(8,128)(2,1)S(1)}, u32[]{:S(2)}, u32[]{:S(2)}) collective-permute-start(s16[272,128]{1,0:T(8,128)(2,1)S(1)} %get-tuple-element.79), channel_id=1, source_target_pairs={{0,1},{1,0},{2,3},{3,2},{4,5},{5,4},{6,7},{7,6},{8,9},{9,8},{10,11... | collective-permute-start | bytes 208904 | tf_op jit(solution)/shard_map/ppermute | solution.py:349
  70.3 8.4 %collective-permute-start.20 = (s16[272,128]{1,0:T(8,128)(2,1)S(1)}, s16[272,128]{1,0:T(8,128)(2,1)S(1)}, u32[]{:S(2)}, u32[]{:S(2)}) collective-permute-start(s16[272,128]{1,0:T(8,128)(2,1)S(1)} %get-tuple-element.80), channel_id=1, source_target_pairs={{0,2},{1,3},{2,0},{3,1},{4,6},{5,7},{6,4},{7,5},{8,10},{9,11},{10,... | collective-permute-start | bytes 208904 | tf_op jit(solution)/shard_map/ppermute | solution.py:349
  70.9 7.8 %collective-permute-start.21 = (s16[272,128]{1,0:T(8,128)(2,1)S(1)}, s16[272,128]{1,0:T(8,128)(2,1)S(1)}, u32[]{:S(2)}, u32[]{:S(2)}) collective-permute-start(s16[272,128]{1,0:T(8,128)(2,1)S(1)} %get-tuple-element.81), channel_id=1, source_target_pairs={{0,3},{1,2},{2,1},{3,0},{4,7},{5,6},{6,5},{7,4},{8,11},{9,10},{10,... | collective-permute-start | bytes 208904 | tf_op jit(solution)/shard_map/ppermute | solution.py:349

commit v4 on v3

--- a/solution.py
+++ b/solution.py
@@ -65,7 +65,7 @@
         scratch_shapes=list(scratch),
         compiler_params=pltpu.CompilerParams(vmem_limit_bytes=limit * 2**20),
         cost_estimate=pl.CostEstimate(flops=flops, bytes_accessed=size, transcendentals=0),
-    )(*prefetch, *anchors, *args, *far)
+    )(*prefetch, *anchors, *args, *(pltpu.with_memory_space_constraint(a, pltpu.HBM) for a in far))
 
 
 def shape(dims, dtype):
@@ -95,12 +95,20 @@
     )
 
 
-def lateral_kernel(rows, frames, mask_ref, *refs):
-    outs, held, sems = refs[5:8], refs[8:13], refs[13]
-    copies = [pltpu.make_async_copy(a, b, sems.at[i]) for i, (a, b) in enumerate(zip(refs[:5], held))]
-    for copy in copies:
+def lateral_kernel(rows, frames, *refs):
+    volumes, kept = refs[6:8], refs[11:13]
+    outs, held, sems, volume_sems = refs[8:11], refs[13:19], refs[19], refs[20]
+    copies = [pltpu.make_async_copy(a, b, sems.at[i]) for i, (a, b) in enumerate(zip(refs[:6], held))]
+    cuts = volume_sems.shape[1]
+    groups = [pl.ds(i * (kept[0].shape[0] // cuts), kept[0].shape[0] // cuts) for i in range(cuts)]
+    brought = [
+        pltpu.make_async_copy(a.at[group], b.at[group], volume_sems.at[j, i])
+        for j, (a, b) in enumerate(zip(volumes, kept))
+        for i, group in enumerate(groups)
+    ]
+    for copy in (*copies, *brought):
         copy.start()
-    id_ref, lo_ref, live_ref, measured_ref, masks_ref = held
+    mask_ref, id_ref, lo_ref, live_ref, measured_ref, masks_ref = held
     odd = lax.axis_index("lat") % 2 == 1
     own_ref = outs[0]
     depth = id_ref.shape[3]
@@ -114,15 +122,16 @@
         ids = [jnp.where((o - 1 >= first) & (o - 1 < end), id_ref[f, o], -1).astype(f32) for o in range(3)]
         for ref, row in zip(outs, (ids[1], jnp.where(odd, ids[0], ids[2]), jnp.where(odd, ids[2], ids[0]))):
             ref[rows + 1, pl.ds(f, 1), pl.ds(0, depth)] = row
-        own_ref[rows, pl.ds(f, 1)] = masks_ref[pl.ds(mask_ref[f], 1)]
+        own_ref[rows, pl.ds(f, 1)] = masks_ref[pl.ds(mask_ref[0, f], 1)]
         for r in range(rows):
             own_ref[r, pl.ds(f, 1)] = measured_ref[f, pl.ds(r, 1)]
     for ref in outs[1:]:
         ref[pl.ds(0, rows + 1)] = own_ref[pl.ds(0, rows + 1)]
-
-
-def prepare_kernel(count, rows, momentum, est_ref, prev_ref, own_ref, *refs):
-    refs[2 * count][...] = own_ref[...]
+    for copy in brought:
+        copy.wait()
+
+
+def prepare_kernel(count, rows, momentum, est_ref, prev_ref, *refs):
     me = lax.axis_index("dep")
     for slot in range(count):
         group = pl.ds((me ^ slot) * rows, rows)
@@ -345,9 +354,8 @@
 
 def depth_exchange(parts):
     count = len(parts)
-    return [parts[0]] + [
-        lax.ppermute(parts[s], "dep", [(i, i ^ s) for i in range(count)]) for s in range(1, count)
-    ]
+    moved = {s: lax.ppermute(parts[s], "dep", [(i, i ^ s) for i in range(count)]) for s in range(count - 1, 0, -1)}
+    return [parts[0]] + [moved[s] for s in range(1, count)]
 
 
 def partner_exchange(to_a, to_b):
@@ -393,6 +401,7 @@
     coded = shape((rows * depth_local + 16, tile), jnp.int16)
 
     small = [
+        mask_id.T,
         jnp.transpose(foot_id, (1, 3, 0, 2)),
         jnp.transpose(foot_lo, (1, 0, 2)),
         jnp.transpose(foot_count, (1, 0, 2)),
@@ -400,23 +409,26 @@
         mask_table,
     ]
     pack = shape((rows + 2, frames, tile), f32)
-    own, to_a, to_b = call(
+    own, to_a, to_b, near_estimate, near_previous = call(
         functools.partial(lateral_kernel, rows, frames),
-        [pack] * 3,
+        [pack] * 3 + [shape(estimate.shape, f32)] * 2,
         [],
-        far=small,
-        scratch=[*(pltpu.VMEM(a.shape, a.dtype) for a in small), pltpu.SemaphoreType.DMA((len(small),))],
-        prefetch=[mask_id[:, 0]],
-        limit=56,
+        far=[*small, estimate, previous],
+        scratch=[
+            pltpu.SMEM(small[0].shape, jnp.int32),
+            *(pltpu.VMEM(a.shape, a.dtype) for a in small[1:]),
+            pltpu.SemaphoreType.DMA((len(small),)),
+            pltpu.SemaphoreType.DMA((2, count)),
+        ],
+
     )
     packs = [own, *partner_exchange(to_a, to_b)]
 
     fold = 2 if 2 * depth_local <= tile else 1
     more = -(-block // (16 * fold)) * 16
     prepared = call(
-        functools.partial(prepare_kernel, count, rows, momenta[0]), [coded] * (2 * count) + [pack], [estimate, previous, own]
-    )
-    packs[0] = prepared[-1]
+        functools.partial(prepare_kernel, count, rows, momenta[0]), [coded] * (2 * count), [near_estimate, near_previous]
+    )
     currents = call(
         functools.partial(fill_kernel, count, rows, frames),
         [shape((rows * depth_local + 16 + more, tile), jnp.int16)] * count,

time: 80.3 us -> 79.1 us (0.985)
  local copies, waits for them, and re-layouts: 4.58 us -> 0.12 us
  waiting for transfers between devices: 11 us -> 14.7 us
    unnamed x16 -> x10, local copies, waits for them, and re-layouts: 4.5 us -> 0.03 us
    ppermute x12, waiting for transfers between devices: 4.82 us -> 7.13 us  [depth_exchange(): lax.ppermute(parts[s], 'dep', [(i, i ^ s) for i in range(count)])]
    ppermute x3, waiting for transfers between devices: 0.01 us -> 1.42 us  [partner_exchange(): lax.ppermute(to_b, 'lat', pairs_b)]
    ppermute x3, starting transfers between devices: 3.73 us -> 4.65 us  [partner_exchange(): lax.ppermute(to_b, 'lat', pairs_b)]
  transfers between devices with their start and end apart: 23 -> 23, of which waited for: 8 -> 10; matrix products, arithmetic and copies ran while one was open for 0% -> 0% of each run, Pallas kernels for 9% -> 9%
where the time goes in v4:
time: 79.1 us; the launch traced here: 78.9 us
  starting transfers between devices  33.5 us (42%)
  Pallas kernels  15.2 us (19%)
  waiting for transfers between devices  14.7 us (19%)
  blocking collectives  14.6 us (18%)
  between operations  0.8 us (1%)
    ppermute x12, starting transfers between devices, depth_exchange(): lax.ppermute(parts[s], 'dep', [(i, i ^ s) for i in range(count)])  18.1 us
    pallas_call x12, Pallas kernels, call(): pl.pallas_call(body, out_shape=tuple(outs), in_specs=[pl.BlockSpec(memory...  15.2 us
    all_to_all x1, blocking collectives, step_sums(): lax.all_to_all(sums, ('lat', 'dep'), split_axis=0, concat_axis=0, tiled=T...  14.6 us
    ppermute x12, waiting for transfers between devices, depth_exchange(): lax.ppermute(parts[s], 'dep', [(i, i ^ s) for i in range(count)])  7.13 us
    ppermute x3, starting transfers between devices, partner_exchange(): lax.ppermute(to_b, 'lat', pairs_b)  4.65 us
    ppermute x2, starting transfers between devices, past_exchange(): lax.ppermute(part_a, 'lat', past_b)  3.5 us
    ppermute x2, starting transfers between devices, past_exchange(): lax.ppermute(part_b, 'lat', past_a)  3.38 us
    all_to_all x1, waiting for transfers between devices, step_sums(): lax.all_to_all(sums, ('lat', 'dep'), split_axis=0, concat_axis=0, tiled=T...  2.99 us
  transfers between devices with their start and end apart: 23, of which 10 were waited for; matrix products, arithmetic and copies ran while one was open for 0% of the time, Pallas kernels for 9%

profile of v4, /device:TPU:0, one launch (start us, length us, event | category | flops | bytes accessed | tf_op | source)
XLA Modules:
  0.0 78.9 jit_solution(8862715062560351329)
XLA Ops:
  0.6 1.6 %shard_map.140 = (f32[6,12,128]{2,1,0:T(8,128)S(1)}, f32[6,12,128]{2,1,0:T(8,128)S(1)}, f32[6,12,128]{2,1,0:T(8,128)S(1)}, f32[16,64,128]{2,1,0:T(8,128)S(1)}, f32[16,64,128]{2,1,0:T(8,128)S(1)}) custom-call(s32[1,12]{1,0:T(1,128)} %bitcast.20, s32[12,3,1,64]{3,2,1,0:T(1,128)} %bitcast.17, s32[12,1,64]{2,1,0:T(1,128)} %bitcast.18, s32[12,1,64]{2,1,0:T(1,128)} %bitcast.19, ...), custom_call_target="tpu_custom_call" | custom-call | bytes 2255920 | tf_op jit(solution)/shard_map/pallas_call | solution.py:60
  2.2 0.5 collective-permute-start
  2.8 3.6 %collective-permute-start.1 = (f32[6,12,128]{2,1,0:T(8,128)S(1)}, f32[6,12,128]{2,1,0:T(8,128)S(1)}, u32[]{:S(2)}, u32[]{:S(2)}) collective-permute-start(f32[6,12,128]{2,1,0:T(8,128)S(1)} %get-tuple-element.45), channel_id=1, source_target_pairs={{0,28},{4,8},{8,4},{12,16},{16,12},{20,24},{24,20},{28,0},{1,29},{... | collective-permute-start | bytes 110600 | tf_op jit(solution)/shard_map/ppermute | solution.py:365
  6.3 0.3 shard_map.141
  6.7 0.0 collective-permute-done.a_ref.refs_4_.refs_1_
  6.7 1.4 %collective-permute-done.1.b_ref.refs_5_.refs_2_ = f32[6,12,128]{2,1,0:T(8,128)S(1)} collective-permute-done((f32[6,12,128]{2,1,0:T(8,128)S(1)}, f32[6,12,128]{2,1,0:T(8,128)S(1)}, u32[]{:S(2)}, u32[]{:S(2)}) %collective-permute-start.1) | collective-permute-done | bytes 36896 | tf_op jit(solution)/shard_map/ppermute | solution.py:365
  8.1 0.1 shard_map.142
  8.2 1.8 %collective-permute-start.2 = (s16[304,128]{1,0:T(8,128)(2,1)S(1)}, s16[304,128]{1,0:T(8,128)(2,1)S(1)}, u32[]{:S(2)}, u32[]{:S(2)}) collective-permute-start(s16[304,128]{1,0:T(8,128)(2,1)S(1)} %get-tuple-element.53), channel_id=1, source_target_pairs={{0,1},{1,0},{2,3},{3,2},{4,5},{5,4},{6,7},{7,6},{8,9},{9,8},{10,11... | collective-permute-start | bytes 233480 | tf_op jit(solution)/shard_map/ppermute | solution.py:357
  10.0 2.6 %collective-permute-start.3 = (s16[304,128]{1,0:T(8,128)(2,1)S(1)}, s16[304,128]{1,0:T(8,128)(2,1)S(1)}, u32[]{:S(2)}, u32[]{:S(2)}) collective-permute-start(s16[304,128]{1,0:T(8,128)(2,1)S(1)} %get-tuple-element.54), channel_id=1, source_target_pairs={{0,2},{1,3},{2,0},{3,1},{4,6},{5,7},{6,4},{7,5},{8,10},{9,11},{10,... | collective-permute-start | bytes 233480 | tf_op jit(solution)/shard_map/ppermute | solution.py:357
  12.6 0.1 collective-permute-start.4
  12.6 0.8 %collective-permute-start.5 = (s16[272,128]{1,0:T(8,128)(2,1)S(1)}, s16[272,128]{1,0:T(8,128)(2,1)S(1)}, u32[]{:S(2)}, u32[]{:S(2)}) collective-permute-start(s16[272,128]{1,0:T(8,128)(2,1)S(1)} %get-tuple-element.57), channel_id=1, source_target_pairs={{0,1},{1,0},{2,3},{3,2},{4,5},{5,4},{6,7},{7,6},{8,9},{9,8},{10,11... | collective-permute-start | bytes 208904 | tf_op jit(solution)/shard_map/ppermute | solution.py:357
  13.5 3.5 %collective-permute-start.6 = (s16[272,128]{1,0:T(8,128)(2,1)S(1)}, s16[272,128]{1,0:T(8,128)(2,1)S(1)}, u32[]{:S(2)}, u32[]{:S(2)}) collective-permute-start(s16[272,128]{1,0:T(8,128)(2,1)S(1)} %get-tuple-element.58), channel_id=1, source_target_pairs={{0,2},{1,3},{2,0},{3,1},{4,6},{5,7},{6,4},{7,5},{8,10},{9,11},{10,... | collective-permute-start | bytes 208904 | tf_op jit(solution)/shard_map/ppermute | solution.py:357
  17.0 0.1 shard_map.143.refs_4_.refs_13_.refs_10_
  17.1 0.0 copy-start.2
  17.1 0.0 copy-start.3
  17.1 0.0 collective-permute-done.2.refs_1_
  17.1 0.1 collective-permute-start.7
  17.3 2.5 %collective-permute-done.3.refs_2_ = s16[304,128]{1,0:T(8,128)(2,1)S(1)} collective-permute-done((s16[304,128]{1,0:T(8,128)(2,1)S(1)}, s16[304,128]{1,0:T(8,128)(2,1)S(1)}, u32[]{:S(2)}, u32[]{:S(2)}) %collective-permute-start.3) | collective-permute-done | bytes 77856 | tf_op jit(solution)/shard_map/ppermute | solution.py:357
  19.8 0.0 collective-permute-done.4.refs_3_
  19.8 2.1 %shard_map.144 = (f32[8,12,128]{2,1,0:T(8,128)S(1)}, f32[8,12,128]{2,1,0:T(8,128)S(1)}, f32[4,12,128]{2,1,0:T(8,128)S(1)}, f32[4,12,128]{2,1,0:T(8,128)S(1)}, bf...) custom-call(s16[304,128]{1,0:T(8,128)(2,1)S(1)} %get-tuple-element.52.anchor_ref.refs_0_, ...), custom_call_target="tpu_custom_call" | custom-call | flops 1006632960 | bytes 3907584 | tf_op jit(solution)/shard_map/pallas_call | solution.py:60
  21.9 1.0 %collective-permute-start.9 = (f32[8,12,128]{2,1,0:T(8,128)S(1)}, f32[8,12,128]{2,1,0:T(8,128)S(1)}, u32[]{:S(2)}, u32[]{:S(2)}) collective-permute-start(f32[8,12,128]{2,1,0:T(8,128)S(1)} %get-tuple-element.62), channel_id=1, source_target_pairs={{0,28},{4,8},{8,4},{12,16},{16,12},{20,24},{24,20},{28,0},{1,29},{... | collective-permute-start | bytes 147464 | tf_op jit(solution)/shard_map/ppermute | solution.py:365
  23.0 0.0 collective-permute-start.8
  23.0 0.0 collective-permute-done.5.refs_0_.refs_5_
  23.0 2.0 %collective-permute-start.11 = (f32[4,12,128]{2,1,0:T(8,128)S(1)}, f32[4,12,128]{2,1,0:T(8,128)S(1)}, u32[]{:S(2)}, u32[]{:S(2)}) collective-permute-start(f32[4,12,128]{2,1,0:T(8,128)S(1)} %get-tuple-element.63), channel_id=1, source_target_pairs={{0,8},{4,28},{8,16},{12,4},{16,24},{20,12},{24,0},{28,20},{1,9},{5... | collective-permute-start | bytes 73736 | tf_op jit(solution)/shard_map/ppermute | solution.py:372
  25.0 0.1 collective-permute-done.6.refs_1_.refs_6_
  25.2 1.9 %collective-permute-start.10 = (f32[4,12,128]{2,1,0:T(8,128)S(1)}, f32[4,12,128]{2,1,0:T(8,128)S(1)}, u32[]{:S(2)}, u32[]{:S(2)}) collective-permute-start(f32[4,12,128]{2,1,0:T(8,128)S(1)} %get-tuple-element.61.refs_7_), channel_id=1, source_target_pairs={{0,24},{4,12},{8,0},{12,20},{16,8},{20,28},{24,16},{28,4},{1,25},{... | collective-permute-start | bytes 73736 | tf_op jit(solution)/shard_map/ppermute | solution.py:372
  27.1 0.5 shard_map.145.refs_12_.refs_9_
  27.6 0.0 copy-start.4
  27.6 0.0 copy-start.1
  27.7 0.0 collective-permute-done.7.refs_2_.refs_7_
  27.7 0.1 collective-permute-done.11.refs_11_
  27.8 1.3 %collective-permute-done.10.refs_10_ = f32[4,12,128]{2,1,0:T(8,128)S(1)} collective-permute-done((f32[4,12,128]{2,1,0:T(8,128)S(1)}, f32[4,12,128]{2,1,0:T(8,128)S(1)}, u32[]{:S(2)}, u32[]{:S(2)}) %collective-permute-start.10) | collective-permute-done | bytes 24608 | tf_op jit(solution)/shard_map/ppermute | solution.py:372
  29.1 0.0 collective-permute-done.9.refs_9_
  29.1 0.0 collective-permute-done.8.refs_8_
  29.1 2.3 %shard_map.146 = (f32[256,512]{1,0:T(8,128)S(1)}, f32[32,128]{1,0:T(8,128)S(1)}) custom-call(s16[272,128]{1,0:T(8,128)(2,1)S(1)} %collective-permute-done.5.refs_0_.refs_5_, s16[272,128]{1,0:T(8,128)(2,1)S(1)} %collective-permute-done.6.refs_1_.refs_6_, s16[272,128]{1,0:T(8,128)(2,1)S(1)} %collective-permute-done.7.refs_2_.refs_7_, ...), custom_call_target="tpu_custom_call" | custom-call | flops 2013265920 | bytes 4280320 | tf_op jit(solution)/shard_map/pallas_call | solution.py:60
  31.4 14.6 %all_to_all.22 = f32[32,1,128]{2,1,0:T(1,128)S(1)} all-to-all(f32[32,1,128]{2,1,0:T(1,128)S(1)} %bitcast.15), channel_id=1, replica_groups=mesh['lat'=8,'dep'=4] {'lat','dep'}, dimensions={0} | all-to-all | bytes 32768 | tf_op jit(solution)/shard_map/all_to_all | solution.py:488
  46.0 0.1 broadcast_in_dim.2.refs_11_.limits_ref
  46.1 2.8 %shard_map.147 = (f32[8,12,128]{2,1,0:T(8,128)S(1)}, f32[8,12,128]{2,1,0:T(8,128)S(1)}, f32[4,12,128]{2,1,0:T(8,128)S(1)}, f32[4,12,128]{2,1,0:T(8,128)S(1)}, f3...) custom-call(s16[304,128]{1,0:T(8,128)(2,1)S(1)} %get-tuple-element.52.anchor_ref.refs_0_, ...), custom_call_target="tpu_custom_call" | custom-call | flops 1006632960 | bytes 5996544 | tf_op jit(solution)/shard_map/pallas_call | solution.py:60
  48.9 0.1 collective-permute-start.16
  49.0 0.7 collective-permute-start.15
  49.7 1.5 %collective-permute-start.18 = (f32[4,12,128]{2,1,0:T(8,128)S(1)}, f32[4,12,128]{2,1,0:T(8,128)S(1)}, u32[]{:S(2)}, u32[]{:S(2)}) collective-permute-start(f32[4,12,128]{2,1,0:T(8,128)S(1)} %get-tuple-element.76), channel_id=1, source_target_pairs={{0,8},{4,28},{8,16},{12,4},{16,24},{20,12},{24,0},{28,20},{1,9},{5... | collective-permute-start | bytes 73736 | tf_op jit(solution)/shard_map/ppermute | solution.py:372
  51.1 1.5 %collective-permute-start.17 = (f32[4,12,128]{2,1,0:T(8,128)S(1)}, f32[4,12,128]{2,1,0:T(8,128)S(1)}, u32[]{:S(2)}, u32[]{:S(2)}) collective-permute-start(f32[4,12,128]{2,1,0:T(8,128)S(1)} %get-tuple-element.74.refs_4_), channel_id=1, source_target_pairs={{0,24},{4,12},{8,0},{12,20},{16,8},{20,28},{24,16},{28,4},{1,25},{... | collective-permute-start | bytes 73736 | tf_op jit(solution)/shard_map/ppermute | solution.py:372
  52.6 0.2 shard_map.148
  52.8 0.5 collective-permute-start.12
  53.4 1.1 %collective-permute-done.18.refs_8_ = f32[4,12,128]{2,1,0:T(8,128)S(1)} collective-permute-done((f32[4,12,128]{2,1,0:T(8,128)S(1)}, f32[4,12,128]{2,1,0:T(8,128)S(1)}, u32[]{:S(2)}, u32[]{:S(2)}) %collective-permute-start.18) | collective-permute-done | bytes 24608 | tf_op jit(solution)/shard_map/ppermute | solution.py:372
  54.5 0.6 collective-permute-done.17.refs_7_
  55.1 0.0 collective-permute-done.16.refs_6_
  55.1 0.0 collective-permute-done.15.refs_5_
  55.1 2.9 %shard_map.149 = (f32[256,512]{1,0:T(8,128)S(1)}, f32[32,128]{1,0:T(8,128)}) custom-call(f32[6,12,128]{2,1,0:T(8,128)S(1)} %get-tuple-element.43.own_ref.refs_3_.refs_0_, f32[6,12,128]{2,1,0:T(8,128)S(1)} %collective-permute-done.a_ref.refs_4_.refs_1_, f32[6,12,128]{2,1,0:T(8,128)S(1)} %collective-permute-done.1.b_ref.refs_5_.refs_2_, ...), custom_call_target="tpu_custom_call" | custom-call | flops 2013265920 | bytes 4280320 | tf_op jit(solution)/shard_map/pallas_call | solution.py:60
  58.0 2.7 %all-to-all-start.1 = ((f32[32,1,128]{2,1,0:T(1,128)}), f32[32,1,128]{2,1,0:T(1,128)S(1)}, u32[]{:S(2)}, u32[]{:S(2)}) async-start(f32[32,1,128]{2,1,0:T(1,128)} %bitcast.9), calls=%async_computation.1 | async-start | bytes 32768 | tf_op jit(solution)/shard_map/all_to_all | solution.py:488
  60.7 2.7 %collective-permute-start.13 = (s16[272,128]{1,0:T(8,128)(2,1)S(1)}, s16[272,128]{1,0:T(8,128)(2,1)S(1)}, u32[]{:S(2)}, u32[]{:S(2)}) collective-permute-start(s16[272,128]{1,0:T(8,128)(2,1)S(1)} %get-tuple-element.71), channel_id=1, source_target_pairs={{0,2},{1,3},{2,0},{3,1},{4,6},{5,7},{6,4},{7,5},{8,10},{9,11},{10,... | collective-permute-start | bytes 208904 | tf_op jit(solution)/shard_map/ppermute | solution.py:357
  63.5 1.5 %collective-permute-start.14 = (s16[272,128]{1,0:T(8,128)(2,1)S(1)}, s16[272,128]{1,0:T(8,128)(2,1)S(1)}, u32[]{:S(2)}, u32[]{:S(2)}) collective-permute-start(s16[272,128]{1,0:T(8,128)(2,1)S(1)} %get-tuple-element.72), channel_id=1, source_target_pairs={{0,3},{1,2},{2,1},{3,0},{4,7},{5,6},{6,5},{7,4},{8,11},{9,10},{10,... | collective-permute-start | bytes 208904 | tf_op jit(solution)/shard_map/ppermute | solution.py:357
  64.9 3.0 %all-to-all-done.1 = f32[32,1,128]{2,1,0:T(1,128)S(1)} async-done(((f32[32,1,128]{2,1,0:T(1,128)}), f32[32,1,128]{2,1,0:T(1,128)S(1)}, u32[]{:S(2)}, u32[]{:S(2)}) %all-to-all-start.1) | async-done | bytes 16416 | tf_op jit(solution)/shard_map/all_to_all | solution.py:488
  67.9 0.9 %shard_map.150 = (s16[272,128]{1,0:T(8,128)(2,1)S(1)}, s16[272,128]{1,0:T(8,128)(2,1)S(1)}, s16[272,128]{1,0:T(8,128)(2,1)S(1)}, s16[272,128]{1,0:T(8,128)(2,1)S(1)}) custom-call(f32[32,128]{1,0:T(8,128)S(1)} %bitcast.14, f32[256,512]{1,0:T(8,128)S(1)} %get-tuple-element.78.current_ref, f32[256,512]{1,0:T(8,128)S(1)} %get-tuple-element.79.grad_ref, ...), custom_call_target="tpu_custom_call" | custom-call | bytes 1605632 | tf_op jit(solution)/shard_map/pallas_call | solution.py:60
  68.9 0.5 collective-permute-start.19
  69.3 0.6 collective-permute-start.20
  70.0 0.0 collective-permute-done.12.refs_1_
  70.0 3.4 %collective-permute-start.21 = (s16[272,128]{1,0:T(8,128)(2,1)S(1)}, s16[272,128]{1,0:T(8,128)(2,1)S(1)}, u32[]{:S(2)}, u32[]{:S(2)}) collective-permute-start(s16[272,128]{1,0:T(8,128)(2,1)S(1)} %get-tuple-element.83), channel_id=1, source_target_pairs={{0,3},{1,2},{2,1},{3,0},{4,7},{5,6},{6,5},{7,4},{8,11},{9,10},{10,... | collective-permute-start | bytes 208904 | tf_op jit(solution)/shard_map/ppermute | solution.py:357
  73.3 0.0 collective-permute-done.13.refs_2_
  73.3 0.0 collective-permute-done.14.refs_3_
  73.3 0.7 collective-permute-done.19.refs_5_
  74.0 3.8 %collective-permute-done.20.refs_6_ = s16[272,128]{1,0:T(8,128)(2,1)S(1)} collective-permute-done((s16[272,128]{1,0:T(8,128)(2,1)S(1)}, s16[272,128]{1,0:T(8,128)(2,1)S(1)}, u32[]{:S(2)}, u32[]{:S(2)}) %collective-permute-start.20) | collective-permute-done | bytes 69664 | tf_op jit(solution)/shard_map/ppermute | solution.py:357
  77.7 0.0 collective-permute-done.21.refs_7_
  77.7 1.2 %shard_map.151 = (f32[16,64,128]{2,1,0:T(8,128)}, f32[16,64,128]{2,1,0:T(8,128)}) custom-call(s16[272,128]{1,0:T(8,128)(2,1)S(1)} %get-tuple-element.69.refs_0_, s16[272,128]{1,0:T(8,128)(2,1)S(1)} %collective-permute-done.12.refs_1_, s16[272,128]{1,0:T(8,128)(2,1)S(1)} %collective-permute-done.13.refs_2_, ...), custom_call_target="tpu_custom_call" | custom-call | bytes 1605632 | tf_op jit(solution)/shard_map/pallas_call | solution.py:60
  (6 shorter events, 0.0 us)
Async XLA Ops:
  0.6 16.3 %copy-start = (bf16[64,128,128]{2,1,0:T(8,128)(2,1)S(1)}, bf16[64,128,128]{2,1,0:T(8,128)(2,1)}, u32[]{:S(2)}) copy-start(bf16[64,128,128]{2,1,0:T(8,128)(2,1)} %table_ref.1) | copy-start | bytes 6291460
  2.2 4.4 %collective-permute-start = (f32[6,12,128]{2,1,0:T(8,128)S(1)}, f32[6,12,128]{2,1,0:T(8,128)S(1)}, u32[]{:S(2)}, u32[]{:S(2)}) collective-permute-start(f32[6,12,128]{2,1,0:T(8,128)S(1)} %get-tuple-element.44), channel_id=1, source_target_pairs={{0,4},{4,0},{8,12},{12,8},{16,20},{20,16},{24,28},{28,24},{1,5},{5... | collective-permute-start | bytes 110600 | tf_op jit(solution)/shard_map/ppermute | solution.py:365
  2.8 5.3 %collective-permute-start.1 = (f32[6,12,128]{2,1,0:T(8,128)S(1)}, f32[6,12,128]{2,1,0:T(8,128)S(1)}, u32[]{:S(2)}, u32[]{:S(2)}) collective-permute-start(f32[6,12,128]{2,1,0:T(8,128)S(1)} %get-tuple-element.45), channel_id=1, source_target_pairs={{0,28},{4,8},{8,4},{12,16},{16,12},{20,24},{24,20},{28,0},{1,29},{... | collective-permute-start | bytes 110600 | tf_op jit(solution)/shard_map/ppermute | solution.py:365
  8.2 8.9 %collective-permute-start.2 = (s16[304,128]{1,0:T(8,128)(2,1)S(1)}, s16[304,128]{1,0:T(8,128)(2,1)S(1)}, u32[]{:S(2)}, u32[]{:S(2)}) collective-permute-start(s16[304,128]{1,0:T(8,128)(2,1)S(1)} %get-tuple-element.53), channel_id=1, source_target_pairs={{0,1},{1,0},{2,3},{3,2},{4,5},{5,4},{6,7},{7,6},{8,9},{9,8},{10,11... | collective-permute-start | bytes 233480 | tf_op jit(solution)/shard_map/ppermute | solution.py:357
  10.0 9.8 %collective-permute-start.3 = (s16[304,128]{1,0:T(8,128)(2,1)S(1)}, s16[304,128]{1,0:T(8,128)(2,1)S(1)}, u32[]{:S(2)}, u32[]{:S(2)}) collective-permute-start(s16[304,128]{1,0:T(8,128)(2,1)S(1)} %get-tuple-element.54), channel_id=1, source_target_pairs={{0,2},{1,3},{2,0},{3,1},{4,6},{5,7},{6,4},{7,5},{8,10},{9,11},{10,... | collective-permute-start | bytes 233480 | tf_op jit(solution)/shard_map/ppermute | solution.py:357
  12.6 7.2 %collective-permute-start.4 = (s16[304,128]{1,0:T(8,128)(2,1)S(1)}, s16[304,128]{1,0:T(8,128)(2,1)S(1)}, u32[]{:S(2)}, u32[]{:S(2)}) collective-permute-start(s16[304,128]{1,0:T(8,128)(2,1)S(1)} %get-tuple-element.55), channel_id=1, source_target_pairs={{0,3},{1,2},{2,1},{3,0},{4,7},{5,6},{6,5},{7,4},{8,11},{9,10},{10,... | collective-permute-start | bytes 233480 | tf_op jit(solution)/shard_map/ppermute | solution.py:357
  12.6 10.3 %collective-permute-start.5 = (s16[272,128]{1,0:T(8,128)(2,1)S(1)}, s16[272,128]{1,0:T(8,128)(2,1)S(1)}, u32[]{:S(2)}, u32[]{:S(2)}) collective-permute-start(s16[272,128]{1,0:T(8,128)(2,1)S(1)} %get-tuple-element.57), channel_id=1, source_target_pairs={{0,1},{1,0},{2,3},{3,2},{4,5},{5,4},{6,7},{7,6},{8,9},{9,8},{10,11... | collective-permute-start | bytes 208904 | tf_op jit(solution)/shard_map/ppermute | solution.py:357
  13.5 11.7 %collective-permute-start.6 = (s16[272,128]{1,0:T(8,128)(2,1)S(1)}, s16[272,128]{1,0:T(8,128)(2,1)S(1)}, u32[]{:S(2)}, u32[]{:S(2)}) collective-permute-start(s16[272,128]{1,0:T(8,128)(2,1)S(1)} %get-tuple-element.58), channel_id=1, source_target_pairs={{0,2},{1,3},{2,0},{3,1},{4,6},{5,7},{6,4},{7,5},{8,10},{9,11},{10,... | collective-permute-start | bytes 208904 | tf_op jit(solution)/shard_map/ppermute | solution.py:357
  17.1 10.0 %copy-start.2 = (bf16[40,2560]{1,0:T(8,128)(2,1)S(1)}, bf16[40,2560]{1,0:T(8,128)(2,1)}, u32[]{:S(2)}) copy-start(bf16[40,2560]{1,0:T(8,128)(2,1)} %constant.7.clone.spread_ref) | copy-start | bytes 614404
  17.1 10.0 %copy-start.3 = (f32[8,2560]{1,0:T(8,128)S(1)}, f32[8,2560]{1,0:T(8,128)}, u32[]{:S(2)}) copy-start(f32[8,2560]{1,0:T(8,128)} %constant.8.clone.number_ref) | copy-start | bytes 245764
  17.1 10.5 %collective-permute-start.7 = (s16[272,128]{1,0:T(8,128)(2,1)S(1)}, s16[272,128]{1,0:T(8,128)(2,1)S(1)}, u32[]{:S(2)}, u32[]{:S(2)}) collective-permute-start(s16[272,128]{1,0:T(8,128)(2,1)S(1)} %get-tuple-element.59), channel_id=1, source_target_pairs={{0,3},{1,2},{2,1},{3,0},{4,7},{5,6},{6,5},{7,4},{8,11},{9,10},{10,... | collective-permute-start | bytes 208904 | tf_op jit(solution)/shard_map/ppermute | solution.py:357
  21.9 7.1 %collective-permute-start.9 = (f32[8,12,128]{2,1,0:T(8,128)S(1)}, f32[8,12,128]{2,1,0:T(8,128)S(1)}, u32[]{:S(2)}, u32[]{:S(2)}) collective-permute-start(f32[8,12,128]{2,1,0:T(8,128)S(1)} %get-tuple-element.62), channel_id=1, source_target_pairs={{0,28},{4,8},{8,4},{12,16},{16,12},{20,24},{24,20},{28,0},{1,29},{... | collective-permute-start | bytes 147464 | tf_op jit(solution)/shard_map/ppermute | solution.py:365
  23.0 6.1 %collective-permute-start.8 = (f32[8,12,128]{2,1,0:T(8,128)S(1)}, f32[8,12,128]{2,1,0:T(8,128)S(1)}, u32[]{:S(2)}, u32[]{:S(2)}) collective-permute-start(f32[8,12,128]{2,1,0:T(8,128)S(1)} %get-tuple-element.60.refs_6_), channel_id=1, source_target_pairs={{0,4},{4,0},{8,12},{12,8},{16,20},{20,16},{24,28},{28,24},{1,5},{5... | collective-permute-start | bytes 147464 | tf_op jit(solution)/shard_map/ppermute | solution.py:365
  23.0 4.8 %collective-permute-start.11 = (f32[4,12,128]{2,1,0:T(8,128)S(1)}, f32[4,12,128]{2,1,0:T(8,128)S(1)}, u32[]{:S(2)}, u32[]{:S(2)}) collective-permute-start(f32[4,12,128]{2,1,0:T(8,128)S(1)} %get-tuple-element.63), channel_id=1, source_target_pairs={{0,8},{4,28},{8,16},{12,4},{16,24},{20,12},{24,0},{28,20},{1,9},{5... | collective-permute-start | bytes 73736 | tf_op jit(solution)/shard_map/ppermute | solution.py:372
  25.2 3.9 %collective-permute-start.10 = (f32[4,12,128]{2,1,0:T(8,128)S(1)}, f32[4,12,128]{2,1,0:T(8,128)S(1)}, u32[]{:S(2)}, u32[]{:S(2)}) collective-permute-start(f32[4,12,128]{2,1,0:T(8,128)S(1)} %get-tuple-element.61.refs_7_), channel_id=1, source_target_pairs={{0,24},{4,12},{8,0},{12,20},{16,8},{20,28},{24,16},{28,4},{1,25},{... | collective-permute-start | bytes 73736 | tf_op jit(solution)/shard_map/ppermute | solution.py:372
  27.6 18.4 %copy-start.4 = (f32[256]{0:T(256)S(1)}, f32[256]{0:T(256)}, u32[]{:S(2)}) copy-start(f32[256]{0:T(256)} %param.22) | copy-start | bytes 3076
  27.6 18.5 %copy-start.1 = (bf16[256,256]{1,0:T(8,128)(2,1)S(1)}, bf16[256,256]{1,0:T(8,128)(2,1)}, u32[]{:S(2)}) copy-start(bf16[256,256]{1,0:T(8,128)(2,1)} %constant.6.clone.refs_10_.had_ref) | copy-start | bytes 393220
  48.9 6.1 %collective-permute-start.16 = (f32[8,12,128]{2,1,0:T(8,128)S(1)}, f32[8,12,128]{2,1,0:T(8,128)S(1)}, u32[]{:S(2)}, u32[]{:S(2)}) collective-permute-start(f32[8,12,128]{2,1,0:T(8,128)S(1)} %get-tuple-element.75), channel_id=1, source_target_pairs={{0,28},{4,8},{8,4},{12,16},{16,12},{20,24},{24,20},{28,0},{1,29},{... | collective-permute-start | bytes 147464 | tf_op jit(solution)/shard_map/ppermute | solution.py:365
  49.0 6.1 %collective-permute-start.15 = (f32[8,12,128]{2,1,0:T(8,128)S(1)}, f32[8,12,128]{2,1,0:T(8,128)S(1)}, u32[]{:S(2)}, u32[]{:S(2)}) collective-permute-start(f32[8,12,128]{2,1,0:T(8,128)S(1)} %get-tuple-element.73.refs_3_), channel_id=1, source_target_pairs={{0,4},{4,0},{8,12},{12,8},{16,20},{20,16},{24,28},{28,24},{1,5},{5... | collective-permute-start | bytes 147464 | tf_op jit(solution)/shard_map/ppermute | solution.py:365
  49.7 4.8 %collective-permute-start.18 = (f32[4,12,128]{2,1,0:T(8,128)S(1)}, f32[4,12,128]{2,1,0:T(8,128)S(1)}, u32[]{:S(2)}, u32[]{:S(2)}) collective-permute-start(f32[4,12,128]{2,1,0:T(8,128)S(1)} %get-tuple-element.76), channel_id=1, source_target_pairs={{0,8},{4,28},{8,16},{12,4},{16,24},{20,12},{24,0},{28,20},{1,9},{5... | collective-permute-start | bytes 73736 | tf_op jit(solution)/shard_map/ppermute | solution.py:372
  51.1 3.9 %collective-permute-start.17 = (f32[4,12,128]{2,1,0:T(8,128)S(1)}, f32[4,12,128]{2,1,0:T(8,128)S(1)}, u32[]{:S(2)}, u32[]{:S(2)}) collective-permute-start(f32[4,12,128]{2,1,0:T(8,128)S(1)} %get-tuple-element.74.refs_4_), channel_id=1, source_target_pairs={{0,24},{4,12},{8,0},{12,20},{16,8},{20,28},{24,16},{28,4},{1,25},{... | collective-permute-start | bytes 73736 | tf_op jit(solution)/shard_map/ppermute | solution.py:372
  52.8 17.1 %collective-permute-start.12 = (s16[272,128]{1,0:T(8,128)(2,1)S(1)}, s16[272,128]{1,0:T(8,128)(2,1)S(1)}, u32[]{:S(2)}, u32[]{:S(2)}) collective-permute-start(s16[272,128]{1,0:T(8,128)(2,1)S(1)} %get-tuple-element.70), channel_id=1, source_target_pairs={{0,1},{1,0},{2,3},{3,2},{4,5},{5,4},{6,7},{7,6},{8,9},{9,8},{10,11... | collective-permute-start | bytes 208904 | tf_op jit(solution)/shard_map/ppermute | solution.py:357
  58.0 9.9 %all-to-all-start.1 = ((f32[32,1,128]{2,1,0:T(1,128)}), f32[32,1,128]{2,1,0:T(1,128)S(1)}, u32[]{:S(2)}, u32[]{:S(2)}) async-start(f32[32,1,128]{2,1,0:T(1,128)} %bitcast.9), calls=%async_computation.1 | async-start | bytes 32768 | tf_op jit(solution)/shard_map/all_to_all | solution.py:488
  60.7 12.6 %collective-permute-start.13 = (s16[272,128]{1,0:T(8,128)(2,1)S(1)}, s16[272,128]{1,0:T(8,128)(2,1)S(1)}, u32[]{:S(2)}, u32[]{:S(2)}) collective-permute-start(s16[272,128]{1,0:T(8,128)(2,1)S(1)} %get-tuple-element.71), channel_id=1, source_target_pairs={{0,2},{1,3},{2,0},{3,1},{4,6},{5,7},{6,4},{7,5},{8,10},{9,11},{10,... | collective-permute-start | bytes 208904 | tf_op jit(solution)/shard_map/ppermute | solution.py:357
  63.5 9.9 %collective-permute-start.14 = (s16[272,128]{1,0:T(8,128)(2,1)S(1)}, s16[272,128]{1,0:T(8,128)(2,1)S(1)}, u32[]{:S(2)}, u32[]{:S(2)}) collective-permute-start(s16[272,128]{1,0:T(8,128)(2,1)S(1)} %get-tuple-element.72), channel_id=1, source_target_pairs={{0,3},{1,2},{2,1},{3,0},{4,7},{5,6},{6,5},{7,4},{8,11},{9,10},{10,... | collective-permute-start | bytes 208904 | tf_op jit(solution)/shard_map/ppermute | solution.py:357
  68.9 5.1 %collective-permute-start.19 = (s16[272,128]{1,0:T(8,128)(2,1)S(1)}, s16[272,128]{1,0:T(8,128)(2,1)S(1)}, u32[]{:S(2)}, u32[]{:S(2)}) collective-permute-start(s16[272,128]{1,0:T(8,128)(2,1)S(1)} %get-tuple-element.81), channel_id=1, source_target_pairs={{0,1},{1,0},{2,3},{3,2},{4,5},{5,4},{6,7},{7,6},{8,9},{9,8},{10,11... | collective-permute-start | bytes 208904 | tf_op jit(solution)/shard_map/ppermute | solution.py:357
  69.3 8.4 %collective-permute-start.20 = (s16[272,128]{1,0:T(8,128)(2,1)S(1)}, s16[272,128]{1,0:T(8,128)(2,1)S(1)}, u32[]{:S(2)}, u32[]{:S(2)}) collective-permute-start(s16[272,128]{1,0:T(8,128)(2,1)S(1)} %get-tuple-element.82), channel_id=1, source_target_pairs={{0,2},{1,3},{2,0},{3,1},{4,6},{5,7},{6,4},{7,5},{8,10},{9,11},{10,... | collective-permute-start | bytes 208904 | tf_op jit(solution)/shard_map/ppermute | solution.py:357
  70.0 7.8 %collective-permute-start.21 = (s16[272,128]{1,0:T(8,128)(2,1)S(1)}, s16[272,128]{1,0:T(8,128)(2,1)S(1)}, u32[]{:S(2)}, u32[]{:S(2)}) collective-permute-start(s16[272,128]{1,0:T(8,128)(2,1)S(1)} %get-tuple-element.83), channel_id=1, source_target_pairs={{0,3},{1,2},{2,1},{3,0},{4,7},{5,6},{6,5},{7,4},{8,11},{9,10},{10,... | collective-permute-start | bytes 208904 | tf_op jit(solution)/shard_map/ppermute | solution.py:357

commit v5 on v4

--- a/solution.py
+++ b/solution.py
@@ -137,7 +137,8 @@
         group = pl.ds((me ^ slot) * rows, rows)
         est = est_ref[group]
         encode(refs[slot], est + momentum * (est - prev_ref[group]))
-        encode(refs[count + slot], est)
+        if slot < len(refs) - count:
+            encode(refs[count + slot], est)
 
 
 def pack_ids(ids, height):
@@ -153,6 +154,12 @@
         half = ids.shape[1] // 2
         ids = jnp.concatenate([ids[:, :half], ids[:, half:]], axis=0)
     return ids[:block, :depth]
+
+
+def estimate_kernel(early, count, rows, anchor_ref, est_ref, *refs):
+    me = lax.axis_index("dep")
+    for slot in range(early, count):
+        encode(refs[slot - early], est_ref[pl.ds((me ^ slot) * rows, rows)])
 
 
 def fill_kernel(count, rows, frames, own_ref, a_ref, b_ref, *refs):
@@ -171,6 +178,10 @@
 
 def table_kernel(anchor_ref, table_ref, out_ref):
     out_ref[...] = table_ref[...]
+
+
+def pass_kernel(*refs):
+    refs[-1][...] = refs[-2][...]
 
 
 def state_kernel(rows, tile, fresh_ref, *refs):
@@ -426,8 +437,9 @@
 
     fold = 2 if 2 * depth_local <= tile else 1
     more = -(-block // (16 * fold)) * 16
+    early = max(1, count - 1)
     prepared = call(
-        functools.partial(prepare_kernel, count, rows, momenta[0]), [coded] * (2 * count), [near_estimate, near_previous]
+        functools.partial(prepare_kernel, count, rows, momenta[0]), [coded] * (count + early), [near_estimate, near_previous]
     )
     currents = call(
         functools.partial(fill_kernel, count, rows, frames),
@@ -442,7 +454,6 @@
         anchors=currents[:1],
     )
     currents = depth_exchange(currents)
-    states = depth_exchange(prepared[count : 2 * count])
     lanes = np.arange(prints * block)
     spread = jnp.asarray(lanes[None] % block == np.arange(block)[:, None], bf16)
     number = jnp.asarray(np.broadcast_to(lanes // block, (8, prints * block)), f32)
@@ -463,8 +474,11 @@
         [spread, number, ids],
     )
 
-    def step_sums(parts, hidden):
-        to_a, to_b, part_a, part_b = parts
+    def exchange_parts(parts):
+        return [*partner_exchange(*parts[:2]), *past_exchange(*parts[2:])]
+
+    def step_sums(parts, received, hidden, late):
+        to_a, part_b = parts[0], parts[3]
         gradient, sums = call(
             functools.partial(back_kernel, len(hidden), *sizes),
             [shape((depth, width), f32), shape((count * lat_count, tile), f32)],
@@ -472,8 +486,7 @@
                 *packs,
                 to_a,
                 part_b,
-                *partner_exchange(to_a, to_b),
-                *past_exchange(part_a, part_b),
+                *received,
                 choose_t,
                 table,
             ],
@@ -485,9 +498,19 @@
             flops=2 * work,
             anchors=hidden,
         )
+        if late:
+            (sums,) = call(pass_kernel, [shape(sums.shape, f32)], [sums], anchors=late)
         return gradient, lax.all_to_all(sums, ("lat", "dep"), split_axis=0, concat_axis=0, tiled=True)
 
-    gradient, sums = step_sums(parts, states[1:])
+    received = exchange_parts(parts)
+    later = call(
+        functools.partial(estimate_kernel, early, count, rows),
+        [coded] * (count - early),
+        [near_estimate],
+        anchors=[received[0]],
+    )
+    states = depth_exchange([*prepared[count:], *later])
+    gradient, sums = step_sums(parts, received, list(states[1:early]), states[early:])
     done = call(
         functools.partial(first_kernel, count, *sizes, depth_local, scale, momenta[1]),
         [double, double, part, part] + [shape((depth, width), f32)] * 2,
@@ -499,7 +522,7 @@
     states = depth_exchange(
         call(functools.partial(state_kernel, rows, tile), [coded] * count, [done[5]])
     )
-    gradient, sums = step_sums(parts, [])
+    gradient, sums = step_sums(parts, exchange_parts(parts), [], [])
     fresh = depth_exchange(
         call(
             functools.partial(last_kernel, count, rows, scale),

time: 79.1 us -> 78.1 us (0.987)
  blocking collectives: 14.6 us -> 8.85 us
  waiting for transfers between devices: 14.7 us -> 19.2 us
    ppermute x12, waiting for transfers between devices: 7.13 us -> 13.1 us  [depth_exchange(): lax.ppermute(parts[s], 'dep', [(i, i ^ s) for i in range(count)])]
    all_to_all x1, blocking collectives: 14.6 us -> 8.85 us  [step_sums(): lax.all_to_all(sums, ('lat', 'dep'), split_axis=0, concat_axis=0, tiled=T...]
    ppermute x2, starting transfers between devices: 3.5 us -> 1.48 us  [past_exchange(): lax.ppermute(part_a, 'lat', past_b)]
    ppermute x2, waiting for transfers between devices: 1.85 us -> 0.58 us  [past_exchange(): lax.ppermute(part_b, 'lat', past_a)]
    ppermute x2, starting transfers between devices: 3.38 us -> 4.37 us  [past_exchange(): lax.ppermute(part_b, 'lat', past_a)]
    ppermute x3, starting transfers between devices: 4.65 us -> 5.52 us  [partner_exchange(): lax.ppermute(to_b, 'lat', pairs_b)]
    pallas_call x12 -> x14, Pallas kernels: 15.2 us -> 15.3 us  [call(): pl.pallas_call(body, out_shape=tuple(outs), in_specs=[pl.BlockSpec(memory...]
  transfers between devices with their start and end apart: 23 -> 23, of which waited for: 10 -> 8; matrix products, arithmetic and copies ran while one was open for 0% -> 0% of each run, Pallas kernels for 9% -> 10%
where the time goes in v5:
time: 78.1 us; the launch traced here: 77.9 us
  starting transfers between devices  33.6 us (43%)
  waiting for transfers between devices  19.2 us (25%)
  Pallas kernels  15.3 us (20%)
  blocking collectives  8.85 us (11%)
  between operations  0.82 us (1%)
    ppermute x12, starting transfers between devices, depth_exchange(): lax.ppermute(parts[s], 'dep', [(i, i ^ s) for i in range(count)])  18.3 us
    pallas_call x14, Pallas kernels, call(): pl.pallas_call(body, out_shape=tuple(outs), in_specs=[pl.BlockSpec(memory...  15.3 us
    ppermute x12, waiting for transfers between devices, depth_exchange(): lax.ppermute(parts[s], 'dep', [(i, i ^ s) for i in range(count)])  13.1 us
    all_to_all x1, blocking collectives, step_sums(): lax.all_to_all(sums, ('lat', 'dep'), split_axis=0, concat_axis=0, tiled=T...  8.85 us
    ppermute x3, starting transfers between devices, partner_exchange(): lax.ppermute(to_b, 'lat', pairs_b)  5.52 us
    ppermute x2, starting transfers between devices, past_exchange(): lax.ppermute(part_b, 'lat', past_a)  4.37 us
    all_to_all x1, waiting for transfers between devices, step_sums(): lax.all_to_all(sums, ('lat', 'dep'), split_axis=0, concat_axis=0, tiled=T...  2.99 us
    all_to_all x1, starting transfers between devices, step_sums(): lax.all_to_all(sums, ('lat', 'dep'), split_axis=0, concat_axis=0, tiled=T...  2.71 us
  transfers between devices with their start and end apart: 23, of which 8 were waited for; matrix products, arithmetic and copies ran while one was open for 0% of the time, Pallas kernels for 10%

profile of v5, /device:TPU:0, one launch (start us, length us, event | category | flops | bytes accessed | tf_op | source)
XLA Modules:
  0.0 77.9 jit_solution(4700669350121627608)
XLA Ops:
  0.6 1.6 %shard_map.140 = (f32[6,12,128]{2,1,0:T(8,128)S(1)}, f32[6,12,128]{2,1,0:T(8,128)S(1)}, f32[6,12,128]{2,1,0:T(8,128)S(1)}, f32[16,64,128]{2,1,0:T(8,128)S(1)}, f32[16,64,128]{2,1,0:T(8,128)S(1)}) custom-call(s32[1,12]{1,0:T(1,128)} %bitcast.20, s32[12,3,1,64]{3,2,1,0:T(1,128)} %bitcast.17, s32[12,1,64]{2,1,0:T(1,128)} %bitcast.18, s32[12,1,64]{2,1,0:T(1,128)} %bitcast.19, ...), custom_call_target="tpu_custom_call" | custom-call | bytes 2255920 | tf_op jit(solution)/shard_map/pallas_call | solution.py:60
  2.2 0.5 collective-permute-start
  2.8 3.6 %collective-permute-start.1 = (f32[6,12,128]{2,1,0:T(8,128)S(1)}, f32[6,12,128]{2,1,0:T(8,128)S(1)}, u32[]{:S(2)}, u32[]{:S(2)}) collective-permute-start(f32[6,12,128]{2,1,0:T(8,128)S(1)} %get-tuple-element.44), channel_id=1, source_target_pairs={{0,28},{4,8},{8,4},{12,16},{16,12},{20,24},{24,20},{28,0},{1,29},{... | collective-permute-start | bytes 110600 | tf_op jit(solution)/shard_map/ppermute | solution.py:376
  6.3 0.3 shard_map.141
  6.6 0.0 collective-permute-done.a_ref.refs_3_.refs_1_
  6.7 1.4 %collective-permute-done.1.b_ref.refs_4_.refs_2_ = f32[6,12,128]{2,1,0:T(8,128)S(1)} collective-permute-done((f32[6,12,128]{2,1,0:T(8,128)S(1)}, f32[6,12,128]{2,1,0:T(8,128)S(1)}, u32[]{:S(2)}, u32[]{:S(2)}) %collective-permute-start.1) | collective-permute-done | bytes 36896 | tf_op jit(solution)/shard_map/ppermute | solution.py:376
  8.1 0.1 shard_map.142
  8.2 1.8 %collective-permute-start.2 = (s16[304,128]{1,0:T(8,128)(2,1)S(1)}, s16[304,128]{1,0:T(8,128)(2,1)S(1)}, u32[]{:S(2)}, u32[]{:S(2)}) collective-permute-start(s16[304,128]{1,0:T(8,128)(2,1)S(1)} %get-tuple-element.52), channel_id=1, source_target_pairs={{0,1},{1,0},{2,3},{3,2},{4,5},{5,4},{6,7},{7,6},{8,9},{9,8},{10,11... | collective-permute-start | bytes 233480 | tf_op jit(solution)/shard_map/ppermute | solution.py:368
  10.0 2.6 %collective-permute-start.3 = (s16[304,128]{1,0:T(8,128)(2,1)S(1)}, s16[304,128]{1,0:T(8,128)(2,1)S(1)}, u32[]{:S(2)}, u32[]{:S(2)}) collective-permute-start(s16[304,128]{1,0:T(8,128)(2,1)S(1)} %get-tuple-element.53), channel_id=1, source_target_pairs={{0,2},{1,3},{2,0},{3,1},{4,6},{5,7},{6,4},{7,5},{8,10},{9,11},{10,... | collective-permute-start | bytes 233480 | tf_op jit(solution)/shard_map/ppermute | solution.py:368
  12.6 0.1 collective-permute-start.4
  12.6 0.1 shard_map.143.refs_4_.refs_12_.refs_13_.refs_10_
  12.8 0.0 copy-start.2
  12.8 0.0 copy-start.3
  12.8 0.0 collective-permute-done.2.refs_1_
  12.8 6.3 %collective-permute-done.3.refs_2_ = s16[304,128]{1,0:T(8,128)(2,1)S(1)} collective-permute-done((s16[304,128]{1,0:T(8,128)(2,1)S(1)}, s16[304,128]{1,0:T(8,128)(2,1)S(1)}, u32[]{:S(2)}, u32[]{:S(2)}) %collective-permute-start.3) | collective-permute-done | bytes 77856 | tf_op jit(solution)/shard_map/ppermute | solution.py:368
  19.1 0.0 collective-permute-done.4.refs_3_
  19.1 2.1 %shard_map.144 = (f32[8,12,128]{2,1,0:T(8,128)S(1)}, f32[8,12,128]{2,1,0:T(8,128)S(1)}, f32[4,12,128]{2,1,0:T(8,128)S(1)}, f32[4,12,128]{2,1,0:T(8,128)S(1)}, bf...) custom-call(s16[304,128]{1,0:T(8,128)(2,1)S(1)} %get-tuple-element.51.anchor_ref.refs_0_, ...), custom_call_target="tpu_custom_call" | custom-call | flops 1006632960 | bytes 3907584 | tf_op jit(solution)/shard_map/pallas_call | solution.py:60
  21.2 0.1 collective-permute-start.7
  21.3 1.5 %collective-permute-start.5 = (s16[272,128]{1,0:T(8,128)(2,1)S(1)}, s16[272,128]{1,0:T(8,128)(2,1)S(1)}, u32[]{:S(2)}, u32[]{:S(2)}) collective-permute-start(s16[272,128]{1,0:T(8,128)(2,1)S(1)} %get-tuple-element.56), channel_id=1, source_target_pairs={{0,1},{1,0},{2,3},{3,2},{4,5},{5,4},{6,7},{7,6},{8,9},{9,8},{10,11... | collective-permute-start | bytes 208904 | tf_op jit(solution)/shard_map/ppermute | solution.py:368
  22.8 1.6 %collective-permute-start.6 = (s16[272,128]{1,0:T(8,128)(2,1)S(1)}, s16[272,128]{1,0:T(8,128)(2,1)S(1)}, u32[]{:S(2)}, u32[]{:S(2)}) collective-permute-start(s16[272,128]{1,0:T(8,128)(2,1)S(1)} %get-tuple-element.57), channel_id=1, source_target_pairs={{0,2},{1,3},{2,0},{3,1},{4,6},{5,7},{6,4},{7,5},{8,10},{9,11},{10,... | collective-permute-start | bytes 208904 | tf_op jit(solution)/shard_map/ppermute | solution.py:368
  24.3 1.9 %collective-permute-start.9 = (f32[8,12,128]{2,1,0:T(8,128)S(1)}, f32[8,12,128]{2,1,0:T(8,128)S(1)}, u32[]{:S(2)}, u32[]{:S(2)}) collective-permute-start(f32[8,12,128]{2,1,0:T(8,128)S(1)} %get-tuple-element.60), channel_id=1, source_target_pairs={{0,28},{4,8},{8,4},{12,16},{16,12},{20,24},{24,20},{28,0},{1,29},{... | collective-permute-start | bytes 147464 | tf_op jit(solution)/shard_map/ppermute | solution.py:376
  26.2 0.0 collective-permute-start.11
  26.2 0.0 collective-permute-done.7.anchor_ref.refs_7_
  26.2 2.9 %collective-permute-start.10 = (f32[4,12,128]{2,1,0:T(8,128)S(1)}, f32[4,12,128]{2,1,0:T(8,128)S(1)}, u32[]{:S(2)}, u32[]{:S(2)}) collective-permute-start(f32[4,12,128]{2,1,0:T(8,128)S(1)} %get-tuple-element.59.refs_6_), channel_id=1, source_target_pairs={{0,24},{4,12},{8,0},{12,20},{16,8},{20,28},{24,16},{28,4},{1,25},{... | collective-permute-start | bytes 73736 | tf_op jit(solution)/shard_map/ppermute | solution.py:383
  29.2 0.5 shard_map.146.refs_11_.refs_9_
  29.7 0.1 shard_map.145
  29.9 0.0 copy-start.4
  29.9 0.0 copy-start.1
  29.9 0.0 collective-permute-done.5.refs_0_.refs_5_
  29.9 1.6 %collective-permute-start.8 = (s16[272,128]{1,0:T(8,128)(2,1)S(1)}, s16[272,128]{1,0:T(8,128)(2,1)S(1)}, u32[]{:S(2)}, u32[]{:S(2)}) collective-permute-start(s16[272,128]{1,0:T(8,128)(2,1)S(1)} %shard_map.145), channel_id=1, source_target_pairs={{0,3},{1,2},{2,1},{3,0},{4,7},{5,6},{6,5},{7,4},{8,11},{9,10},{10,... | collective-permute-start | bytes 208904 | tf_op jit(solution)/shard_map/ppermute | solution.py:368
  31.5 0.0 collective-permute-done.6.refs_1_.refs_6_
  31.5 0.0 collective-permute-done.11.refs_10_
  31.5 0.0 collective-permute-done.10.refs_9_
  31.5 0.0 collective-permute-done.9.refs_8_
  31.5 2.3 %shard_map.147 = (f32[256,512]{1,0:T(8,128)S(1)}, f32[32,128]{1,0:T(8,128)S(1)}) custom-call(s16[272,128]{1,0:T(8,128)(2,1)S(1)} %collective-permute-done.5.refs_0_.refs_5_, s16[272,128]{1,0:T(8,128)(2,1)S(1)} %collective-permute-done.6.refs_1_.refs_6_, f32[6,12,128]{2,1,0:T(8,128)S(1)} %get-tuple-element.42.own_ref.refs_2_.refs_0_, ...), custom_call_target="tpu_custom_call" | custom-call | flops 2013265920 | bytes 4280320 | tf_op jit(solution)/shard_map/pallas_call | solution.py:60
  33.8 2.4 %collective-permute-done.8.refs_0_.refs_7_ = s16[272,128]{1,0:T(8,128)(2,1)S(1)} collective-permute-done((s16[272,128]{1,0:T(8,128)(2,1)S(1)}, s16[272,128]{1,0:T(8,128)(2,1)S(1)}, u32[]{:S(2)}, u32[]{:S(2)}) %collective-permute-start.8) | collective-permute-done | bytes 69664 | tf_op jit(solution)/shard_map/ppermute | solution.py:368
  36.2 8.8 %all_to_all.22 = f32[32,1,128]{2,1,0:T(1,128)S(1)} all-to-all(f32[32,1,128]{2,1,0:T(1,128)S(1)} %bitcast.14), channel_id=1, replica_groups=mesh['lat'=8,'dep'=4] {'lat','dep'}, dimensions={0} | all-to-all | bytes 32768 | tf_op jit(solution)/shard_map/all_to_all | solution.py:503
  45.0 0.1 broadcast_in_dim.2.refs_11_.limits_ref
  45.1 2.8 %shard_map.149 = (f32[8,12,128]{2,1,0:T(8,128)S(1)}, f32[8,12,128]{2,1,0:T(8,128)S(1)}, f32[4,12,128]{2,1,0:T(8,128)S(1)}, f32[4,12,128]{2,1,0:T(8,128)S(1)}, f3...) custom-call(s16[304,128]{1,0:T(8,128)(2,1)S(1)} %get-tuple-element.51.anchor_ref.refs_0_, ...), custom_call_target="tpu_custom_call" | custom-call | flops 1006632960 | bytes 5996544 | tf_op jit(solution)/shard_map/pallas_call | solution.py:60
  48.0 0.1 collective-permute-start.16
  48.0 0.7 collective-permute-start.15
  48.7 1.5 %collective-permute-start.18 = (f32[4,12,128]{2,1,0:T(8,128)S(1)}, f32[4,12,128]{2,1,0:T(8,128)S(1)}, u32[]{:S(2)}, u32[]{:S(2)}) collective-permute-start(f32[4,12,128]{2,1,0:T(8,128)S(1)} %get-tuple-element.74), channel_id=1, source_target_pairs={{0,8},{4,28},{8,16},{12,4},{16,24},{20,12},{24,0},{28,20},{1,9},{5... | collective-permute-start | bytes 73736 | tf_op jit(solution)/shard_map/ppermute | solution.py:383
  50.2 1.4 %collective-permute-start.17 = (f32[4,12,128]{2,1,0:T(8,128)S(1)}, f32[4,12,128]{2,1,0:T(8,128)S(1)}, u32[]{:S(2)}, u32[]{:S(2)}) collective-permute-start(f32[4,12,128]{2,1,0:T(8,128)S(1)} %get-tuple-element.72.refs_4_), channel_id=1, source_target_pairs={{0,24},{4,12},{8,0},{12,20},{16,8},{20,28},{24,16},{28,4},{1,25},{... | collective-permute-start | bytes 73736 | tf_op jit(solution)/shard_map/ppermute | solution.py:383
  51.6 0.2 shard_map.150
  51.8 0.6 collective-permute-start.12
  52.4 1.1 %collective-permute-done.18.refs_8_ = f32[4,12,128]{2,1,0:T(8,128)S(1)} collective-permute-done((f32[4,12,128]{2,1,0:T(8,128)S(1)}, f32[4,12,128]{2,1,0:T(8,128)S(1)}, u32[]{:S(2)}, u32[]{:S(2)}) %collective-permute-start.18) | collective-permute-done | bytes 24608 | tf_op jit(solution)/shard_map/ppermute | solution.py:383
  53.5 0.6 collective-permute-done.17.refs_7_
  54.1 0.0 collective-permute-done.16.refs_6_
  54.1 0.0 collective-permute-done.15.refs_5_
  54.1 2.9 %shard_map.151 = (f32[256,512]{1,0:T(8,128)S(1)}, f32[32,128]{1,0:T(8,128)}) custom-call(f32[6,12,128]{2,1,0:T(8,128)S(1)} %get-tuple-element.42.own_ref.refs_2_.refs_0_, f32[6,12,128]{2,1,0:T(8,128)S(1)} %collective-permute-done.a_ref.refs_3_.refs_1_, f32[6,12,128]{2,1,0:T(8,128)S(1)} %collective-permute-done.1.b_ref.refs_4_.refs_2_, ...), custom_call_target="tpu_custom_call" | custom-call | flops 2013265920 | bytes 4280320 | tf_op jit(solution)/shard_map/pallas_call | solution.py:60
  57.0 2.7 %all-to-all-start.1 = ((f32[32,1,128]{2,1,0:T(1,128)}), f32[32,1,128]{2,1,0:T(1,128)S(1)}, u32[]{:S(2)}, u32[]{:S(2)}) async-start(f32[32,1,128]{2,1,0:T(1,128)} %bitcast.9), calls=%async_computation.1 | async-start | bytes 32768 | tf_op jit(solution)/shard_map/all_to_all | solution.py:503
  59.7 2.7 %collective-permute-start.13 = (s16[272,128]{1,0:T(8,128)(2,1)S(1)}, s16[272,128]{1,0:T(8,128)(2,1)S(1)}, u32[]{:S(2)}, u32[]{:S(2)}) collective-permute-start(s16[272,128]{1,0:T(8,128)(2,1)S(1)} %get-tuple-element.69), channel_id=1, source_target_pairs={{0,2},{1,3},{2,0},{3,1},{4,6},{5,7},{6,4},{7,5},{8,10},{9,11},{10,... | collective-permute-start | bytes 208904 | tf_op jit(solution)/shard_map/ppermute | solution.py:368
  62.5 1.5 %collective-permute-start.14 = (s16[272,128]{1,0:T(8,128)(2,1)S(1)}, s16[272,128]{1,0:T(8,128)(2,1)S(1)}, u32[]{:S(2)}, u32[]{:S(2)}) collective-permute-start(s16[272,128]{1,0:T(8,128)(2,1)S(1)} %get-tuple-element.70), channel_id=1, source_target_pairs={{0,3},{1,2},{2,1},{3,0},{4,7},{5,6},{6,5},{7,4},{8,11},{9,10},{10,... | collective-permute-start | bytes 208904 | tf_op jit(solution)/shard_map/ppermute | solution.py:368
  63.9 3.0 %all-to-all-done.1 = f32[32,1,128]{2,1,0:T(1,128)S(1)} async-done(((f32[32,1,128]{2,1,0:T(1,128)}), f32[32,1,128]{2,1,0:T(1,128)S(1)}, u32[]{:S(2)}, u32[]{:S(2)}) %all-to-all-start.1) | async-done | bytes 16416 | tf_op jit(solution)/shard_map/all_to_all | solution.py:503
  66.9 0.9 %shard_map.152 = (s16[272,128]{1,0:T(8,128)(2,1)S(1)}, s16[272,128]{1,0:T(8,128)(2,1)S(1)}, s16[272,128]{1,0:T(8,128)(2,1)S(1)}, s16[272,128]{1,0:T(8,128)(2,1)S(1)}) custom-call(f32[32,128]{1,0:T(8,128)S(1)} %bitcast.15, f32[256,512]{1,0:T(8,128)S(1)} %get-tuple-element.76.current_ref, f32[256,512]{1,0:T(8,128)S(1)} %get-tuple-element.77.grad_ref, ...), custom_call_target="tpu_custom_call" | custom-call | bytes 1605632 | tf_op jit(solution)/shard_map/pallas_call | solution.py:60
  67.9 0.5 collective-permute-start.19
  68.4 0.6 collective-permute-start.20
  69.0 0.0 collective-permute-done.12.refs_1_
  69.0 3.4 %collective-permute-start.21 = (s16[272,128]{1,0:T(8,128)(2,1)S(1)}, s16[272,128]{1,0:T(8,128)(2,1)S(1)}, u32[]{:S(2)}, u32[]{:S(2)}) collective-permute-start(s16[272,128]{1,0:T(8,128)(2,1)S(1)} %get-tuple-element.81), channel_id=1, source_target_pairs={{0,3},{1,2},{2,1},{3,0},{4,7},{5,6},{6,5},{7,4},{8,11},{9,10},{10,... | collective-permute-start | bytes 208904 | tf_op jit(solution)/shard_map/ppermute | solution.py:368
  72.4 0.0 collective-permute-done.13.refs_2_
  72.4 0.7 collective-permute-done.19.refs_5_
  73.0 3.7 %collective-permute-done.20.refs_6_ = s16[272,128]{1,0:T(8,128)(2,1)S(1)} collective-permute-done((s16[272,128]{1,0:T(8,128)(2,1)S(1)}, s16[272,128]{1,0:T(8,128)(2,1)S(1)}, u32[]{:S(2)}, u32[]{:S(2)}) %collective-permute-start.20) | collective-permute-done | bytes 69664 | tf_op jit(solution)/shard_map/ppermute | solution.py:368
  76.8 0.0 collective-permute-done.21.refs_7_
  76.8 1.2 %shard_map.153 = (f32[16,64,128]{2,1,0:T(8,128)}, f32[16,64,128]{2,1,0:T(8,128)}) custom-call(s16[272,128]{1,0:T(8,128)(2,1)S(1)} %get-tuple-element.67.refs_0_, s16[272,128]{1,0:T(8,128)(2,1)S(1)} %collective-permute-done.12.refs_1_, s16[272,128]{1,0:T(8,128)(2,1)S(1)} %collective-permute-done.13.refs_2_, ...), custom_call_target="tpu_custom_call" | custom-call | bytes 1605632 | tf_op jit(solution)/shard_map/pallas_call | solution.py:60
  (8 shorter events, 0.0 us)
Async XLA Ops:
  0.6 12.0 %copy-start = (bf16[64,128,128]{2,1,0:T(8,128)(2,1)S(1)}, bf16[64,128,128]{2,1,0:T(8,128)(2,1)}, u32[]{:S(2)}) copy-start(bf16[64,128,128]{2,1,0:T(8,128)(2,1)} %table_ref.1) | copy-start | bytes 6291460
  2.2 4.4 %collective-permute-start = (f32[6,12,128]{2,1,0:T(8,128)S(1)}, f32[6,12,128]{2,1,0:T(8,128)S(1)}, u32[]{:S(2)}, u32[]{:S(2)}) collective-permute-start(f32[6,12,128]{2,1,0:T(8,128)S(1)} %get-tuple-element.43), channel_id=1, source_target_pairs={{0,4},{4,0},{8,12},{12,8},{16,20},{20,16},{24,28},{28,24},{1,5},{5... | collective-permute-start | bytes 110600 | tf_op jit(solution)/shard_map/ppermute | solution.py:376
  2.8 5.3 %collective-permute-start.1 = (f32[6,12,128]{2,1,0:T(8,128)S(1)}, f32[6,12,128]{2,1,0:T(8,128)S(1)}, u32[]{:S(2)}, u32[]{:S(2)}) collective-permute-start(f32[6,12,128]{2,1,0:T(8,128)S(1)} %get-tuple-element.44), channel_id=1, source_target_pairs={{0,28},{4,8},{8,4},{12,16},{16,12},{20,24},{24,20},{28,0},{1,29},{... | collective-permute-start | bytes 110600 | tf_op jit(solution)/shard_map/ppermute | solution.py:376
  8.2 4.6 %collective-permute-start.2 = (s16[304,128]{1,0:T(8,128)(2,1)S(1)}, s16[304,128]{1,0:T(8,128)(2,1)S(1)}, u32[]{:S(2)}, u32[]{:S(2)}) collective-permute-start(s16[304,128]{1,0:T(8,128)(2,1)S(1)} %get-tuple-element.52), channel_id=1, source_target_pairs={{0,1},{1,0},{2,3},{3,2},{4,5},{5,4},{6,7},{7,6},{8,9},{9,8},{10,11... | collective-permute-start | bytes 233480 | tf_op jit(solution)/shard_map/ppermute | solution.py:368
  10.0 9.1 %collective-permute-start.3 = (s16[304,128]{1,0:T(8,128)(2,1)S(1)}, s16[304,128]{1,0:T(8,128)(2,1)S(1)}, u32[]{:S(2)}, u32[]{:S(2)}) collective-permute-start(s16[304,128]{1,0:T(8,128)(2,1)S(1)} %get-tuple-element.53), channel_id=1, source_target_pairs={{0,2},{1,3},{2,0},{3,1},{4,6},{5,7},{6,4},{7,5},{8,10},{9,11},{10,... | collective-permute-start | bytes 233480 | tf_op jit(solution)/shard_map/ppermute | solution.py:368
  12.6 6.5 %collective-permute-start.4 = (s16[304,128]{1,0:T(8,128)(2,1)S(1)}, s16[304,128]{1,0:T(8,128)(2,1)S(1)}, u32[]{:S(2)}, u32[]{:S(2)}) collective-permute-start(s16[304,128]{1,0:T(8,128)(2,1)S(1)} %get-tuple-element.54), channel_id=1, source_target_pairs={{0,3},{1,2},{2,1},{3,0},{4,7},{5,6},{6,5},{7,4},{8,11},{9,10},{10,... | collective-permute-start | bytes 233480 | tf_op jit(solution)/shard_map/ppermute | solution.py:368
  12.8 16.4 %copy-start.2 = (bf16[40,2560]{1,0:T(8,128)(2,1)S(1)}, bf16[40,2560]{1,0:T(8,128)(2,1)}, u32[]{:S(2)}) copy-start(bf16[40,2560]{1,0:T(8,128)(2,1)} %constant.7.clone.spread_ref) | copy-start | bytes 614404
  12.8 16.4 %copy-start.3 = (f32[8,2560]{1,0:T(8,128)S(1)}, f32[8,2560]{1,0:T(8,128)}, u32[]{:S(2)}) copy-start(f32[8,2560]{1,0:T(8,128)} %constant.8.clone.number_ref) | copy-start | bytes 245764
  21.2 5.0 %collective-permute-start.7 = (f32[8,12,128]{2,1,0:T(8,128)S(1)}, f32[8,12,128]{2,1,0:T(8,128)S(1)}, u32[]{:S(2)}, u32[]{:S(2)}) collective-permute-start(f32[8,12,128]{2,1,0:T(8,128)S(1)} %get-tuple-element.58.refs_5_), channel_id=1, source_target_pairs={{0,4},{4,0},{8,12},{12,8},{16,20},{20,16},{24,28},{28,24},{1,5},{5... | collective-permute-start | bytes 147464 | tf_op jit(solution)/shard_map/ppermute | solution.py:376
  21.3 8.6 %collective-permute-start.5 = (s16[272,128]{1,0:T(8,128)(2,1)S(1)}, s16[272,128]{1,0:T(8,128)(2,1)S(1)}, u32[]{:S(2)}, u32[]{:S(2)}) collective-permute-start(s16[272,128]{1,0:T(8,128)(2,1)S(1)} %get-tuple-element.56), channel_id=1, source_target_pairs={{0,1},{1,0},{2,3},{3,2},{4,5},{5,4},{6,7},{7,6},{8,9},{9,8},{10,11... | collective-permute-start | bytes 208904 | tf_op jit(solution)/shard_map/ppermute | solution.py:368
  22.8 8.7 %collective-permute-start.6 = (s16[272,128]{1,0:T(8,128)(2,1)S(1)}, s16[272,128]{1,0:T(8,128)(2,1)S(1)}, u32[]{:S(2)}, u32[]{:S(2)}) collective-permute-start(s16[272,128]{1,0:T(8,128)(2,1)S(1)} %get-tuple-element.57), channel_id=1, source_target_pairs={{0,2},{1,3},{2,0},{3,1},{4,6},{5,7},{6,4},{7,5},{8,10},{9,11},{10,... | collective-permute-start | bytes 208904 | tf_op jit(solution)/shard_map/ppermute | solution.py:368
  24.3 7.1 %collective-permute-start.9 = (f32[8,12,128]{2,1,0:T(8,128)S(1)}, f32[8,12,128]{2,1,0:T(8,128)S(1)}, u32[]{:S(2)}, u32[]{:S(2)}) collective-permute-start(f32[8,12,128]{2,1,0:T(8,128)S(1)} %get-tuple-element.60), channel_id=1, source_target_pairs={{0,28},{4,8},{8,4},{12,16},{16,12},{20,24},{24,20},{28,0},{1,29},{... | collective-permute-start | bytes 147464 | tf_op jit(solution)/shard_map/ppermute | solution.py:376
  26.2 5.2 %collective-permute-start.11 = (f32[4,12,128]{2,1,0:T(8,128)S(1)}, f32[4,12,128]{2,1,0:T(8,128)S(1)}, u32[]{:S(2)}, u32[]{:S(2)}) collective-permute-start(f32[4,12,128]{2,1,0:T(8,128)S(1)} %get-tuple-element.61), channel_id=1, source_target_pairs={{0,8},{4,28},{8,16},{12,4},{16,24},{20,12},{24,0},{28,20},{1,9},{5... | collective-permute-start | bytes 73736 | tf_op jit(solution)/shard_map/ppermute | solution.py:383
  26.2 5.2 %collective-permute-start.10 = (f32[4,12,128]{2,1,0:T(8,128)S(1)}, f32[4,12,128]{2,1,0:T(8,128)S(1)}, u32[]{:S(2)}, u32[]{:S(2)}) collective-permute-start(f32[4,12,128]{2,1,0:T(8,128)S(1)} %get-tuple-element.59.refs_6_), channel_id=1, source_target_pairs={{0,24},{4,12},{8,0},{12,20},{16,8},{20,28},{24,16},{28,4},{1,25},{... | collective-permute-start | bytes 73736 | tf_op jit(solution)/shard_map/ppermute | solution.py:383
  29.9 15.2 %copy-start.4 = (f32[256]{0:T(256)S(1)}, f32[256]{0:T(256)}, u32[]{:S(2)}) copy-start(f32[256]{0:T(256)} %param.22) | copy-start | bytes 3076
  29.9 15.3 %copy-start.1 = (bf16[256,256]{1,0:T(8,128)(2,1)S(1)}, bf16[256,256]{1,0:T(8,128)(2,1)}, u32[]{:S(2)}) copy-start(bf16[256,256]{1,0:T(8,128)(2,1)} %constant.6.clone.refs_10_.had_ref) | copy-start | bytes 393220
  29.9 6.3 %collective-permute-start.8 = (s16[272,128]{1,0:T(8,128)(2,1)S(1)}, s16[272,128]{1,0:T(8,128)(2,1)S(1)}, u32[]{:S(2)}, u32[]{:S(2)}) collective-permute-start(s16[272,128]{1,0:T(8,128)(2,1)S(1)} %shard_map.145), channel_id=1, source_target_pairs={{0,3},{1,2},{2,1},{3,0},{4,7},{5,6},{6,5},{7,4},{8,11},{9,10},{10,... | collective-permute-start | bytes 208904 | tf_op jit(solution)/shard_map/ppermute | solution.py:368
  48.0 6.2 %collective-permute-start.16 = (f32[8,12,128]{2,1,0:T(8,128)S(1)}, f32[8,12,128]{2,1,0:T(8,128)S(1)}, u32[]{:S(2)}, u32[]{:S(2)}) collective-permute-start(f32[8,12,128]{2,1,0:T(8,128)S(1)} %get-tuple-element.73), channel_id=1, source_target_pairs={{0,28},{4,8},{8,4},{12,16},{16,12},{20,24},{24,20},{28,0},{1,29},{... | collective-permute-start | bytes 147464 | tf_op jit(solution)/shard_map/ppermute | solution.py:376
  48.0 6.1 %collective-permute-start.15 = (f32[8,12,128]{2,1,0:T(8,128)S(1)}, f32[8,12,128]{2,1,0:T(8,128)S(1)}, u32[]{:S(2)}, u32[]{:S(2)}) collective-permute-start(f32[8,12,128]{2,1,0:T(8,128)S(1)} %get-tuple-element.71.refs_3_), channel_id=1, source_target_pairs={{0,4},{4,0},{8,12},{12,8},{16,20},{20,16},{24,28},{28,24},{1,5},{5... | collective-permute-start | bytes 147464 | tf_op jit(solution)/shard_map/ppermute | solution.py:376
  48.7 4.8 %collective-permute-start.18 = (f32[4,12,128]{2,1,0:T(8,128)S(1)}, f32[4,12,128]{2,1,0:T(8,128)S(1)}, u32[]{:S(2)}, u32[]{:S(2)}) collective-permute-start(f32[4,12,128]{2,1,0:T(8,128)S(1)} %get-tuple-element.74), channel_id=1, source_target_pairs={{0,8},{4,28},{8,16},{12,4},{16,24},{20,12},{24,0},{28,20},{1,9},{5... | collective-permute-start | bytes 73736 | tf_op jit(solution)/shard_map/ppermute | solution.py:383
  50.2 3.9 %collective-permute-start.17 = (f32[4,12,128]{2,1,0:T(8,128)S(1)}, f32[4,12,128]{2,1,0:T(8,128)S(1)}, u32[]{:S(2)}, u32[]{:S(2)}) collective-permute-start(f32[4,12,128]{2,1,0:T(8,128)S(1)} %get-tuple-element.72.refs_4_), channel_id=1, source_target_pairs={{0,24},{4,12},{8,0},{12,20},{16,8},{20,28},{24,16},{28,4},{1,25},{... | collective-permute-start | bytes 73736 | tf_op jit(solution)/shard_map/ppermute | solution.py:383
  51.8 17.1 %collective-permute-start.12 = (s16[272,128]{1,0:T(8,128)(2,1)S(1)}, s16[272,128]{1,0:T(8,128)(2,1)S(1)}, u32[]{:S(2)}, u32[]{:S(2)}) collective-permute-start(s16[272,128]{1,0:T(8,128)(2,1)S(1)} %get-tuple-element.68), channel_id=1, source_target_pairs={{0,1},{1,0},{2,3},{3,2},{4,5},{5,4},{6,7},{7,6},{8,9},{9,8},{10,11... | collective-permute-start | bytes 208904 | tf_op jit(solution)/shard_map/ppermute | solution.py:368
  57.0 9.9 %all-to-all-start.1 = ((f32[32,1,128]{2,1,0:T(1,128)}), f32[32,1,128]{2,1,0:T(1,128)S(1)}, u32[]{:S(2)}, u32[]{:S(2)}) async-start(f32[32,1,128]{2,1,0:T(1,128)} %bitcast.9), calls=%async_computation.1 | async-start | bytes 32768 | tf_op jit(solution)/shard_map/all_to_all | solution.py:503
  59.7 12.6 %collective-permute-start.13 = (s16[272,128]{1,0:T(8,128)(2,1)S(1)}, s16[272,128]{1,0:T(8,128)(2,1)S(1)}, u32[]{:S(2)}, u32[]{:S(2)}) collective-permute-start(s16[272,128]{1,0:T(8,128)(2,1)S(1)} %get-tuple-element.69), channel_id=1, source_target_pairs={{0,2},{1,3},{2,0},{3,1},{4,6},{5,7},{6,4},{7,5},{8,10},{9,11},{10,... | collective-permute-start | bytes 208904 | tf_op jit(solution)/shard_map/ppermute | solution.py:368
  62.5 9.9 %collective-permute-start.14 = (s16[272,128]{1,0:T(8,128)(2,1)S(1)}, s16[272,128]{1,0:T(8,128)(2,1)S(1)}, u32[]{:S(2)}, u32[]{:S(2)}) collective-permute-start(s16[272,128]{1,0:T(8,128)(2,1)S(1)} %get-tuple-element.70), channel_id=1, source_target_pairs={{0,3},{1,2},{2,1},{3,0},{4,7},{5,6},{6,5},{7,4},{8,11},{9,10},{10,... | collective-permute-start | bytes 208904 | tf_op jit(solution)/shard_map/ppermute | solution.py:368
  67.9 5.1 %collective-permute-start.19 = (s16[272,128]{1,0:T(8,128)(2,1)S(1)}, s16[272,128]{1,0:T(8,128)(2,1)S(1)}, u32[]{:S(2)}, u32[]{:S(2)}) collective-permute-start(s16[272,128]{1,0:T(8,128)(2,1)S(1)} %get-tuple-element.79), channel_id=1, source_target_pairs={{0,1},{1,0},{2,3},{3,2},{4,5},{5,4},{6,7},{7,6},{8,9},{9,8},{10,11... | collective-permute-start | bytes 208904 | tf_op jit(solution)/shard_map/ppermute | solution.py:368
  68.4 8.4 %collective-permute-start.20 = (s16[272,128]{1,0:T(8,128)(2,1)S(1)}, s16[272,128]{1,0:T(8,128)(2,1)S(1)}, u32[]{:S(2)}, u32[]{:S(2)}) collective-permute-start(s16[272,128]{1,0:T(8,128)(2,1)S(1)} %get-tuple-element.80), channel_id=1, source_target_pairs={{0,2},{1,3},{2,0},{3,1},{4,6},{5,7},{6,4},{7,5},{8,10},{9,11},{10,... | collective-permute-start | bytes 208904 | tf_op jit(solution)/shard_map/ppermute | solution.py:368
  69.0 7.8 %collective-permute-start.21 = (s16[272,128]{1,0:T(8,128)(2,1)S(1)}, s16[272,128]{1,0:T(8,128)(2,1)S(1)}, u32[]{:S(2)}, u32[]{:S(2)}) collective-permute-start(s16[272,128]{1,0:T(8,128)(2,1)S(1)} %get-tuple-element.81), channel_id=1, source_target_pairs={{0,3},{1,2},{2,1},{3,0},{4,7},{5,6},{6,5},{7,4},{8,11},{9,10},{10,... | collective-permute-start | bytes 208904 | tf_op jit(solution)/shard_map/ppermute | solution.py:368

commit v6 on v5

--- a/solution.py
+++ b/solution.py
@@ -199,7 +199,7 @@
 
 
 def project(rows, block, frames, prints, lifted, choose_ref, table_ref, acc_ref, outs):
-    per = 8 if prints % 8 == 0 else 2
+    per = 16 if prints % 16 == 0 else 2
     tile = table_ref.shape[1]
     total = jnp.zeros((rows * block, tile), f32)
     for start in range(0, prints, per):

time: 78.1 us -> 77.2 us (0.988)
  Pallas kernels: 15.3 us -> 14.4 us
    pallas_call x14, Pallas kernels: 15.3 us -> 14.4 us  [call(): pl.pallas_call(body, out_shape=tuple(outs), in_specs=[pl.BlockSpec(memory...]
where the time goes in v6:
time: 77.2 us; the launch traced here: 77 us
  starting transfers between devices  33.6 us (44%)
  waiting for transfers between devices  19.3 us (25%)
  Pallas kernels  14.4 us (19%)
  blocking collectives  8.85 us (11%)
  between operations  0.82 us (1%)
    ppermute x12, starting transfers between devices, depth_exchange(): lax.ppermute(parts[s], 'dep', [(i, i ^ s) for i in range(count)])  18.2 us
    pallas_call x14, Pallas kernels, call(): pl.pallas_call(body, out_shape=tuple(outs), in_specs=[pl.BlockSpec(memory...  14.4 us
    ppermute x12, waiting for transfers between devices, depth_exchange(): lax.ppermute(parts[s], 'dep', [(i, i ^ s) for i in range(count)])  13.1 us
    all_to_all x1, blocking collectives, step_sums(): lax.all_to_all(sums, ('lat', 'dep'), split_axis=0, concat_axis=0, tiled=T...  8.85 us
    ppermute x3, starting transfers between devices, partner_exchange(): lax.ppermute(to_b, 'lat', pairs_b)  5.5 us
    ppermute x2, starting transfers between devices, past_exchange(): lax.ppermute(part_b, 'lat', past_a)  4.37 us
    all_to_all x1, waiting for transfers between devices, step_sums(): lax.all_to_all(sums, ('lat', 'dep'), split_axis=0, concat_axis=0, tiled=T...  2.99 us
    all_to_all x1, starting transfers between devices, step_sums(): lax.all_to_all(sums, ('lat', 'dep'), split_axis=0, concat_axis=0, tiled=T...  2.71 us
  transfers between devices with their start and end apart: 23, of which 8 were waited for; matrix products, arithmetic and copies ran while one was open for 0% of the time, Pallas kernels for 10%

profile of v6, /device:TPU:0, one launch (start us, length us, event | category | flops | bytes accessed | tf_op | source)
XLA Modules:
  0.0 77.0 jit_solution(2419332272159813107)
XLA Ops:
  0.6 1.6 %shard_map.140 = (f32[6,12,128]{2,1,0:T(8,128)S(1)}, f32[6,12,128]{2,1,0:T(8,128)S(1)}, f32[6,12,128]{2,1,0:T(8,128)S(1)}, f32[16,64,128]{2,1,0:T(8,128)S(1)}, f32[16,64,128]{2,1,0:T(8,128)S(1)}) custom-call(s32[1,12]{1,0:T(1,128)} %bitcast.20, s32[12,3,1,64]{3,2,1,0:T(1,128)} %bitcast.17, s32[12,1,64]{2,1,0:T(1,128)} %bitcast.18, s32[12,1,64]{2,1,0:T(1,128)} %bitcast.19, ...), custom_call_target="tpu_custom_call" | custom-call | bytes 2255920 | tf_op jit(solution)/shard_map/pallas_call | solution.py:60
  2.2 0.5 collective-permute-start
  2.8 3.6 %collective-permute-start.1 = (f32[6,12,128]{2,1,0:T(8,128)S(1)}, f32[6,12,128]{2,1,0:T(8,128)S(1)}, u32[]{:S(2)}, u32[]{:S(2)}) collective-permute-start(f32[6,12,128]{2,1,0:T(8,128)S(1)} %get-tuple-element.44), channel_id=1, source_target_pairs={{0,28},{4,8},{8,4},{12,16},{16,12},{20,24},{24,20},{28,0},{1,29},{... | collective-permute-start | bytes 110600 | tf_op jit(solution)/shard_map/ppermute | solution.py:376
  6.3 0.3 shard_map.141
  6.6 0.0 collective-permute-done.a_ref.refs_3_.refs_1_
  6.7 1.4 %collective-permute-done.1.b_ref.refs_4_.refs_2_ = f32[6,12,128]{2,1,0:T(8,128)S(1)} collective-permute-done((f32[6,12,128]{2,1,0:T(8,128)S(1)}, f32[6,12,128]{2,1,0:T(8,128)S(1)}, u32[]{:S(2)}, u32[]{:S(2)}) %collective-permute-start.1) | collective-permute-done | bytes 36896 | tf_op jit(solution)/shard_map/ppermute | solution.py:376
  8.1 0.1 shard_map.142
  8.2 1.8 %collective-permute-start.2 = (s16[304,128]{1,0:T(8,128)(2,1)S(1)}, s16[304,128]{1,0:T(8,128)(2,1)S(1)}, u32[]{:S(2)}, u32[]{:S(2)}) collective-permute-start(s16[304,128]{1,0:T(8,128)(2,1)S(1)} %get-tuple-element.52), channel_id=1, source_target_pairs={{0,1},{1,0},{2,3},{3,2},{4,5},{5,4},{6,7},{7,6},{8,9},{9,8},{10,11... | collective-permute-start | bytes 233480 | tf_op jit(solution)/shard_map/ppermute | solution.py:368
  10.0 2.6 %collective-permute-start.3 = (s16[304,128]{1,0:T(8,128)(2,1)S(1)}, s16[304,128]{1,0:T(8,128)(2,1)S(1)}, u32[]{:S(2)}, u32[]{:S(2)}) collective-permute-start(s16[304,128]{1,0:T(8,128)(2,1)S(1)} %get-tuple-element.53), channel_id=1, source_target_pairs={{0,2},{1,3},{2,0},{3,1},{4,6},{5,7},{6,4},{7,5},{8,10},{9,11},{10,... | collective-permute-start | bytes 233480 | tf_op jit(solution)/shard_map/ppermute | solution.py:368
  12.6 0.1 collective-permute-start.4
  12.6 0.1 shard_map.143.refs_4_.refs_12_.refs_13_.refs_10_
  12.8 0.0 copy-start.2
  12.8 0.0 copy-start.3
  12.8 0.0 collective-permute-done.2.refs_1_
  12.8 6.3 %collective-permute-done.3.refs_2_ = s16[304,128]{1,0:T(8,128)(2,1)S(1)} collective-permute-done((s16[304,128]{1,0:T(8,128)(2,1)S(1)}, s16[304,128]{1,0:T(8,128)(2,1)S(1)}, u32[]{:S(2)}, u32[]{:S(2)}) %collective-permute-start.3) | collective-permute-done | bytes 77856 | tf_op jit(solution)/shard_map/ppermute | solution.py:368
  19.1 0.0 collective-permute-done.4.refs_3_
  19.1 1.7 %shard_map.144 = (f32[8,12,128]{2,1,0:T(8,128)S(1)}, f32[8,12,128]{2,1,0:T(8,128)S(1)}, f32[4,12,128]{2,1,0:T(8,128)S(1)}, f32[4,12,128]{2,1,0:T(8,128)S(1)}, bf...) custom-call(s16[304,128]{1,0:T(8,128)(2,1)S(1)} %get-tuple-element.51.anchor_ref.refs_0_, ...), custom_call_target="tpu_custom_call" | custom-call | flops 1006632960 | bytes 3907584 | tf_op jit(solution)/shard_map/pallas_call | solution.py:60
  20.7 0.1 collective-permute-start.7
  20.8 1.5 %collective-permute-start.5 = (s16[272,128]{1,0:T(8,128)(2,1)S(1)}, s16[272,128]{1,0:T(8,128)(2,1)S(1)}, u32[]{:S(2)}, u32[]{:S(2)}) collective-permute-start(s16[272,128]{1,0:T(8,128)(2,1)S(1)} %get-tuple-element.56), channel_id=1, source_target_pairs={{0,1},{1,0},{2,3},{3,2},{4,5},{5,4},{6,7},{7,6},{8,9},{9,8},{10,11... | collective-permute-start | bytes 208904 | tf_op jit(solution)/shard_map/ppermute | solution.py:368
  22.3 1.6 %collective-permute-start.6 = (s16[272,128]{1,0:T(8,128)(2,1)S(1)}, s16[272,128]{1,0:T(8,128)(2,1)S(1)}, u32[]{:S(2)}, u32[]{:S(2)}) collective-permute-start(s16[272,128]{1,0:T(8,128)(2,1)S(1)} %get-tuple-element.57), channel_id=1, source_target_pairs={{0,2},{1,3},{2,0},{3,1},{4,6},{5,7},{6,4},{7,5},{8,10},{9,11},{10,... | collective-permute-start | bytes 208904 | tf_op jit(solution)/shard_map/ppermute | solution.py:368
  23.9 1.9 %collective-permute-start.9 = (f32[8,12,128]{2,1,0:T(8,128)S(1)}, f32[8,12,128]{2,1,0:T(8,128)S(1)}, u32[]{:S(2)}, u32[]{:S(2)}) collective-permute-start(f32[8,12,128]{2,1,0:T(8,128)S(1)} %get-tuple-element.60), channel_id=1, source_target_pairs={{0,28},{4,8},{8,4},{12,16},{16,12},{20,24},{24,20},{28,0},{1,29},{... | collective-permute-start | bytes 147464 | tf_op jit(solution)/shard_map/ppermute | solution.py:376
  25.8 0.0 collective-permute-start.11
  25.8 0.0 collective-permute-done.7.anchor_ref.refs_7_
  25.8 2.9 %collective-permute-start.10 = (f32[4,12,128]{2,1,0:T(8,128)S(1)}, f32[4,12,128]{2,1,0:T(8,128)S(1)}, u32[]{:S(2)}, u32[]{:S(2)}) collective-permute-start(f32[4,12,128]{2,1,0:T(8,128)S(1)} %get-tuple-element.59.refs_6_), channel_id=1, source_target_pairs={{0,24},{4,12},{8,0},{12,20},{16,8},{20,28},{24,16},{28,4},{1,25},{... | collective-permute-start | bytes 73736 | tf_op jit(solution)/shard_map/ppermute | solution.py:383
  28.7 0.5 shard_map.146.refs_11_.refs_9_
  29.3 0.1 shard_map.145
  29.4 0.0 copy-start.4
  29.4 0.0 copy-start.1
  29.4 0.0 collective-permute-done.5.refs_0_.refs_5_
  29.4 1.5 %collective-permute-start.8 = (s16[272,128]{1,0:T(8,128)(2,1)S(1)}, s16[272,128]{1,0:T(8,128)(2,1)S(1)}, u32[]{:S(2)}, u32[]{:S(2)}) collective-permute-start(s16[272,128]{1,0:T(8,128)(2,1)S(1)} %shard_map.145), channel_id=1, source_target_pairs={{0,3},{1,2},{2,1},{3,0},{4,7},{5,6},{6,5},{7,4},{8,11},{9,10},{10,... | collective-permute-start | bytes 208904 | tf_op jit(solution)/shard_map/ppermute | solution.py:368
  31.0 0.0 collective-permute-done.6.refs_1_.refs_6_
  31.0 0.0 collective-permute-done.11.refs_10_
  31.0 0.0 collective-permute-done.10.refs_9_
  31.0 0.0 collective-permute-done.9.refs_8_
  31.0 2.3 %shard_map.147 = (f32[256,512]{1,0:T(8,128)S(1)}, f32[32,128]{1,0:T(8,128)S(1)}) custom-call(s16[272,128]{1,0:T(8,128)(2,1)S(1)} %collective-permute-done.5.refs_0_.refs_5_, s16[272,128]{1,0:T(8,128)(2,1)S(1)} %collective-permute-done.6.refs_1_.refs_6_, f32[6,12,128]{2,1,0:T(8,128)S(1)} %get-tuple-element.42.own_ref.refs_2_.refs_0_, ...), custom_call_target="tpu_custom_call" | custom-call | flops 2013265920 | bytes 4280320 | tf_op jit(solution)/shard_map/pallas_call | solution.py:60
  33.3 2.4 %collective-permute-done.8.refs_0_.refs_7_ = s16[272,128]{1,0:T(8,128)(2,1)S(1)} collective-permute-done((s16[272,128]{1,0:T(8,128)(2,1)S(1)}, s16[272,128]{1,0:T(8,128)(2,1)S(1)}, u32[]{:S(2)}, u32[]{:S(2)}) %collective-permute-start.8) | collective-permute-done | bytes 69664 | tf_op jit(solution)/shard_map/ppermute | solution.py:368
  35.7 8.8 %all_to_all.22 = f32[32,1,128]{2,1,0:T(1,128)S(1)} all-to-all(f32[32,1,128]{2,1,0:T(1,128)S(1)} %bitcast.14), channel_id=1, replica_groups=mesh['lat'=8,'dep'=4] {'lat','dep'}, dimensions={0} | all-to-all | bytes 32768 | tf_op jit(solution)/shard_map/all_to_all | solution.py:503
  44.6 0.1 broadcast_in_dim.2.refs_11_.limits_ref
  44.7 2.4 %shard_map.149 = (f32[8,12,128]{2,1,0:T(8,128)S(1)}, f32[8,12,128]{2,1,0:T(8,128)S(1)}, f32[4,12,128]{2,1,0:T(8,128)S(1)}, f32[4,12,128]{2,1,0:T(8,128)S(1)}, f3...) custom-call(s16[304,128]{1,0:T(8,128)(2,1)S(1)} %get-tuple-element.51.anchor_ref.refs_0_, ...), custom_call_target="tpu_custom_call" | custom-call | flops 1006632960 | bytes 5996544 | tf_op jit(solution)/shard_map/pallas_call | solution.py:60
  47.0 0.1 collective-permute-start.16
  47.1 0.7 collective-permute-start.15
  47.8 1.5 %collective-permute-start.18 = (f32[4,12,128]{2,1,0:T(8,128)S(1)}, f32[4,12,128]{2,1,0:T(8,128)S(1)}, u32[]{:S(2)}, u32[]{:S(2)}) collective-permute-start(f32[4,12,128]{2,1,0:T(8,128)S(1)} %get-tuple-element.74), channel_id=1, source_target_pairs={{0,8},{4,28},{8,16},{12,4},{16,24},{20,12},{24,0},{28,20},{1,9},{5... | collective-permute-start | bytes 73736 | tf_op jit(solution)/shard_map/ppermute | solution.py:383
  49.3 1.4 %collective-permute-start.17 = (f32[4,12,128]{2,1,0:T(8,128)S(1)}, f32[4,12,128]{2,1,0:T(8,128)S(1)}, u32[]{:S(2)}, u32[]{:S(2)}) collective-permute-start(f32[4,12,128]{2,1,0:T(8,128)S(1)} %get-tuple-element.72.refs_4_), channel_id=1, source_target_pairs={{0,24},{4,12},{8,0},{12,20},{16,8},{20,28},{24,16},{28,4},{1,25},{... | collective-permute-start | bytes 73736 | tf_op jit(solution)/shard_map/ppermute | solution.py:383
  50.7 0.2 shard_map.150
  50.9 0.6 collective-permute-start.12
  51.5 1.1 %collective-permute-done.18.refs_8_ = f32[4,12,128]{2,1,0:T(8,128)S(1)} collective-permute-done((f32[4,12,128]{2,1,0:T(8,128)S(1)}, f32[4,12,128]{2,1,0:T(8,128)S(1)}, u32[]{:S(2)}, u32[]{:S(2)}) %collective-permute-start.18) | collective-permute-done | bytes 24608 | tf_op jit(solution)/shard_map/ppermute | solution.py:383
  52.6 0.6 collective-permute-done.17.refs_7_
  53.2 0.0 collective-permute-done.16.refs_6_
  53.2 0.0 collective-permute-done.15.refs_5_
  53.2 2.9 %shard_map.151 = (f32[256,512]{1,0:T(8,128)S(1)}, f32[32,128]{1,0:T(8,128)}) custom-call(f32[6,12,128]{2,1,0:T(8,128)S(1)} %get-tuple-element.42.own_ref.refs_2_.refs_0_, f32[6,12,128]{2,1,0:T(8,128)S(1)} %collective-permute-done.a_ref.refs_3_.refs_1_, f32[6,12,128]{2,1,0:T(8,128)S(1)} %collective-permute-done.1.b_ref.refs_4_.refs_2_, ...), custom_call_target="tpu_custom_call" | custom-call | flops 2013265920 | bytes 4280320 | tf_op jit(solution)/shard_map/pallas_call | solution.py:60
  56.1 2.7 %all-to-all-start.1 = ((f32[32,1,128]{2,1,0:T(1,128)}), f32[32,1,128]{2,1,0:T(1,128)S(1)}, u32[]{:S(2)}, u32[]{:S(2)}) async-start(f32[32,1,128]{2,1,0:T(1,128)} %bitcast.9), calls=%async_computation.1 | async-start | bytes 32768 | tf_op jit(solution)/shard_map/all_to_all | solution.py:503
  58.8 2.7 %collective-permute-start.13 = (s16[272,128]{1,0:T(8,128)(2,1)S(1)}, s16[272,128]{1,0:T(8,128)(2,1)S(1)}, u32[]{:S(2)}, u32[]{:S(2)}) collective-permute-start(s16[272,128]{1,0:T(8,128)(2,1)S(1)} %get-tuple-element.69), channel_id=1, source_target_pairs={{0,2},{1,3},{2,0},{3,1},{4,6},{5,7},{6,4},{7,5},{8,10},{9,11},{10,... | collective-permute-start | bytes 208904 | tf_op jit(solution)/shard_map/ppermute | solution.py:368
  61.6 1.5 %collective-permute-start.14 = (s16[272,128]{1,0:T(8,128)(2,1)S(1)}, s16[272,128]{1,0:T(8,128)(2,1)S(1)}, u32[]{:S(2)}, u32[]{:S(2)}) collective-permute-start(s16[272,128]{1,0:T(8,128)(2,1)S(1)} %get-tuple-element.70), channel_id=1, source_target_pairs={{0,3},{1,2},{2,1},{3,0},{4,7},{5,6},{6,5},{7,4},{8,11},{9,10},{10,... | collective-permute-start | bytes 208904 | tf_op jit(solution)/shard_map/ppermute | solution.py:368
  63.0 3.0 %all-to-all-done.1 = f32[32,1,128]{2,1,0:T(1,128)S(1)} async-done(((f32[32,1,128]{2,1,0:T(1,128)}), f32[32,1,128]{2,1,0:T(1,128)S(1)}, u32[]{:S(2)}, u32[]{:S(2)}) %all-to-all-start.1) | async-done | bytes 16416 | tf_op jit(solution)/shard_map/all_to_all | solution.py:503
  66.0 0.9 %shard_map.152 = (s16[272,128]{1,0:T(8,128)(2,1)S(1)}, s16[272,128]{1,0:T(8,128)(2,1)S(1)}, s16[272,128]{1,0:T(8,128)(2,1)S(1)}, s16[272,128]{1,0:T(8,128)(2,1)S(1)}) custom-call(f32[32,128]{1,0:T(8,128)S(1)} %bitcast.15, f32[256,512]{1,0:T(8,128)S(1)} %get-tuple-element.76.current_ref, f32[256,512]{1,0:T(8,128)S(1)} %get-tuple-element.77.grad_ref, ...), custom_call_target="tpu_custom_call" | custom-call | bytes 1605632 | tf_op jit(solution)/shard_map/pallas_call | solution.py:60
  67.0 0.5 collective-permute-start.19
  67.4 0.6 collective-permute-start.20
  68.1 0.0 collective-permute-done.12.refs_1_
  68.1 3.4 %collective-permute-start.21 = (s16[272,128]{1,0:T(8,128)(2,1)S(1)}, s16[272,128]{1,0:T(8,128)(2,1)S(1)}, u32[]{:S(2)}, u32[]{:S(2)}) collective-permute-start(s16[272,128]{1,0:T(8,128)(2,1)S(1)} %get-tuple-element.81), channel_id=1, source_target_pairs={{0,3},{1,2},{2,1},{3,0},{4,7},{5,6},{6,5},{7,4},{8,11},{9,10},{10,... | collective-permute-start | bytes 208904 | tf_op jit(solution)/shard_map/ppermute | solution.py:368
  71.4 0.0 collective-permute-done.13.refs_2_
  71.4 0.0 collective-permute-done.14.refs_3_
  71.4 0.7 collective-permute-done.19.refs_5_
  72.1 3.7 %collective-permute-done.20.refs_6_ = s16[272,128]{1,0:T(8,128)(2,1)S(1)} collective-permute-done((s16[272,128]{1,0:T(8,128)(2,1)S(1)}, s16[272,128]{1,0:T(8,128)(2,1)S(1)}, u32[]{:S(2)}, u32[]{:S(2)}) %collective-permute-start.20) | collective-permute-done | bytes 69664 | tf_op jit(solution)/shard_map/ppermute | solution.py:368
  75.8 1.2 %shard_map.153 = (f32[16,64,128]{2,1,0:T(8,128)}, f32[16,64,128]{2,1,0:T(8,128)}) custom-call(s16[272,128]{1,0:T(8,128)(2,1)S(1)} %get-tuple-element.67.refs_0_, s16[272,128]{1,0:T(8,128)(2,1)S(1)} %collective-permute-done.12.refs_1_, s16[272,128]{1,0:T(8,128)(2,1)S(1)} %collective-permute-done.13.refs_2_, ...), custom_call_target="tpu_custom_call" | custom-call | bytes 1605632 | tf_op jit(solution)/shard_map/pallas_call | solution.py:60
  (8 shorter events, 0.0 us)
Async XLA Ops:
  0.6 12.0 %copy-start = (bf16[64,128,128]{2,1,0:T(8,128)(2,1)S(1)}, bf16[64,128,128]{2,1,0:T(8,128)(2,1)}, u32[]{:S(2)}) copy-start(bf16[64,128,128]{2,1,0:T(8,128)(2,1)} %table_ref.1) | copy-start | bytes 6291460
  2.2 4.4 %collective-permute-start = (f32[6,12,128]{2,1,0:T(8,128)S(1)}, f32[6,12,128]{2,1,0:T(8,128)S(1)}, u32[]{:S(2)}, u32[]{:S(2)}) collective-permute-start(f32[6,12,128]{2,1,0:T(8,128)S(1)} %get-tuple-element.43), channel_id=1, source_target_pairs={{0,4},{4,0},{8,12},{12,8},{16,20},{20,16},{24,28},{28,24},{1,5},{5... | collective-permute-start | bytes 110600 | tf_op jit(solution)/shard_map/ppermute | solution.py:376
  2.8 5.3 %collective-permute-start.1 = (f32[6,12,128]{2,1,0:T(8,128)S(1)}, f32[6,12,128]{2,1,0:T(8,128)S(1)}, u32[]{:S(2)}, u32[]{:S(2)}) collective-permute-start(f32[6,12,128]{2,1,0:T(8,128)S(1)} %get-tuple-element.44), channel_id=1, source_target_pairs={{0,28},{4,8},{8,4},{12,16},{16,12},{20,24},{24,20},{28,0},{1,29},{... | collective-permute-start | bytes 110600 | tf_op jit(solution)/shard_map/ppermute | solution.py:376
  8.2 4.6 %collective-permute-start.2 = (s16[304,128]{1,0:T(8,128)(2,1)S(1)}, s16[304,128]{1,0:T(8,128)(2,1)S(1)}, u32[]{:S(2)}, u32[]{:S(2)}) collective-permute-start(s16[304,128]{1,0:T(8,128)(2,1)S(1)} %get-tuple-element.52), channel_id=1, source_target_pairs={{0,1},{1,0},{2,3},{3,2},{4,5},{5,4},{6,7},{7,6},{8,9},{9,8},{10,11... | collective-permute-start | bytes 233480 | tf_op jit(solution)/shard_map/ppermute | solution.py:368
  10.0 9.1 %collective-permute-start.3 = (s16[304,128]{1,0:T(8,128)(2,1)S(1)}, s16[304,128]{1,0:T(8,128)(2,1)S(1)}, u32[]{:S(2)}, u32[]{:S(2)}) collective-permute-start(s16[304,128]{1,0:T(8,128)(2,1)S(1)} %get-tuple-element.53), channel_id=1, source_target_pairs={{0,2},{1,3},{2,0},{3,1},{4,6},{5,7},{6,4},{7,5},{8,10},{9,11},{10,... | collective-permute-start | bytes 233480 | tf_op jit(solution)/shard_map/ppermute | solution.py:368
  12.6 6.5 %collective-permute-start.4 = (s16[304,128]{1,0:T(8,128)(2,1)S(1)}, s16[304,128]{1,0:T(8,128)(2,1)S(1)}, u32[]{:S(2)}, u32[]{:S(2)}) collective-permute-start(s16[304,128]{1,0:T(8,128)(2,1)S(1)} %get-tuple-element.54), channel_id=1, source_target_pairs={{0,3},{1,2},{2,1},{3,0},{4,7},{5,6},{6,5},{7,4},{8,11},{9,10},{10,... | collective-permute-start | bytes 233480 | tf_op jit(solution)/shard_map/ppermute | solution.py:368
  12.8 15.9 %copy-start.2 = (bf16[40,2560]{1,0:T(8,128)(2,1)S(1)}, bf16[40,2560]{1,0:T(8,128)(2,1)}, u32[]{:S(2)}) copy-start(bf16[40,2560]{1,0:T(8,128)(2,1)} %constant.7.clone.spread_ref) | copy-start | bytes 614404
  12.8 15.9 %copy-start.3 = (f32[8,2560]{1,0:T(8,128)S(1)}, f32[8,2560]{1,0:T(8,128)}, u32[]{:S(2)}) copy-start(f32[8,2560]{1,0:T(8,128)} %constant.8.clone.number_ref) | copy-start | bytes 245764
  20.7 5.0 %collective-permute-start.7 = (f32[8,12,128]{2,1,0:T(8,128)S(1)}, f32[8,12,128]{2,1,0:T(8,128)S(1)}, u32[]{:S(2)}, u32[]{:S(2)}) collective-permute-start(f32[8,12,128]{2,1,0:T(8,128)S(1)} %get-tuple-element.58.refs_5_), channel_id=1, source_target_pairs={{0,4},{4,0},{8,12},{12,8},{16,20},{20,16},{24,28},{28,24},{1,5},{5... | collective-permute-start | bytes 147464 | tf_op jit(solution)/shard_map/ppermute | solution.py:376
  20.8 8.6 %collective-permute-start.5 = (s16[272,128]{1,0:T(8,128)(2,1)S(1)}, s16[272,128]{1,0:T(8,128)(2,1)S(1)}, u32[]{:S(2)}, u32[]{:S(2)}) collective-permute-start(s16[272,128]{1,0:T(8,128)(2,1)S(1)} %get-tuple-element.56), channel_id=1, source_target_pairs={{0,1},{1,0},{2,3},{3,2},{4,5},{5,4},{6,7},{7,6},{8,9},{9,8},{10,11... | collective-permute-start | bytes 208904 | tf_op jit(solution)/shard_map/ppermute | solution.py:368
  22.3 8.7 %collective-permute-start.6 = (s16[272,128]{1,0:T(8,128)(2,1)S(1)}, s16[272,128]{1,0:T(8,128)(2,1)S(1)}, u32[]{:S(2)}, u32[]{:S(2)}) collective-permute-start(s16[272,128]{1,0:T(8,128)(2,1)S(1)} %get-tuple-element.57), channel_id=1, source_target_pairs={{0,2},{1,3},{2,0},{3,1},{4,6},{5,7},{6,4},{7,5},{8,10},{9,11},{10,... | collective-permute-start | bytes 208904 | tf_op jit(solution)/shard_map/ppermute | solution.py:368
  23.9 7.1 %collective-permute-start.9 = (f32[8,12,128]{2,1,0:T(8,128)S(1)}, f32[8,12,128]{2,1,0:T(8,128)S(1)}, u32[]{:S(2)}, u32[]{:S(2)}) collective-permute-start(f32[8,12,128]{2,1,0:T(8,128)S(1)} %get-tuple-element.60), channel_id=1, source_target_pairs={{0,28},{4,8},{8,4},{12,16},{16,12},{20,24},{24,20},{28,0},{1,29},{... | collective-permute-start | bytes 147464 | tf_op jit(solution)/shard_map/ppermute | solution.py:376
  25.8 5.2 %collective-permute-start.11 = (f32[4,12,128]{2,1,0:T(8,128)S(1)}, f32[4,12,128]{2,1,0:T(8,128)S(1)}, u32[]{:S(2)}, u32[]{:S(2)}) collective-permute-start(f32[4,12,128]{2,1,0:T(8,128)S(1)} %get-tuple-element.61), channel_id=1, source_target_pairs={{0,8},{4,28},{8,16},{12,4},{16,24},{20,12},{24,0},{28,20},{1,9},{5... | collective-permute-start | bytes 73736 | tf_op jit(solution)/shard_map/ppermute | solution.py:383
  25.8 5.2 %collective-permute-start.10 = (f32[4,12,128]{2,1,0:T(8,128)S(1)}, f32[4,12,128]{2,1,0:T(8,128)S(1)}, u32[]{:S(2)}, u32[]{:S(2)}) collective-permute-start(f32[4,12,128]{2,1,0:T(8,128)S(1)} %get-tuple-element.59.refs_6_), channel_id=1, source_target_pairs={{0,24},{4,12},{8,0},{12,20},{16,8},{20,28},{24,16},{28,4},{1,25},{... | collective-permute-start | bytes 73736 | tf_op jit(solution)/shard_map/ppermute | solution.py:383
  29.4 15.2 %copy-start.4 = (f32[256]{0:T(256)S(1)}, f32[256]{0:T(256)}, u32[]{:S(2)}) copy-start(f32[256]{0:T(256)} %param.22) | copy-start | bytes 3076
  29.4 15.3 %copy-start.1 = (bf16[256,256]{1,0:T(8,128)(2,1)S(1)}, bf16[256,256]{1,0:T(8,128)(2,1)}, u32[]{:S(2)}) copy-start(bf16[256,256]{1,0:T(8,128)(2,1)} %constant.6.clone.refs_10_.had_ref) | copy-start | bytes 393220
  29.4 6.3 %collective-permute-start.8 = (s16[272,128]{1,0:T(8,128)(2,1)S(1)}, s16[272,128]{1,0:T(8,128)(2,1)S(1)}, u32[]{:S(2)}, u32[]{:S(2)}) collective-permute-start(s16[272,128]{1,0:T(8,128)(2,1)S(1)} %shard_map.145), channel_id=1, source_target_pairs={{0,3},{1,2},{2,1},{3,0},{4,7},{5,6},{6,5},{7,4},{8,11},{9,10},{10,... | collective-permute-start | bytes 208904 | tf_op jit(solution)/shard_map/ppermute | solution.py:368
  47.0 6.2 %collective-permute-start.16 = (f32[8,12,128]{2,1,0:T(8,128)S(1)}, f32[8,12,128]{2,1,0:T(8,128)S(1)}, u32[]{:S(2)}, u32[]{:S(2)}) collective-permute-start(f32[8,12,128]{2,1,0:T(8,128)S(1)} %get-tuple-element.73), channel_id=1, source_target_pairs={{0,28},{4,8},{8,4},{12,16},{16,12},{20,24},{24,20},{28,0},{1,29},{... | collective-permute-start | bytes 147464 | tf_op jit(solution)/shard_map/ppermute | solution.py:376
  47.1 6.1 %collective-permute-start.15 = (f32[8,12,128]{2,1,0:T(8,128)S(1)}, f32[8,12,128]{2,1,0:T(8,128)S(1)}, u32[]{:S(2)}, u32[]{:S(2)}) collective-permute-start(f32[8,12,128]{2,1,0:T(8,128)S(1)} %get-tuple-element.71.refs_3_), channel_id=1, source_target_pairs={{0,4},{4,0},{8,12},{12,8},{16,20},{20,16},{24,28},{28,24},{1,5},{5... | collective-permute-start | bytes 147464 | tf_op jit(solution)/shard_map/ppermute | solution.py:376
  47.8 4.8 %collective-permute-start.18 = (f32[4,12,128]{2,1,0:T(8,128)S(1)}, f32[4,12,128]{2,1,0:T(8,128)S(1)}, u32[]{:S(2)}, u32[]{:S(2)}) collective-permute-start(f32[4,12,128]{2,1,0:T(8,128)S(1)} %get-tuple-element.74), channel_id=1, source_target_pairs={{0,8},{4,28},{8,16},{12,4},{16,24},{20,12},{24,0},{28,20},{1,9},{5... | collective-permute-start | bytes 73736 | tf_op jit(solution)/shard_map/ppermute | solution.py:383
  49.3 3.9 %collective-permute-start.17 = (f32[4,12,128]{2,1,0:T(8,128)S(1)}, f32[4,12,128]{2,1,0:T(8,128)S(1)}, u32[]{:S(2)}, u32[]{:S(2)}) collective-permute-start(f32[4,12,128]{2,1,0:T(8,128)S(1)} %get-tuple-element.72.refs_4_), channel_id=1, source_target_pairs={{0,24},{4,12},{8,0},{12,20},{16,8},{20,28},{24,16},{28,4},{1,25},{... | collective-permute-start | bytes 73736 | tf_op jit(solution)/shard_map/ppermute | solution.py:383
  50.9 17.1 %collective-permute-start.12 = (s16[272,128]{1,0:T(8,128)(2,1)S(1)}, s16[272,128]{1,0:T(8,128)(2,1)S(1)}, u32[]{:S(2)}, u32[]{:S(2)}) collective-permute-start(s16[272,128]{1,0:T(8,128)(2,1)S(1)} %get-tuple-element.68), channel_id=1, source_target_pairs={{0,1},{1,0},{2,3},{3,2},{4,5},{5,4},{6,7},{7,6},{8,9},{9,8},{10,11... | collective-permute-start | bytes 208904 | tf_op jit(solution)/shard_map/ppermute | solution.py:368
  56.1 9.9 %all-to-all-start.1 = ((f32[32,1,128]{2,1,0:T(1,128)}), f32[32,1,128]{2,1,0:T(1,128)S(1)}, u32[]{:S(2)}, u32[]{:S(2)}) async-start(f32[32,1,128]{2,1,0:T(1,128)} %bitcast.9), calls=%async_computation.1 | async-start | bytes 32768 | tf_op jit(solution)/shard_map/all_to_all | solution.py:503
  58.8 12.6 %collective-permute-start.13 = (s16[272,128]{1,0:T(8,128)(2,1)S(1)}, s16[272,128]{1,0:T(8,128)(2,1)S(1)}, u32[]{:S(2)}, u32[]{:S(2)}) collective-permute-start(s16[272,128]{1,0:T(8,128)(2,1)S(1)} %get-tuple-element.69), channel_id=1, source_target_pairs={{0,2},{1,3},{2,0},{3,1},{4,6},{5,7},{6,4},{7,5},{8,10},{9,11},{10,... | collective-permute-start | bytes 208904 | tf_op jit(solution)/shard_map/ppermute | solution.py:368
  61.6 9.9 %collective-permute-start.14 = (s16[272,128]{1,0:T(8,128)(2,1)S(1)}, s16[272,128]{1,0:T(8,128)(2,1)S(1)}, u32[]{:S(2)}, u32[]{:S(2)}) collective-permute-start(s16[272,128]{1,0:T(8,128)(2,1)S(1)} %get-tuple-element.70), channel_id=1, source_target_pairs={{0,3},{1,2},{2,1},{3,0},{4,7},{5,6},{6,5},{7,4},{8,11},{9,10},{10,... | collective-permute-start | bytes 208904 | tf_op jit(solution)/shard_map/ppermute | solution.py:368
  67.0 5.1 %collective-permute-start.19 = (s16[272,128]{1,0:T(8,128)(2,1)S(1)}, s16[272,128]{1,0:T(8,128)(2,1)S(1)}, u32[]{:S(2)}, u32[]{:S(2)}) collective-permute-start(s16[272,128]{1,0:T(8,128)(2,1)S(1)} %get-tuple-element.79), channel_id=1, source_target_pairs={{0,1},{1,0},{2,3},{3,2},{4,5},{5,4},{6,7},{7,6},{8,9},{9,8},{10,11... | collective-permute-start | bytes 208904 | tf_op jit(solution)/shard_map/ppermute | solution.py:368
  67.4 8.4 %collective-permute-start.20 = (s16[272,128]{1,0:T(8,128)(2,1)S(1)}, s16[272,128]{1,0:T(8,128)(2,1)S(1)}, u32[]{:S(2)}, u32[]{:S(2)}) collective-permute-start(s16[272,128]{1,0:T(8,128)(2,1)S(1)} %get-tuple-element.80), channel_id=1, source_target_pairs={{0,2},{1,3},{2,0},{3,1},{4,6},{5,7},{6,4},{7,5},{8,10},{9,11},{10,... | collective-permute-start | bytes 208904 | tf_op jit(solution)/shard_map/ppermute | solution.py:368
  68.1 7.8 %collective-permute-start.21 = (s16[272,128]{1,0:T(8,128)(2,1)S(1)}, s16[272,128]{1,0:T(8,128)(2,1)S(1)}, u32[]{:S(2)}, u32[]{:S(2)}) collective-permute-start(s16[272,128]{1,0:T(8,128)(2,1)S(1)} %get-tuple-element.81), channel_id=1, source_target_pairs={{0,3},{1,2},{2,1},{3,0},{4,7},{5,6},{6,5},{7,4},{8,11},{9,10},{10,... | collective-permute-start | bytes 208904 | tf_op jit(solution)/shard_map/ppermute | solution.py:368
